TPU v7x, 512 devices: a whole 4x8x8 slice. The times are simulated.
512 devices in a mesh: path: 16 (over y_hi, x), shard: 32 (over y_lo, z, core).
Axes of the slice: x: 4, y: 8 (y_hi: 4, y_lo: 2; y = y_hi * 2 + y_lo), z: 8, core: 2. Of those that a mesh axis runs over, the one named last changes fastest.
Arguments:
- tokens: bfloat16 [8192, 2048], P('path', 'shard'), may hold values from -6 to 6
- cotangent: bfloat16 [8192, 2048], P('path', 'shard'), may hold values from -6 to 6
- weights: bfloat16 [16, 4, 3, 7168, 128], P('path', None, None, 'shard'), may hold values from -0.125 to 0.125
- momentum: float32 [16, 4, 3, 7168, 128], P('path', None, None, 'shard'), may hold values from -4 to 4
- cluster: int32 [64], replicated, may hold values from 0 to 15, as said below
- path_module: int32 [16, 1], replicated, may hold values from 0 to 3
- owner: int32 [4, 16], replicated, may hold values from 0 to 15, each once within a row
Outputs:
- input_grad: bfloat16 [8192, 2048], P('path', 'shard')
- new_weights: float32 [16, 4, 3, 7168, 128], P('path', None, None, 'shard')
- new_momentum: float32 [16, 4, 3, 7168, 128], P('path', None, None, 'shard')
Inputs may be any that keep to these rules, and one draw needn't show every extreme that they name: `cluster`: every path receives exactly 4 blocks; each path sends exactly one of its 4 blocks to each of 4 distinct paths (possibly itself). `path_module`: every module is used by at least one path. `owner`: each row names every path once.
All inputs are finite; a program needn't handle non-finite values.
Results may differ from a plain program's by a relative error of at most 0.005.
Values may be sent and summed in bfloat16 or wider, within the bound.
No kernel may reach another device: no remote copies, remote signals or barrier semaphores. Data moves between devices by JAX's collectives and lax.ppermute only.
A program may use at most 64 MiB of HBM per device.

v0:
```python
import jax
import jax.numpy as jnp
from jax import lax
from jax.sharding import PartitionSpec as P

MODULES = 4
BLK = 128


MU = 0.9
LR_INNER = 0.05
LR_OUTER = 0.02


def delta_tiles(grad):
    return (LR_INNER * grad).astype(jnp.bfloat16)


def body(tokens, cotangent, weights, momentum, cluster, path_module, owner):
    paths = lax.axis_size("path")
    here = lax.axis_index("path")
    modules_of = path_module[:, 0]
    module_here = modules_of[here]
    local_blocks = tokens.shape[0] // BLK
    slots = (local_blocks + paths - 1) // paths
    piece_cols = tokens.shape[1]
    block_ids = jnp.arange(paths * local_blocks, dtype=jnp.int32)
    source_of = block_ids // local_blocks
    same_dest = cluster[:, None] == cluster[None, :]
    same_source = source_of[:, None] == source_of[None, :]
    earlier = block_ids[None, :] < block_ids[:, None]
    slot_rank = jnp.sum((same_dest & same_source & earlier).astype(jnp.int32), axis=1)
    own_dest = lax.dynamic_slice_in_dim(cluster, here * local_blocks, local_blocks)
    own_rank = lax.dynamic_slice_in_dim(slot_rank, here * local_blocks, local_blocks)
    own_slot = own_dest * slots + own_rank
    slot_ids = jnp.arange(paths * slots, dtype=jnp.int32)
    matched = own_slot[None, :] == slot_ids[:, None]
    filled = jnp.any(matched, axis=1)
    pick_block = jnp.sum(
        jnp.where(matched, jnp.arange(local_blocks, dtype=jnp.int32)[None, :], 0), axis=1
    )
    flat_tokens = tokens.reshape(local_blocks, BLK * piece_cols)
    flat_cot = cotangent.reshape(local_blocks, BLK * piece_cols)
    zero_value = jnp.zeros((), jnp.bfloat16)
    send_tokens = jnp.where(filled[:, None], jnp.take(flat_tokens, pick_block, axis=0), zero_value)
    send_cot = jnp.where(filled[:, None], jnp.take(flat_cot, pick_block, axis=0), zero_value)
    recv_tokens, recv_cot = (
        lax.all_to_all(send_tokens, "path", split_axis=0, concat_axis=0, tiled=True),
        lax.all_to_all(send_cot, "path", split_axis=0, concat_axis=0, tiled=True),
    )
    order = jnp.argsort(cluster, stable=True)
    arrived = lax.dynamic_slice_in_dim(order, here * local_blocks, local_blocks)
    arrived_slot = jnp.take(source_of, arrived) * slots + jnp.take(slot_rank, arrived)
    path_tokens = jnp.take(recv_tokens, arrived_slot, axis=0).reshape(
        local_blocks * BLK, piece_cols
    )
    path_cot = jnp.take(recv_cot, arrived_slot, axis=0).reshape(local_blocks * BLK, piece_cols)
    owned = weights[0]
    send_weights = jnp.take(owned, modules_of, axis=0)
    recv_weights = lax.all_to_all(send_weights, "path", split_axis=0, concat_axis=0, tiled=True)
    owner_row = owner[module_here]
    module_tiles = jnp.take(recv_weights, owner_row, axis=0)
    w_gate = module_tiles[:, 0]
    w_up = module_tiles[:, 1]
    w_down = module_tiles[:, 2]
    tile_rows = w_gate.shape[-1]
    full_tokens, full_cot = (
        lax.all_gather(path_tokens, "shard", axis=1, tiled=True),
        lax.all_gather(path_cot, "shard", axis=1, tiled=True),
    )
    row_count = full_tokens.shape[0]
    tokens_split = full_tokens.reshape(row_count, paths, tile_rows)
    cot_split = full_cot.reshape(row_count, paths, tile_rows)
    path_ids = jnp.arange(paths, dtype=jnp.int32)
    tile_of_owner = jnp.sum(
        jnp.where(owner_row[None, :] == path_ids[:, None], path_ids[None, :], 0), axis=1
    )
    gate_pre = jnp.einsum("rjd,jfd->rf", tokens_split, w_gate, preferred_element_type=jnp.float32)
    up_pre = jnp.einsum("rjd,jfd->rf", tokens_split, w_up, preferred_element_type=jnp.float32)
    gate_sigmoid = jax.nn.sigmoid(gate_pre)
    gate_act = gate_pre * gate_sigmoid
    hidden = (gate_act * up_pre).astype(jnp.bfloat16)
    hidden_grad = jnp.einsum("rjd,jfd->rf", cot_split, w_down, preferred_element_type=jnp.float32)
    grad_down = jnp.einsum("rjd,rf->jfd", cot_split, hidden, preferred_element_type=jnp.float32)
    gate_grad = (
        hidden_grad * up_pre * gate_sigmoid * (1.0 + gate_pre * (1.0 - gate_sigmoid))
    ).astype(jnp.bfloat16)
    up_grad = (hidden_grad * gate_act).astype(jnp.bfloat16)
    grad_gate = jnp.einsum(
        "rjd,rf->jfd", tokens_split, gate_grad, preferred_element_type=jnp.float32
    )
    grad_up = jnp.einsum("rjd,rf->jfd", tokens_split, up_grad, preferred_element_type=jnp.float32)
    all_tiles = jnp.stack(
        [delta_tiles(grad_gate), delta_tiles(grad_up), delta_tiles(grad_down)], axis=1
    )
    recv_delta = lax.all_to_all(
        jnp.take(all_tiles, tile_of_owner, axis=0), "path", split_axis=0, concat_axis=0, tiled=True
    )
    grad_terms = jnp.einsum("rf,jfd->rjd", gate_grad, w_gate, preferred_element_type=jnp.float32)
    grad_terms = grad_terms + jnp.einsum(
        "rf,jfd->rjd", up_grad, w_up, preferred_element_type=jnp.float32
    )
    grad_terms = grad_terms.reshape(row_count, paths * tile_rows)
    input_grad = lax.psum_scatter(grad_terms, "shard", scatter_dimension=1, tiled=True).astype(
        jnp.bfloat16
    )
    member = modules_of[None, :] == jnp.arange(MODULES, dtype=jnp.int32)[:, None]
    counts = jnp.sum(member.astype(jnp.float32), axis=1)
    sums = jnp.einsum(
        "mq,qabc->mabc", member.astype(jnp.bfloat16), recv_delta, preferred_element_type=jnp.float32
    )
    mean_delta = sums / counts[:, None, None, None]
    new_moment = MU * momentum[0] + mean_delta
    new_tiles = owned.astype(jnp.float32) - LR_OUTER * (mean_delta + MU * new_moment)
    return (input_grad, new_tiles[None], new_moment[None])


def solution(mesh):
    return jax.shard_map(
        body,
        mesh=mesh,
        in_specs=(
            P("path", "shard"),
            P("path", "shard"),
            P("path", None, None, "shard", None),
            P("path", None, None, "shard", None),
            P(),
            P(),
            P(),
        ),
        out_specs=(
            P("path", "shard"),
            P("path", None, None, "shard", None),
            P("path", None, None, "shard", None),
        ),
        check_vma=False,
    )
```

profile of v0, /device:TPU:1, one launch (start us, length us, event | category | flops | bytes accessed | tf_op | source)
XLA Modules:
  0.0 375.7 jit_solution(7509993078390837855)
XLA Ops:
  7.2 1.2 constant_dynamic-slice_fusion
  9.7 0.9 convert_reduce_fusion
  13.1 1.0 copy.79
  14.2 1.0 copy.72
  18.2 0.9 reshape.203
  19.1 10.2 %all-to-all-start = ((bf16[16,2,4096]{2,1,0:T(2,128)(2,1)}), bf16[16,2,4096]{2,1,0:T(2,128)(2,1)S(1)}, u32[]{:S(2)}, u32[]{:S(2)}) async-start(bf16[16,2,4096]{2,1,0:T(2,128)(2,1)} %reshape.203), calls=%async_computation | async-start | bytes 524288 | tf_op jit(solution)/shard_map/all_to_all | solution.py:49
  29.3 2.0 sort.17
  32.2 0.9 reshape.201
  33.1 6.3 %all-to-all-done = bf16[16,2,4096]{2,1,0:T(2,128)(2,1)S(1)} async-done(((bf16[16,2,4096]{2,1,0:T(2,128)(2,1)}), bf16[16,2,4096]{2,1,0:T(2,128)(2,1)S(1)}, u32[]{:S(2)}, u32[]{:S(2)}) %all-to-all-start) | async-done | bytes 262176 | tf_op jit(solution)/shard_map/all_to_all | solution.py:49
  39.4 6.4 %all-to-all-start.2 = ((bf16[16,2,4096]{2,1,0:T(2,128)(2,1)}), bf16[16,2,4096]{2,1,0:T(2,128)(2,1)S(1)}, u32[]{:S(2)}, u32[]{:S(2)}) async-start(bf16[16,2,4096]{2,1,0:T(2,128)(2,1)} %reshape.201), calls=%async_computation.2 | async-start | bytes 524288 | tf_op jit(solution)/shard_map/all_to_all | solution.py:48
  47.9 9.2 %all-to-all-done.2 = bf16[16,2,4096]{2,1,0:T(2,128)(2,1)S(1)} async-done(((bf16[16,2,4096]{2,1,0:T(2,128)(2,1)}), bf16[16,2,4096]{2,1,0:T(2,128)(2,1)S(1)}, u32[]{:S(2)}, u32[]{:S(2)}) %all-to-all-start.2) | async-done | bytes 262176 | tf_op jit(solution)/shard_map/all_to_all | solution.py:48
  60.5 1.1 gather_fusion
  61.6 1.9 broadcast_select_fusion.1
  63.5 3.7 all-to-all-start.1
  68.3 74.0 %all-to-all-done.1 = bf16[16,3,224,128]{3,2,1,0:T(8,128)(2,1)S(1)} async-done(((bf16[16,3,224,128]{3,2,1,0:T(8,128)(2,1)}), bf16[16,3,224,128]{3,2,1,0:T(8,128)(2,1)S(1)}, u32[]{:S(2)}, u32[]{:S(2)}) %all-to-all-start.1) | async-done | bytes 2752544 | tf_op jit(solution)/shard_map/all_to_all | solution.py:60
  142.3 2.5 gather_fusion.5
  144.7 3.7 copy_select_fusion
  148.4 2.6 convolution_bitcast_fusion.1
  151.1 2.6 convolution_bitcast_fusion
  153.7 57.5 %all-gather.3.cloned.1.call-done = bf16[512,2048]{0,1:T(8,128)(2,1)} async-done(((bf16[512,64]{0,1:T(8,128)(2,1)}), bf16[512,2048]{0,1:T(8,128)(2,1)}) %all-gather.3.cloned.1.call-update) | async-done | bytes 2097168 | tf_op jit(solution)/shard_map/all_gather | solution.py:69
  211.2 2.8 fusion.14
  214.8 2.7 convolution_add_fusion
  220.3 2.5 gather_fusion.8
  222.8 3.7 broadcast_select_fusion
  226.5 8.6 %all-to-all-start.3 = ((bf16[16,3,224,128]{3,2,1,0:T(8,128)(2,1)}), bf16[16,3,224,128]{3,2,1,0:T(8,128)(2,1)S(1)}, u32[]{:S(2)}, u32[]{:S(2)}) async-start(bf16[16,3,224,128]{3,2,1,0:T(8,128)(2,1)} %broadcast_select_fusion), calls=%async_computation.4 | async-start | bytes 5505024 | tf_op jit(solution)/shard_map/all_to_all | solution.py:96
  235.2 2.6 broadcast_multiply_fusion
  237.8 70.9 %all-to-all-done.3 = bf16[16,3,224,128]{3,2,1,0:T(8,128)(2,1)S(1)} async-done(((bf16[16,3,224,128]{3,2,1,0:T(8,128)(2,1)}), bf16[16,3,224,128]{3,2,1,0:T(8,128)(2,1)S(1)}, u32[]{:S(2)}, u32[]{:S(2)}) %all-to-all-start.3) | async-done | bytes 2752544 | tf_op jit(solution)/shard_map/all_to_all | solution.py:96
  308.7 3.6 fusion.11
  312.4 1.2 copy.89
  313.6 1.2 copy.90
  314.7 52.9 %reduce-scatter.2.cloned.1.call-done = f32[512,64]{0,1:T(8,128)} async-done(((f32[512,2048]{0,1:T(8,128)}), f32[512,64]{0,1:T(8,128)}) %reduce-scatter.2.cloned.1.call-update) | async-done | bytes 131088 | tf_op jit(solution)/shard_map/reduce_scatter | solution.py:104
  367.7 1.5 convert_element_type.43
  (73 shorter events, 15.8 us)
Async XLA Ops:
  16.0 13.3 %copy-start.4 = (s32[64]{0:T(128)S(1)}, s32[64]{0:T(128)}, u32[]{:S(2)}) copy-start(s32[64]{0:T(128)} %param.19) | copy-start | bytes 772
  19.1 20.3 %all-to-all-start = ((bf16[16,2,4096]{2,1,0:T(2,128)(2,1)}), bf16[16,2,4096]{2,1,0:T(2,128)(2,1)S(1)}, u32[]{:S(2)}, u32[]{:S(2)}) async-start(bf16[16,2,4096]{2,1,0:T(2,128)(2,1)} %reshape.203), calls=%async_computation | async-start | bytes 524288 | tf_op jit(solution)/shard_map/all_to_all | solution.py:49
  39.4 17.7 %all-to-all-start.2 = ((bf16[16,2,4096]{2,1,0:T(2,128)(2,1)}), bf16[16,2,4096]{2,1,0:T(2,128)(2,1)S(1)}, u32[]{:S(2)}, u32[]{:S(2)}) async-start(bf16[16,2,4096]{2,1,0:T(2,128)(2,1)} %reshape.201), calls=%async_computation.2 | async-start | bytes 524288 | tf_op jit(solution)/shard_map/all_to_all | solution.py:48
  45.8 102.6 %all-gather.5.cloned.1.call-start = ((), (), s32[]{:S(2)}) async-start(), calls=%async_computation.6 | async-start | bytes 2162688 | tf_op jit(solution)/shard_map/all_gather | solution.py:68
  46.6 13.4 %copy-start.2 = (bf16[1,4,3,224,128]{4,3,2,1,0:T(8,128)(2,1)S(1)}, bf16[1,4,3,224,128]{4,3,2,1,0:T(8,128)(2,1)}, u32[]{:S(2)}) copy-start(bf16[1,4,3,224,128]{4,3,2,1,0:T(8,128)(2,1)} %param.17) | copy-start | bytes 2064388
  57.4 3.1 copy-start.6
  63.5 78.8 %all-to-all-start.1 = ((bf16[16,3,224,128]{3,2,1,0:T(8,128)(2,1)}), bf16[16,3,224,128]{3,2,1,0:T(8,128)(2,1)S(1)}, u32[]{:S(2)}, u32[]{:S(2)}) async-start(bf16[16,3,224,128]{3,2,1,0:T(8,128)(2,1)} %broadcast_select_fusion.1), calls=%async_computation.1 | async-start | bytes 5505024 | tf_op jit(solution)/shard_map/all_to_all | solution.py:60
  67.2 144.0 %all-gather.3.cloned.1.call-start = ((), (), s32[]{:S(2)}) async-start(), calls=%async_computation.5 | async-start | bytes 2162688 | tf_op jit(solution)/shard_map/all_gather | solution.py:69
  68.2 299.5 %reduce-scatter.2.cloned.1.call-start = ((), (), s32[]{:S(2)}) async-start(), calls=%async_computation.7 | async-start | bytes 4325376 | tf_op jit(solution)/shard_map/reduce_scatter | solution.py:104
  148.4 2.7 copy-start
  211.2 2.8 copy-start.1
  217.5 1.6 copy-start.5
  217.5 1.6 copy-start.7
  226.5 82.3 %all-to-all-start.3 = ((bf16[16,3,224,128]{3,2,1,0:T(8,128)(2,1)}), bf16[16,3,224,128]{3,2,1,0:T(8,128)(2,1)S(1)}, u32[]{:S(2)}, u32[]{:S(2)}) async-start(bf16[16,3,224,128]{3,2,1,0:T(8,128)(2,1)} %broadcast_select_fusion), calls=%async_computation.4 | async-start | bytes 5505024 | tf_op jit(solution)/shard_map/all_to_all | solution.py:96
  235.1 73.7 %copy-start.3 = (bf16[1,4,3,224,128]{4,3,2,1,0:T(8,128)(2,1)S(1)}, bf16[1,4,3,224,128]{4,3,2,1,0:T(8,128)(2,1)}, u32[]{:S(2)}) copy-start(bf16[1,4,3,224,128]{4,3,2,1,0:T(8,128)(2,1)} %param.17) | copy-start | bytes 2064388
Sparse Core Ops, SparseCore 0:
  60.1 83.0 all-gather.4
  145.9 65.2 all-gather.2
  217.6 150.0 reduce-scatter.1
where the time goes:
time: 380 us; the launch traced here: 376 us
  waiting for transfers between devices  271 us (71%)
  starting transfers between devices  29.1 us (8%)
  local copies, waits for them, and re-layouts  21.5 us (6%)
  other arithmetic  20.6 us (5%)
  matrix products  17.5 us (5%)
  between operations  16.1 us (4%)
    all_to_all x1, waiting for transfers between devices, body(): lax.all_to_all(send_weights, 'path', split_axis=0, concat_axis=0, tiled=T...  74 us
    all_to_all x1, waiting for transfers between devices, body(): lax.all_to_all(jnp.take(all_tiles, tile_of_owner, axis=0), 'path', split_...  70.9 us
    all_gather x1, waiting for transfers between devices, body(): lax.all_gather(path_cot, 'shard', axis=1, tiled=True)  57.5 us
    reduce_scatter x1, waiting for transfers between devices, body(): lax.psum_scatter(grad_terms, 'shard', scatter_dimension=1, tiled=True)  52.9 us
    all_to_all x1, starting transfers between devices, body(): lax.all_to_all(send_cot, 'path', split_axis=0, concat_axis=0, tiled=True)  10.2 us
    all_to_all x1, waiting for transfers between devices, body(): lax.all_to_all(send_tokens, 'path', split_axis=0, concat_axis=0, tiled=True)  9.16 us
    all_to_all x1, starting transfers between devices, body(): lax.all_to_all(jnp.take(all_tiles, tile_of_owner, axis=0), 'path', split_...  8.58 us
    unnamed x27, local copies, waits for them, and re-layouts  7.65 us
  transfers between devices with their start and end apart: 7, of which 6 were waited for; matrix products, arithmetic and copies ran while one was open for 10% of the time, Pallas kernels for 0%

commit v1 on v0

v1 whole, which is shorter than its diff:
```python
import jax
import jax.numpy as jnp
from jax import lax
from jax.experimental import pallas as pl
from jax.experimental.pallas import tpu as pltpu
from jax.sharding import Mesh, PartitionSpec as P

MODULES = 4
BLK = 128
MU = 0.9
LR_INNER = 0.05
LR_OUTER = 0.02

PATH = ("yh", "x")
SHARD = ("yl", "z", "c")
CHIPS = ("yl", "z")
VMEM_LIMIT = 48 * 1024 * 1024


def grads_kernel(tile_ref, core_ref, w_ref, mine_ref, other_ref, delta_ref, dgu_ref, xp, yp, g_s, u_s, d_s, h_s):
    owners, _, units, width = w_ref.shape
    core = core_ref[0]

    def place(o, carry):
        j = pl.multiple_of(tile_ref[o] * width, width)
        to = pl.multiple_of(o * width, width)
        a = mine_ref[pl.ds(j, width), :]
        b = other_ref[pl.ds(j, width), :]
        xp[pl.ds(to, width), :] = jnp.where(core == 0, a, b)
        yp[pl.ds(to, width), :] = jnp.where(core == 0, b, a)
        return carry

    lax.fori_loop(0, owners, place, 0)

    def matrix(k):
        return jnp.concatenate([w_ref[o, k] for o in range(owners)], axis=1)

    g_s[...] = jnp.dot(matrix(0), xp[...], preferred_element_type=jnp.float32)
    u_s[...] = jnp.dot(matrix(1), xp[...], preferred_element_type=jnp.float32)
    d_s[...] = jnp.dot(matrix(2), yp[...], preferred_element_type=jnp.float32)
    step = 32

    def act(i, carry):
        at = pl.multiple_of(i * step, step)
        rows = pl.ds(at, step)
        gate = g_s[rows, :]
        up = u_s[rows, :]
        dh = d_s[rows, :]
        sig = jax.nn.sigmoid(gate)
        silu = gate * sig
        h_s[rows, :] = (silu * up).astype(jnp.bfloat16)
        dgu_ref[rows, :] = (dh * up * sig * (1.0 + gate * (1.0 - sig))).astype(jnp.bfloat16)
        dgu_ref[pl.ds(pl.multiple_of(units + at, step), step), :] = (dh * silu).astype(jnp.bfloat16)
        return carry

    lax.fori_loop(0, units // step, act, 0)
    nt = (((1,), (1,)), ((), ()))

    def back(p, carry):
        rows = pl.ds(pl.multiple_of(p * 2 * width, 2 * width), 2 * width)
        gu = LR_INNER * lax.dot_general(dgu_ref[...], xp[rows, :], nt, preferred_element_type=jnp.float32)
        dn = LR_INNER * lax.dot_general(h_s[...], yp[rows, :], nt, preferred_element_type=jnp.float32)
        gu = gu.astype(jnp.bfloat16)
        dn = dn.astype(jnp.bfloat16)
        for half in range(2):
            lanes = slice(half * width, (half + 1) * width)
            delta_ref[2 * p + half, 0] = gu[:units, lanes]
            delta_ref[2 * p + half, 1] = gu[units:, lanes]
            delta_ref[2 * p + half, 2] = dn[:, lanes]
        return carry

    lax.fori_loop(0, owners // 2, back, 0)


def input_kernel(tile_ref, w_ref, dgu_ref, dx_ref):
    owners, _, units, width = w_ref.shape
    half = width // 2

    def one(o, carry):
        w = w_ref[o, 0:2].reshape(2 * units, width)
        part = lax.dot_general(w, dgu_ref[...], (((0,), (0,)), ((), ())), preferred_element_type=jnp.float32)
        j = tile_ref[o]
        dx_ref[0, j] = part[:half]
        dx_ref[1, j] = part[half:]
        return carry

    lax.fori_loop(0, owners, one, 0)


def grads(tile_of, core, w, mine, other):
    owners, _, units, width = w.shape
    rows = mine.shape[1]
    smem = pl.BlockSpec(memory_space=pltpu.SMEM)
    vmem = pl.BlockSpec(memory_space=pltpu.VMEM)
    return pl.pallas_call(
        grads_kernel,
        out_shape=(
            jax.ShapeDtypeStruct(w.shape, jnp.bfloat16),
            jax.ShapeDtypeStruct((2 * units, rows), jnp.bfloat16),
        ),
        in_specs=[smem, smem, vmem, vmem, vmem],
        out_specs=(vmem, vmem),
        scratch_shapes=[
            pltpu.VMEM(mine.shape, jnp.bfloat16),
            pltpu.VMEM(mine.shape, jnp.bfloat16),
            pltpu.VMEM((units, rows), jnp.float32),
            pltpu.VMEM((units, rows), jnp.float32),
            pltpu.VMEM((units, rows), jnp.float32),
            pltpu.VMEM((units, rows), jnp.bfloat16),
        ],
        compiler_params=pltpu.CompilerParams(vmem_limit_bytes=VMEM_LIMIT),
        cost_estimate=pl.CostEstimate(
            flops=12 * units * rows * owners * width, bytes_accessed=12 * 2**20, transcendentals=units * rows
        ),
        name="grads",
    )(tile_of, core, w, mine, other)


def input_partial(tile_of, w, dgu):
    owners, _, units, width = w.shape
    rows = dgu.shape[1]
    smem = pl.BlockSpec(memory_space=pltpu.SMEM)
    vmem = pl.BlockSpec(memory_space=pltpu.VMEM)
    return pl.pallas_call(
        input_kernel,
        out_shape=jax.ShapeDtypeStruct((2, owners, width // 2, rows), jnp.float32),
        in_specs=[smem, vmem, vmem],
        out_specs=vmem,
        compiler_params=pltpu.CompilerParams(vmem_limit_bytes=VMEM_LIMIT),
        cost_estimate=pl.CostEstimate(
            flops=4 * units * rows * owners * width, bytes_accessed=8 * 2**20, transcendentals=0
        ),
        name="input_partial",
    )(tile_of, w, dgu)


def pick(array, index):
    return array.at[index].get(mode="promise_in_bounds")


def body(tokens, cotangent, weights, momentum, cluster, path_module, owner):
    paths = lax.axis_size(PATH)
    here = lax.axis_index(PATH)
    core = lax.axis_index("c")
    modules_of = path_module[:, 0]
    path_ids = jnp.arange(paths, dtype=jnp.int32)
    blocks = tokens.shape[0] // BLK
    cols = tokens.shape[1]
    owned = weights[0]

    send_w = pick(owned, modules_of)
    recv_w = lax.all_to_all(send_w, PATH, split_axis=0, concat_axis=0, tiled=True)

    def feature_major(array):
        return array.reshape(blocks, BLK, cols).transpose(0, 2, 1)

    both = jnp.stack([feature_major(tokens), feature_major(cotangent)], axis=1)
    own_dest = lax.dynamic_slice_in_dim(cluster, here * blocks, blocks)
    goes = own_dest[None, :] == path_ids[:, None]
    block_ids = jnp.arange(blocks, dtype=jnp.int32)
    send_x = pick(both, jnp.sum(jnp.where(goes, block_ids[None, :], 0), axis=1))
    recv_x = lax.all_to_all(
        send_x.reshape(paths * 2, cols, BLK), PATH + ("c",), split_axis=0, concat_axis=0, tiled=True
    ).reshape(paths, 2, cols, BLK)
    has = jnp.any(cluster.reshape(paths, blocks) == here, axis=1)
    before = jnp.sum((has[None, :] & (path_ids[None, :] < path_ids[:, None])).astype(jnp.int32), axis=1)
    comes = has[None, :] & (before[None, :] == block_ids[:, None])
    sources = jnp.sum(jnp.where(comes, path_ids[None, :], 0), axis=1)
    piece = pick(recv_x, sources).transpose(1, 2, 0, 3).reshape(2 * cols, blocks * BLK)

    mine = lax.all_gather(piece, CHIPS, axis=0, tiled=True)
    swap = [(0, 1), (1, 0)]
    other = lax.ppermute(mine, "c", swap)

    owner_row = owner[modules_of[here]]
    tile_of = jnp.sum(jnp.where(owner_row[None, :] == path_ids[:, None], path_ids[None, :], 0), axis=1)
    delta, dgu = grads(tile_of, core.reshape(1), recv_w, mine, other)
    recv_delta = lax.all_to_all(delta, PATH, split_axis=0, concat_axis=0, tiled=True)

    dx = input_partial(tile_of, recv_w, dgu)
    keep = lax.dynamic_index_in_dim(dx, core, 0, keepdims=False)
    give = lax.dynamic_index_in_dim(dx, 1 - core, 0, keepdims=False)
    chip_dx = keep + lax.ppermute(give, "c", swap)
    chip_dx = chip_dx.reshape(paths * cols, blocks * BLK)
    total = lax.psum_scatter(chip_dx, CHIPS, scatter_dimension=0, tiled=True)
    input_grad = total.astype(jnp.bfloat16).T

    member = modules_of[None, :] == jnp.arange(MODULES, dtype=jnp.int32)[:, None]
    counts = jnp.sum(member.astype(jnp.float32), axis=1)
    sums = jnp.einsum(
        "mq,qabc->mabc", member.astype(jnp.bfloat16), recv_delta, preferred_element_type=jnp.float32
    )
    mean_delta = sums / counts[:, None, None, None]
    new_moment = MU * momentum[0] + mean_delta
    new_tiles = owned.astype(jnp.float32) - LR_OUTER * (mean_delta + MU * new_moment)
    return (input_grad, new_tiles[None], new_moment[None])


def solution(mesh):
    fine = Mesh(mesh.devices.reshape(4, 4, 2, 8, 2), PATH + SHARD)
    tiles = P(PATH, None, None, SHARD, None)
    return jax.shard_map(
        body,
        mesh=fine,
        in_specs=(P(PATH, SHARD), P(PATH, SHARD), tiles, tiles, P(), P(), P()),
        out_specs=(P(PATH, SHARD), tiles, tiles),
        check_vma=False,
    )
```

time: 380 us -> 292 us (0.77)
  the two profiles are of different devices: /device:TPU:1 before, /device:TPU:40 now
where the time goes in v1:
time: 292 us; the launch traced here: 291 us
  waiting for transfers between devices  194 us (66%)
  starting transfers between devices  34.3 us (12%)
  local copies, waits for them, and re-layouts  18.1 us (6%)
  between operations  16.2 us (6%)
  Pallas kernels  15.9 us (5%)
  other arithmetic  9.65 us (3%)
  matrix products  3.62 us (1%)
    all_gather x1, waiting for transfers between devices, body(): mine = lax.all_gather(piece, CHIPS, axis=0, tiled=True)  90.1 us
    all_to_all x1, waiting for transfers between devices, body(): lax.all_to_all(delta, PATH, split_axis=0, concat_axis=0, tiled=True)  62.7 us
    reduce_scatter x1, waiting for transfers between devices, body(): total = lax.psum_scatter(chip_dx, CHIPS, scatter_dimension=0, tiled=True)  27.4 us
    all_to_all x1, waiting for transfers between devices, body(): lax.all_to_all(send_x.reshape(paths * 2, cols, BLK), PATH + ('c',), split...  12.3 us
    all_to_all x1, starting transfers between devices, body(): lax.all_to_all(delta, PATH, split_axis=0, concat_axis=0, tiled=True)  10.2 us
    all_to_all x1, starting transfers between devices, body(): lax.all_to_all(send_x.reshape(paths * 2, cols, BLK), PATH + ('c',), split...  9.83 us
    all_to_all x1, starting transfers between devices, body(): lax.all_to_all(send_w, PATH, split_axis=0, concat_axis=0, tiled=True)  9.8 us
    pallas_call x1, Pallas kernels, grads(): pl.pallas_call(grads_kernel, out_shape=(jax.ShapeDtypeStruct(w.shape, jnp...  9.38 us
  transfers between devices with their start and end apart: 7, of which 5 were waited for; matrix products, arithmetic and copies ran while one was open for 6% of the time, Pallas kernels for 0%

profile of v1, /device:TPU:40, one launch (start us, length us, event | category | flops | bytes accessed | tf_op | source)
XLA Modules:
  0.0 291.5 jit_solution(13962167351976626059)
XLA Ops:
  7.2 0.8 dynamic_slice.18
  8.1 0.7 fusion.13
  8.8 0.9 bitcast_bitcast_fusion
  9.7 1.4 gather_fusion.1
  11.1 9.8 %all-to-all-start.1 = ((bf16[32,64,128]{2,1,0:T(8,128)(2,1)}), bf16[32,64,128]{2,1,0:T(8,128)(2,1)S(1)}, u32[]{:S(2)}, u32[]{:S(2)}) async-start(bf16[32,64,128]{2,1,0:T(8,128)(2,1)} %bitcast.11), calls=%async_computation.1 | async-start | bytes 1048576 | tf_op jit(solution)/shard_map/all_to_all | solution.py:162
  21.5 12.3 %all-to-all-done.1 = bf16[32,64,128]{2,1,0:T(8,128)(2,1)S(1)} async-done(((bf16[32,64,128]{2,1,0:T(8,128)(2,1)}), bf16[32,64,128]{2,1,0:T(8,128)(2,1)S(1)}, u32[]{:S(2)}, u32[]{:S(2)}) %all-to-all-start.1) | async-done | bytes 524320 | tf_op jit(solution)/shard_map/all_to_all | solution.py:162
  33.8 0.6 gather_fusion.2
  34.5 0.7 copy.65
  35.2 0.4 copy.64
  35.7 2.5 gather_fusion
  38.1 9.8 %all-to-all-start = ((bf16[16,3,224,128]{3,2,1,0:T(8,128)(2,1)}), bf16[16,3,224,128]{3,2,1,0:T(8,128)(2,1)S(1)}, u32[]{:S(2)}, u32[]{:S(2)}) async-start(bf16[16,3,224,128]{3,2,1,0:T(8,128)(2,1)} %gather_fusion), calls=%async_computation | async-start | bytes 5505024 | tf_op jit(solution)/shard_map/all_to_all | solution.py:152
  47.9 90.1 %all-gather.2.cloned.1.call-done.mine_ref = bf16[2048,512]{1,0:T(8,128)(2,1)} async-done(((bf16[128,512]{1,0:T(8,128)(2,1)}), bf16[2048,512]{1,0:T(8,128)(2,1)}) %all-gather.2.cloned.1.call-update) | async-done | bytes 2097168 | tf_op jit(solution)/shard_map/all_gather | solution.py:171
  138.0 1.9 collective-permute-start
  139.9 0.6 constant_dynamic-slice_fusion.1
  142.5 0.7 fusion.12
  143.3 1.1 collective-permute-done.other_ref
  144.4 0.4 copy-done.1
  144.8 1.6 copy-done.3
  146.4 9.4 %grads.1 = (bf16[16,3,224,128]{3,2,1,0:T(8,128)(2,1)}, bf16[448,512]{1,0:T(8,128)(2,1)S(1)}) custom-call(s32[16]{0:T(128)S(1)} %select_reduce_fusion.tile_ref, s32[1]{0:T(128)} %bitcast.4.core_ref, bf16[16,3,224,128]{3,2,1,0:T(8,128)(2,1)} %copy-done.1, bf16[2048,512]{1,0:T(8,128)(2,1)S(1)} %copy-done.3, bf16[2048,512]{1,0:T(8,128)(2,1)} %collective-permute-done.other_ref), custom_call_target="tpu_custom_call" | custom-call | flops 2818572288 | bytes 12582912 | tf_op jit(solution)/shard_map/grads/pallas_call | solution.py:95
  155.8 1.8 copy-done.2
  157.6 6.5 %input_partial.1 = f32[2,16,64,512]{3,2,1,0:T(8,128)} custom-call(s32[16]{0:T(128)S(1)} %select_reduce_fusion.tile_ref, bf16[16,3,224,128]{3,2,1,0:T(8,128)(2,1)S(1)} %copy-done.2, bf16[448,512]{1,0:T(8,128)(2,1)S(1)} %get-tuple-element.5.dgu_ref), custom_call_target="tpu_custom_call" | custom-call | flops 939524096 | bytes 8388608 | tf_op jit(solution)/shard_map/input_partial/pallas_call | solution.py:124
  164.1 3.2 %dynamic-slice_bitcast_fusion = f32[16,64,512]{2,1,0:T(8,128)} fusion(f32[2,16,64,512]{3,2,1,0:T(8,128)} %input_partial.1, s32[]{:T(128)S(6)} %select_n.62), kind=kLoop, calls=%fused_computation.6 | loop fusion | bytes 4194308 | tf_op jit(solution)/shard_map/jit(dynamic_index_in_dim)/squeeze | solution.py:182
  167.3 2.4 collective-permute-start.1
  169.7 10.2 %all-to-all-start.2 = ((bf16[16,3,224,128]{3,2,1,0:T(8,128)(2,1)}), bf16[16,3,224,128]{3,2,1,0:T(8,128)(2,1)S(1)}, u32[]{:S(2)}, u32[]{:S(2)}) async-start(bf16[16,3,224,128]{3,2,1,0:T(8,128)(2,1)} %get-tuple-element.6), calls=%async_computation.3 | async-start | bytes 5505024 | tf_op jit(solution)/shard_map/all_to_all | solution.py:178
  180.0 4.2 %bitcast_add_fusion = f32[16,64,512]{2,1,0:T(8,128)} fusion(f32[16,64,512]{2,1,0:T(8,128)} %collective-permute-done.1, f32[2,16,64,512]{3,2,1,0:T(8,128)} %input_partial.1, s32[]{:T(128)S(6)} %select_n.61), kind=kLoop, calls=%fused_computation.5 | loop fusion | flops 524288 | bytes 6291460 | tf_op jit(solution)/shard_map/add | solution.py:183
  184.4 2.5 broadcast_multiply_fusion
  186.9 62.7 %all-to-all-done.2 = bf16[16,3,224,128]{3,2,1,0:T(8,128)(2,1)S(1)} async-done(((bf16[16,3,224,128]{3,2,1,0:T(8,128)(2,1)}), bf16[16,3,224,128]{3,2,1,0:T(8,128)(2,1)S(1)}, u32[]{:S(2)}, u32[]{:S(2)}) %all-to-all-start.2) | async-done | bytes 2752544 | tf_op jit(solution)/shard_map/all_to_all | solution.py:178
  249.7 3.6 %fusion.6 = (f32[1,4,3,224,128]{4,1,3,2,0:T(4,128)S(1)}, f32[1,4,3,224,128]{4,1,3,2,0:T(4,128)S(1)}) fusion(f32[1,4,3,224,128]{4,3,2,1,0:T(8,128)} %broadcast_multiply_fusion, bf16[1,4,3,224,128]{4,3,2,1,0:T(8,128)(2,1)S(1)} %copy-done.4, f32[4]{0:T(128)S(1)} %convert_reduce_fusion.1, bf16[16,3,224,128]{3,2,1,0:T(8,128)(2,1)S(1)} %all-to-all-done.2, ...), kind=kOutput, calls=%fused_computation.13 | convolution fusion | flops 13418560 | bytes 7569488 | tf_op jit(solution)/shard_map/mq,qabc->mabc/dot_general | solution.py:190
  253.3 1.2 copy.38
  254.5 1.2 copy.39
  255.7 27.4 %reduce-scatter.2.cloned.1.call-done = f32[64,512]{1,0:T(8,128)} async-done(((f32[1024,512]{1,0:T(8,128)}), f32[64,512]{1,0:T(8,128)}) %reduce-scatter.2.cloned.1.call-update) | async-done | bytes 131088 | tf_op jit(solution)/shard_map/reduce_scatter | solution.py:185
  283.1 1.5 convert_bitcast_fusion
  (32 shorter events, 1.1 us)
Async XLA Ops:
  7.2 1.6 copy-start
  7.2 13.8 %copy-start.6 = (s32[64]{0:T(128)S(1)}, s32[64]{0:T(128)}, u32[]{:S(2)}) copy-start(s32[64]{0:T(128)} %param.11) | copy-start | bytes 772
  7.2 28.0 %copy-start.4 = (bf16[1,4,3,224,128]{4,3,2,1,0:T(8,128)(2,1)S(1)}, bf16[1,4,3,224,128]{4,3,2,1,0:T(8,128)(2,1)}, u32[]{:S(2)}) copy-start(bf16[1,4,3,224,128]{4,3,2,1,0:T(8,128)(2,1)} %param.9) | copy-start | bytes 2064388
  11.1 22.7 %all-to-all-start.1 = ((bf16[32,64,128]{2,1,0:T(8,128)(2,1)}), bf16[32,64,128]{2,1,0:T(8,128)(2,1)S(1)}, u32[]{:S(2)}, u32[]{:S(2)}) async-start(bf16[32,64,128]{2,1,0:T(8,128)(2,1)} %bitcast.11), calls=%async_computation.1 | async-start | bytes 1048576 | tf_op jit(solution)/shard_map/all_to_all | solution.py:162
  20.9 117.1 %all-gather.2.cloned.1.call-start = ((), (), s32[]{:S(2)}) async-start(), calls=%async_computation.4 | async-start | bytes 2228224 | tf_op jit(solution)/shard_map/all_gather | solution.py:171
  38.1 101.8 %copy-start.5 = (s32[16,1]{0,1:T(1,128)S(1)}, s32[16,1]{0,1:T(1,128)}, u32[]{:S(2)}) copy-start(s32[16,1]{0,1:T(1,128)} %param.12) | copy-start | bytes 196
  38.1 105.1 %all-to-all-start = ((bf16[16,3,224,128]{3,2,1,0:T(8,128)(2,1)}), bf16[16,3,224,128]{3,2,1,0:T(8,128)(2,1)S(1)}, u32[]{:S(2)}, u32[]{:S(2)}) async-start(bf16[16,3,224,128]{3,2,1,0:T(8,128)(2,1)} %gather_fusion), calls=%async_computation | async-start | bytes 5505024 | tf_op jit(solution)/shard_map/all_to_all | solution.py:152
  138.0 6.4 %collective-permute-start = (bf16[2048,512]{1,0:T(8,128)(2,1)}, bf16[2048,512]{1,0:T(8,128)(2,1)}, u32[]{:S(2)}, u32[]{:S(2)}) collective-permute-start(bf16[2048,512]{1,0:T(8,128)(2,1)} %all-gather.2.cloned.1.call-done.mine_ref), channel_id=1, source_target_pairs={{0,1},{1,0},{2,3},{3,2},{4,5},{5,4},{6,7},{7,6},{8,9},{9,8},{10,11... | collective-permute-start | bytes 6291464 | tf_op jit(solution)/shard_map/ppermute | solution.py:173
  143.3 1.6 copy-start.1
  144.8 1.6 copy-start.3
  155.8 1.8 copy-start.2
  167.3 12.7 %collective-permute-start.1 = (f32[16,64,512]{2,1,0:T(8,128)}, f32[16,64,512]{2,1,0:T(8,128)}, u32[]{:S(2)}, u32[]{:S(2)}) collective-permute-start(f32[16,64,512]{2,1,0:T(8,128)} %dynamic-slice_bitcast_fusion), channel_id=1, source_target_pairs={{0,1},{1,0},{2,3},{3,2},{4,5},{5,4},{6,7},{7,6},{8,9},{9,8},{10,11... | collective-permute-start | bytes 6291464 | tf_op jit(solution)/shard_map/ppermute | solution.py:183
  169.7 79.9 %all-to-all-start.2 = ((bf16[16,3,224,128]{3,2,1,0:T(8,128)(2,1)}), bf16[16,3,224,128]{3,2,1,0:T(8,128)(2,1)S(1)}, u32[]{:S(2)}, u32[]{:S(2)}) async-start(bf16[16,3,224,128]{3,2,1,0:T(8,128)(2,1)} %get-tuple-element.6), calls=%async_computation.3 | async-start | bytes 5505024 | tf_op jit(solution)/shard_map/all_to_all | solution.py:178
  180.0 103.1 %reduce-scatter.2.cloned.1.call-start = ((), (), s32[]{:S(2)}) async-start(), calls=%async_computation.5 | async-start | bytes 2228224 | tf_op jit(solution)/shard_map/reduce_scatter | solution.py:185
Sparse Core Ops, SparseCore 0:
  35.3 102.6 all-gather.1
  184.4 98.7 reduce-scatter.1

commit v2 on v1

--- a/solution.py
+++ b/solution.py
@@ -13,7 +13,6 @@
 
 PATH = ("yh", "x")
 SHARD = ("yl", "z", "c")
-CHIPS = ("yl", "z")
 VMEM_LIMIT = 48 * 1024 * 1024
 
 
@@ -72,19 +71,48 @@
     lax.fori_loop(0, owners // 2, back, 0)
 
 
-def input_kernel(tile_ref, w_ref, dgu_ref, dx_ref):
+def input_kernel(slot_ref, core_ref, w_ref, dgu_ref, keep_ref, give_ref):
     owners, _, units, width = w_ref.shape
     half = width // 2
+    core = core_ref[0]
 
     def one(o, carry):
         w = w_ref[o, 0:2].reshape(2 * units, width)
         part = lax.dot_general(w, dgu_ref[...], (((0,), (0,)), ((), ())), preferred_element_type=jnp.float32)
-        j = tile_ref[o]
-        dx_ref[0, j] = part[:half]
-        dx_ref[1, j] = part[half:]
+        j = slot_ref[o]
+        low, high = part[:half], part[half:]
+        keep_ref[j] = jnp.where(core == 0, low, high)
+        give_ref[j] = jnp.where(core == 0, high, low).astype(jnp.bfloat16)
         return carry
 
     lax.fori_loop(0, owners, one, 0)
+
+
+def pair_kernel(keep_ref, came_ref, own_ref, *out_refs):
+    for k in range(len(out_refs) + 1):
+        at = slice(2 * k, 2 * k + 2)
+        total = keep_ref[at] + came_ref[at].astype(jnp.float32)
+        if k == 0:
+            own_ref[...] = total
+        else:
+            out_refs[k - 1][...] = total.astype(jnp.bfloat16)
+
+
+def update_kernel(module_ref, count_ref, delta_ref, weight_ref, momentum_ref, new_w_ref, new_m_ref, acc):
+    modules = weight_ref.shape[0]
+    acc[...] = jnp.zeros_like(acc)
+
+    def add(q, carry):
+        m = module_ref[q]
+        acc[m] += delta_ref[q, 0].astype(jnp.float32)
+        return carry
+
+    lax.fori_loop(0, delta_ref.shape[0], add, 0)
+    for m in range(modules):
+        mean = acc[m] / count_ref[m]
+        moment = MU * momentum_ref[m, 0] + mean
+        new_m_ref[m, 0] = moment
+        new_w_ref[m, 0] = weight_ref[m, 0].astype(jnp.float32) - LR_OUTER * (mean + MU * moment)
 
 
 def grads(tile_of, core, w, mine, other):
@@ -116,26 +144,92 @@
     )(tile_of, core, w, mine, other)
 
 
-def input_partial(tile_of, w, dgu):
+def input_partial(slot_of, core, w, dgu):
     owners, _, units, width = w.shape
     rows = dgu.shape[1]
     smem = pl.BlockSpec(memory_space=pltpu.SMEM)
     vmem = pl.BlockSpec(memory_space=pltpu.VMEM)
+    shape = (owners, width // 2, rows)
     return pl.pallas_call(
         input_kernel,
-        out_shape=jax.ShapeDtypeStruct((2, owners, width // 2, rows), jnp.float32),
-        in_specs=[smem, vmem, vmem],
-        out_specs=vmem,
+        out_shape=(jax.ShapeDtypeStruct(shape, jnp.float32), jax.ShapeDtypeStruct(shape, jnp.bfloat16)),
+        in_specs=[smem, smem, vmem, vmem],
+        out_specs=(vmem, vmem),
         compiler_params=pltpu.CompilerParams(vmem_limit_bytes=VMEM_LIMIT),
-        cost_estimate=pl.CostEstimate(
-            flops=4 * units * rows * owners * width, bytes_accessed=8 * 2**20, transcendentals=0
-        ),
+        cost_estimate=pl.CostEstimate(flops=1000, bytes_accessed=1000, transcendentals=0),
         name="input_partial",
-    )(tile_of, w, dgu)
+    )(slot_of, core, w, dgu)
+
+
+def pair_sums(keep, came):
+    tiles, feats, rows = keep.shape
+    vmem = pl.BlockSpec(memory_space=pltpu.VMEM)
+    part = (2, feats, rows)
+    steps = tiles // 2
+    return pl.pallas_call(
+        pair_kernel,
+        out_shape=(jax.ShapeDtypeStruct(part, jnp.float32),)
+        + (jax.ShapeDtypeStruct(part, jnp.bfloat16),) * (steps - 1),
+        in_specs=[vmem, vmem],
+        out_specs=(vmem,) * steps,
+        compiler_params=pltpu.CompilerParams(vmem_limit_bytes=VMEM_LIMIT),
+        cost_estimate=pl.CostEstimate(flops=1000, bytes_accessed=1000, transcendentals=0),
+        name="pair_sums",
+    )(keep, came)
+
+
+def update(modules_of, counts, delta, owned, momentum):
+    paths = delta.shape[0]
+    modules, mats, units, width = owned.shape
+    rows = units // 2
+    smem = pl.BlockSpec(memory_space=pltpu.SMEM)
+    tile = pl.BlockSpec((modules, 1, rows, width), lambda k, i: (0, k, i, 0))
+    return pl.pallas_call(
+        update_kernel,
+        grid=(mats, units // rows),
+        out_shape=(jax.ShapeDtypeStruct(momentum.shape, jnp.float32),) * 2,
+        in_specs=[
+            smem,
+            smem,
+            pl.BlockSpec((paths, 1, rows, width), lambda k, i: (0, k, i, 0)),
+            tile,
+            tile,
+        ],
+        out_specs=(tile, tile),
+        scratch_shapes=[pltpu.VMEM((modules, rows, width), jnp.float32)],
+        compiler_params=pltpu.CompilerParams(vmem_limit_bytes=VMEM_LIMIT),
+        cost_estimate=pl.CostEstimate(flops=10**6, bytes_accessed=8 * 2**20, transcendentals=0),
+        name="update",
+    )(modules_of, counts, delta, owned, momentum)
 
 
 def pick(array, index):
     return array.at[index].get(mode="promise_in_bounds")
+
+
+def turn(size, k):
+    return [(i, (i + k) % size) for i in range(size)]
+
+
+def ring_gather(piece):
+    depth = lax.axis_size("z")
+    beside = lax.ppermute(piece, "yl", [(0, 1), (1, 0)])
+    first = lax.axis_index("yl") == 0
+    pair = jnp.concatenate([jnp.where(first, piece, beside), jnp.where(first, beside, piece)], axis=0)
+    half = piece.shape[0]
+    up = down = pair
+    parts = [pair]
+    at = [0] * depth
+    for k in range(1, depth // 2):
+        up = lax.ppermute(up, "z", turn(depth, 1))
+        down = lax.ppermute(down, "z", turn(depth, -1))
+        at[depth - k] = len(parts)
+        at[k] = len(parts) + 1
+        parts += [up, down]
+    at[depth // 2] = len(parts)
+    parts.append(lax.ppermute(up[:half], "z", turn(depth, 1)))
+    parts.append(lax.ppermute(down[half:], "z", turn(depth, -1)))
+    return jnp.concatenate(parts, axis=0), at
 
 
 def body(tokens, cotangent, weights, momentum, cluster, path_module, owner):
@@ -168,31 +262,35 @@
     sources = jnp.sum(jnp.where(comes, path_ids[None, :], 0), axis=1)
     piece = pick(recv_x, sources).transpose(1, 2, 0, 3).reshape(2 * cols, blocks * BLK)
 
-    mine = lax.all_gather(piece, CHIPS, axis=0, tiled=True)
+    mine, at = ring_gather(piece)
     swap = [(0, 1), (1, 0)]
     other = lax.ppermute(mine, "c", swap)
 
     owner_row = owner[modules_of[here]]
     tile_of = jnp.sum(jnp.where(owner_row[None, :] == path_ids[:, None], path_ids[None, :], 0), axis=1)
-    delta, dgu = grads(tile_of, core.reshape(1), recv_w, mine, other)
+    z = lax.axis_index("z")
+    depth = lax.axis_size("z")
+    away = (tile_of % depth - z) % depth
+    side = tile_of // depth
+    place = jnp.sum(jnp.where(away[:, None] == jnp.arange(depth)[None, :], jnp.array(at, jnp.int32)[None, :], 0), axis=1)
+    core_id = core.reshape(1)
+    delta, dgu = grads(place * 2 + side, core_id, recv_w, mine, other)
     recv_delta = lax.all_to_all(delta, PATH, split_axis=0, concat_axis=0, tiled=True)
 
-    dx = input_partial(tile_of, recv_w, dgu)
-    keep = lax.dynamic_index_in_dim(dx, core, 0, keepdims=False)
-    give = lax.dynamic_index_in_dim(dx, 1 - core, 0, keepdims=False)
-    chip_dx = keep + lax.ppermute(give, "c", swap)
-    chip_dx = chip_dx.reshape(paths * cols, blocks * BLK)
-    total = lax.psum_scatter(chip_dx, CHIPS, scatter_dimension=0, tiled=True)
+    keep, give = input_partial(away * 2 + side, core_id, recv_w, dgu)
+    sums = pair_sums(keep, lax.ppermute(give, "c", swap))
+    came = [lax.ppermute(sums[k], "z", turn(depth, k)) for k in range(1, depth)]
+    total = sums[0]
+    for part in came:
+        total = total + part.astype(jnp.float32)
+    yl = lax.axis_index("yl")
+    theirs = lax.ppermute(lax.dynamic_index_in_dim(total, 1 - yl, 0, keepdims=False), "yl", swap)
+    total = lax.dynamic_index_in_dim(total, yl, 0, keepdims=False) + theirs
     input_grad = total.astype(jnp.bfloat16).T
 
     member = modules_of[None, :] == jnp.arange(MODULES, dtype=jnp.int32)[:, None]
     counts = jnp.sum(member.astype(jnp.float32), axis=1)
-    sums = jnp.einsum(
-        "mq,qabc->mabc", member.astype(jnp.bfloat16), recv_delta, preferred_element_type=jnp.float32
-    )
-    mean_delta = sums / counts[:, None, None, None]
-    new_moment = MU * momentum[0] + mean_delta
-    new_tiles = owned.astype(jnp.float32) - LR_OUTER * (mean_delta + MU * new_moment)
+    new_tiles, new_moment = update(modules_of, counts, recv_delta, owned, momentum[0])
     return (input_grad, new_tiles[None], new_moment[None])
 
 

time: 292 us -> 249 us (0.85)
  the two profiles are of different devices: /device:TPU:40 before, /device:TPU:1 now
where the time goes in v2:
time: 249 us; the launch traced here: 247 us
  waiting for transfers between devices  111 us (45%)
  starting transfers between devices  94.2 us (38%)
  Pallas kernels  20.2 us (8%)
  local copies, waits for them, and re-layouts  13.6 us (5%)
  other arithmetic  4.68 us (2%)
  between operations  3.11 us (1%)
    ppermute x1, waiting for transfers between devices, ring_gather(): beside = lax.ppermute(piece, 'yl', [(0, 1), (1, 0)])  61.3 us
    ppermute x7, starting transfers between devices, body(): came = [lax.ppermute(sums[k], 'z', turn(depth, k)) for k in range(1, depth)]  25.6 us
    ppermute x3, starting transfers between devices, ring_gather(): down = lax.ppermute(down, 'z', turn(depth, -1))  17.7 us
    all_to_all x1, waiting for transfers between devices, body(): lax.all_to_all(send_x.reshape(paths * 2, cols, BLK), PATH + ('c',), split...  15.9 us
    ppermute x7, waiting for transfers between devices, body(): came = [lax.ppermute(sums[k], 'z', turn(depth, k)) for k in range(1, depth)]  13.3 us
    all_to_all x1, starting transfers between devices, body(): lax.all_to_all(send_x.reshape(paths * 2, cols, BLK), PATH + ('c',), split...  11.2 us
    pallas_call x1, Pallas kernels, grads(): pl.pallas_call(grads_kernel, out_shape=(jax.ShapeDtypeStruct(w.shape, jnp...  9.37 us
    ppermute x3, waiting for transfers between devices, ring_gather(): up = lax.ppermute(up, 'z', turn(depth, 1))  8.46 us
  transfers between devices with their start and end apart: 22, of which 15 were waited for; matrix products, arithmetic and copies ran while one was open for 4% of the time, Pallas kernels for 3%

profile of v2, /device:TPU:1, one launch (start us, length us, event | category | flops | bytes accessed | tf_op | source)
XLA Modules:
  0.0 247.1 jit_solution(11507678957109425648)
XLA Ops:
  4.5 11.2 %all-to-all-start.1 = ((bf16[32,64,128]{2,1,0:T(8,128)(2,1)}), bf16[32,64,128]{2,1,0:T(8,128)(2,1)S(1)}, u32[]{:S(2)}, u32[]{:S(2)}) async-start(bf16[32,64,128]{2,1,0:T(8,128)(2,1)} %bitcast.11), calls=%async_computation.1 | async-start | bytes 1048576 | tf_op jit(solution)/shard_map/all_to_all | solution.py:256
  15.8 2.4 gather_fusion
  18.2 15.9 %all-to-all-done.1 = bf16[32,64,128]{2,1,0:T(8,128)(2,1)S(1)} async-done(((bf16[32,64,128]{2,1,0:T(8,128)(2,1)}), bf16[32,64,128]{2,1,0:T(8,128)(2,1)S(1)}, u32[]{:S(2)}, u32[]{:S(2)}) %all-to-all-start.1) | async-done | bytes 524320 | tf_op jit(solution)/shard_map/all_to_all | solution.py:256
  34.2 4.5 %all-to-all-start = ((bf16[16,3,224,128]{3,2,1,0:T(8,128)(2,1)}), bf16[16,3,224,128]{3,2,1,0:T(8,128)(2,1)}, u32[]{:S(2)}, u32[]{:S(2)}) async-start(bf16[16,3,224,128]{3,2,1,0:T(8,128)(2,1)} %gather_fusion), calls=%async_computation | async-start | bytes 5505024 | tf_op jit(solution)/shard_map/all_to_all | solution.py:246
  39.9 1.9 collective-permute-start
  41.8 61.3 %collective-permute-done = bf16[128,512]{1,0:T(8,128)(2,1)S(1)} collective-permute-done((bf16[128,512]{1,0:T(8,128)(2,1)S(1)}, bf16[128,512]{1,0:T(8,128)(2,1)S(1)}, u32[]{:S(2)}, u32[]{:S(2)}) %collective-permute-start) | collective-permute-done | bytes 131104 | tf_op jit(solution)/shard_map/ppermute | solution.py:216
  103.2 4.0 %collective-permute-start.1 = (bf16[256,512]{1,0:T(8,128)(2,1)S(1)}, bf16[256,512]{1,0:T(8,128)(2,1)S(1)}, u32[]{:S(2)}, u32[]{:S(2)}) collective-permute-start(bf16[256,512]{1,0:T(8,128)(2,1)S(1)} %pad_maximum_fusion), channel_id=1, source_target_pairs={{0,2},{2,4},{4,6},{6,8},{8,10},{10,12},{12,14},{14,0},{1,3},{3,5},... | collective-permute-start | bytes 786440 | tf_op jit(solution)/shard_map/ppermute | solution.py:224
  107.2 8.6 %collective-permute-start.2 = (bf16[256,512]{1,0:T(8,128)(2,1)S(1)}, bf16[256,512]{1,0:T(8,128)(2,1)S(1)}, u32[]{:S(2)}, u32[]{:S(2)}) collective-permute-start(bf16[256,512]{1,0:T(8,128)(2,1)S(1)} %pad_maximum_fusion), channel_id=1, source_target_pairs={{0,14},{2,0},{4,2},{6,4},{8,6},{10,8},{12,10},{14,12},{1,15},{3,1}... | collective-permute-start | bytes 786440 | tf_op jit(solution)/shard_map/ppermute | solution.py:225
  115.8 3.9 %collective-permute-done.1 = bf16[256,512]{1,0:T(8,128)(2,1)S(1)} collective-permute-done((bf16[256,512]{1,0:T(8,128)(2,1)S(1)}, bf16[256,512]{1,0:T(8,128)(2,1)S(1)}, u32[]{:S(2)}, u32[]{:S(2)}) %collective-permute-start.1) | collective-permute-done | bytes 262176 | tf_op jit(solution)/shard_map/ppermute | solution.py:224
  121.6 4.6 %collective-permute-start.4 = (bf16[256,512]{1,0:T(8,128)(2,1)S(1)}, bf16[256,512]{1,0:T(8,128)(2,1)S(1)}, u32[]{:S(2)}, u32[]{:S(2)}) collective-permute-start(bf16[256,512]{1,0:T(8,128)(2,1)S(1)} %collective-permute-done.2), channel_id=1, source_target_pairs={{0,14},{2,0},{4,2},{6,4},{8,6},{10,8},{12,10},{14,12},{1,15},{3,1}... | collective-permute-start | bytes 786440 | tf_op jit(solution)/shard_map/ppermute | solution.py:225
  126.2 2.9 %collective-permute-done.3 = bf16[256,512]{1,0:T(8,128)(2,1)S(1)} collective-permute-done((bf16[256,512]{1,0:T(8,128)(2,1)S(1)}, bf16[256,512]{1,0:T(8,128)(2,1)S(1)}, u32[]{:S(2)}, u32[]{:S(2)}) %collective-permute-start.3) | collective-permute-done | bytes 262176 | tf_op jit(solution)/shard_map/ppermute | solution.py:224
  131.0 4.6 %collective-permute-start.6 = (bf16[256,512]{1,0:T(8,128)(2,1)S(1)}, bf16[256,512]{1,0:T(8,128)(2,1)S(1)}, u32[]{:S(2)}, u32[]{:S(2)}) collective-permute-start(bf16[256,512]{1,0:T(8,128)(2,1)S(1)} %collective-permute-done.4), channel_id=1, source_target_pairs={{0,14},{2,0},{4,2},{6,4},{8,6},{10,8},{12,10},{14,12},{1,15},{3,1}... | collective-permute-start | bytes 786440 | tf_op jit(solution)/shard_map/ppermute | solution.py:225
  137.4 1.9 collective-permute-start.7
  139.4 4.6 %collective-permute-start.8 = (bf16[128,512]{1,0:T(8,128)(2,1)S(1)}, bf16[128,512]{1,0:T(8,128)(2,1)S(1)}, u32[]{:S(2)}, u32[]{:S(2)}) collective-permute-start(bf16[128,512]{1,0:T(8,128)(2,1)S(1)} %slice.15), channel_id=1, source_target_pairs={{0,14},{2,0},{4,2},{6,4},{8,6},{10,8},{12,10},{14,12},{1,15},{3,1}... | collective-permute-start | bytes 393224 | tf_op jit(solution)/shard_map/ppermute | solution.py:231
  145.9 6.6 %collective-permute-start.9 = (bf16[2048,512]{1,0:T(8,128)(2,1)S(1)}, bf16[2048,512]{1,0:T(8,128)(2,1)}, u32[]{:S(2)}, u32[]{:S(2)}) collective-permute-start(bf16[2048,512]{1,0:T(8,128)(2,1)S(1)} %constant_dynamic-update-slice_fusion.mine_ref), channel_id=1, source_target_pairs={{0,1},{1,0},{2,3},{3,2},{4,5},{5,4},{6,7},{7,6},{8,9},{9,8},{10,11... | collective-permute-start | bytes 6291464 | tf_op jit(solution)/shard_map/ppermute | solution.py:267
  156.4 9.4 %grads.1 = (bf16[16,3,224,128]{3,2,1,0:T(8,128)(2,1)}, bf16[448,512]{1,0:T(8,128)(2,1)S(1)}) custom-call(s32[16]{0:T(128)S(1)} %get-tuple-element.35.tile_ref, s32[1]{0:T(128)} %bitcast.2.core_ref, bf16[16,3,224,128]{3,2,1,0:T(8,128)(2,1)} %all-to-all-done.w_ref, bf16[2048,512]{1,0:T(8,128)(2,1)S(1)} %constant_dynamic-update-slice_fusion.mine_ref, ...), custom_call_target="tpu_custom_call" | custom-call | flops 2818572288 | bytes 12582912 | tf_op jit(solution)/shard_map/grads/pallas_call | solution.py:123
  166.5 7.8 %all-to-all-start.2 = ((bf16[16,3,224,128]{3,2,1,0:T(8,128)(2,1)}), bf16[16,3,224,128]{3,2,1,0:T(8,128)(2,1)S(1)}, u32[]{:S(2)}, u32[]{:S(2)}) async-start(bf16[16,3,224,128]{3,2,1,0:T(8,128)(2,1)} %get-tuple-element.28), calls=%async_computation.2 | async-start | bytes 5505024 | tf_op jit(solution)/shard_map/all_to_all | solution.py:278
  175.3 5.8 %input_partial.1 = (f32[16,64,512]{2,1,0:T(8,128)S(1)}, bf16[16,64,512]{2,1,0:T(8,128)(2,1)S(1)}) custom-call(s32[16]{0:T(128)S(1)} %multiply_add_fusion.1.slot_ref, s32[1]{0:T(128)} %bitcast.2.core_ref, bf16[16,3,224,128]{3,2,1,0:T(8,128)(2,1)} %all-to-all-done.w_ref, bf16[448,512]{1,0:T(8,128)(2,1)S(1)} %copy-done.4), custom_call_target="tpu_custom_call" | custom-call | flops 1000 | bytes 1000 | tf_op jit(solution)/shard_map/input_partial/pallas_call | solution.py:153
  181.2 2.6 %collective-permute-start.10 = (bf16[16,64,512]{2,1,0:T(8,128)(2,1)S(1)}, bf16[16,64,512]{2,1,0:T(8,128)(2,1)S(1)}, u32[]{:S(2)}, u32[]{:S(2)}) collective-permute-start(bf16[16,64,512]{2,1,0:T(8,128)(2,1)S(1)} %get-tuple-element.19), channel_id=1, source_target_pairs={{0,1},{1,0},{2,3},{3,2},{4,5},{5,4},{6,7},{7,6},{8,9},{9,8},{10,11... | collective-permute-start | bytes 3145736 | tf_op jit(solution)/shard_map/ppermute | solution.py:281
  183.8 2.3 collective-permute-done.10.came_ref
  187.6 5.3 %collective-permute-start.17 = (bf16[2,64,512]{2,1,0:T(8,128)(2,1)S(1)}, bf16[2,64,512]{2,1,0:T(8,128)(2,1)S(1)}, u32[]{:S(2)}, u32[]{:S(2)}) collective-permute-start(bf16[2,64,512]{2,1,0:T(8,128)(2,1)S(1)} %get-tuple-element.27), channel_id=1, source_target_pairs={{0,14},{2,0},{4,2},{6,4},{8,6},{10,8},{12,10},{14,12},{1,15},{3,1}... | collective-permute-start | bytes 393224 | tf_op jit(solution)/shard_map/ppermute | solution.py:282
  192.9 1.9 collective-permute-start.16
  194.8 3.9 %collective-permute-start.15 = (bf16[2,64,512]{2,1,0:T(8,128)(2,1)}, bf16[2,64,512]{2,1,0:T(8,128)(2,1)}, u32[]{:S(2)}, u32[]{:S(2)}) collective-permute-start(bf16[2,64,512]{2,1,0:T(8,128)(2,1)} %get-tuple-element.25), channel_id=1, source_target_pairs={{0,10},{2,12},{4,14},{6,0},{8,2},{10,4},{12,6},{14,8},{1,11},{3,13... | collective-permute-start | bytes 393224 | tf_op jit(solution)/shard_map/ppermute | solution.py:282
  198.7 5.3 %collective-permute-start.14 = (bf16[2,64,512]{2,1,0:T(8,128)(2,1)}, bf16[2,64,512]{2,1,0:T(8,128)(2,1)}, u32[]{:S(2)}, u32[]{:S(2)}) collective-permute-start(bf16[2,64,512]{2,1,0:T(8,128)(2,1)} %get-tuple-element.24), channel_id=1, source_target_pairs={{0,8},{2,10},{4,12},{6,14},{8,0},{10,2},{12,4},{14,6},{1,9},{3,11}... | collective-permute-start | bytes 393224 | tf_op jit(solution)/shard_map/ppermute | solution.py:282
  204.0 1.9 collective-permute-start.13
  206.0 5.3 %collective-permute-start.12 = (bf16[2,64,512]{2,1,0:T(8,128)(2,1)}, bf16[2,64,512]{2,1,0:T(8,128)(2,1)}, u32[]{:S(2)}, u32[]{:S(2)}) collective-permute-start(bf16[2,64,512]{2,1,0:T(8,128)(2,1)} %get-tuple-element.22), channel_id=1, source_target_pairs={{0,4},{2,6},{4,8},{6,10},{8,12},{10,14},{12,0},{14,2},{1,5},{3,7},... | collective-permute-start | bytes 393224 | tf_op jit(solution)/shard_map/ppermute | solution.py:282
  212.0 1.9 collective-permute-start.11
  215.8 6.5 %collective-permute-done.13 = bf16[2,64,512]{2,1,0:T(8,128)(2,1)} collective-permute-done((bf16[2,64,512]{2,1,0:T(8,128)(2,1)}, bf16[2,64,512]{2,1,0:T(8,128)(2,1)}, u32[]{:S(2)}, u32[]{:S(2)}) %collective-permute-start.13) | collective-permute-done | bytes 131104 | tf_op jit(solution)/shard_map/ppermute | solution.py:282
  223.5 3.8 %collective-permute-done.11 = bf16[2,64,512]{2,1,0:T(8,128)(2,1)} collective-permute-done((bf16[2,64,512]{2,1,0:T(8,128)(2,1)}, bf16[2,64,512]{2,1,0:T(8,128)(2,1)}, u32[]{:S(2)}, u32[]{:S(2)}) %collective-permute-start.11) | collective-permute-done | bytes 131104 | tf_op jit(solution)/shard_map/ppermute | solution.py:282
  230.1 2.0 collective-permute-start.18
  232.3 7.0 %collective-permute-done.18 = f32[64,512]{1,0:T(8,128)} collective-permute-done((f32[64,512]{1,0:T(8,128)}, f32[64,512]{1,0:T(8,128)}, u32[]{:S(2)}, u32[]{:S(2)}) %collective-permute-start.18) | collective-permute-done | bytes 131104 | tf_op jit(solution)/shard_map/ppermute | solution.py:287
  243.0 4.1 %update.1 = (f32[4,3,224,128]{3,2,1,0:T(8,128)}, f32[4,3,224,128]{3,2,1,0:T(8,128)}) custom-call(s32[16]{0:T(128)S(1)} %bitcast.65, f32[4]{0:T(128)S(1)} %convert_reduce_fusion.1.count_ref, bf16[16,3,224,128]{3,2,1,0:T(8,128)(2,1)S(1)} %all-to-all-done.2.delta_ref, bf16[4,3,224,128]{3,2,1,0:T(8,128)(2,1)S(1)} %bitcast.62, f32[4,3,224,128]{3,2,1,0:T(8,128)S(1)} %bitcast.63), custom_call_target="tpu_custom_call" | custom-call | flops 1000000 | bytes 8388608 | tf_op jit(solution)/shard_map/update/pallas_call | solution.py:187
  (83 shorter events, 28.4 us)
Async XLA Ops:
  0.6 1.6 copy-start
  0.6 15.1 %copy-start.1 = (bf16[1,4,3,224,128]{4,3,2,1,0:T(8,128)(2,1)S(1)}, bf16[1,4,3,224,128]{4,3,2,1,0:T(8,128)(2,1)}, u32[]{:S(2)}) copy-start(bf16[1,4,3,224,128]{4,3,2,1,0:T(8,128)(2,1)} %param.10) | copy-start | bytes 2064388
  4.5 29.6 %all-to-all-start.1 = ((bf16[32,64,128]{2,1,0:T(8,128)(2,1)}), bf16[32,64,128]{2,1,0:T(8,128)(2,1)S(1)}, u32[]{:S(2)}, u32[]{:S(2)}) async-start(bf16[32,64,128]{2,1,0:T(8,128)(2,1)} %bitcast.11), calls=%async_computation.1 | async-start | bytes 1048576 | tf_op jit(solution)/shard_map/all_to_all | solution.py:256
  18.2 20.4 %copy-start.10 = (s32[64]{0:T(128)S(1)}, s32[64]{0:T(128)}, u32[]{:S(2)}) copy-start(s32[64]{0:T(128)} %param.12) | copy-start | bytes 772
  34.2 122.2 %all-to-all-start = ((bf16[16,3,224,128]{3,2,1,0:T(8,128)(2,1)}), bf16[16,3,224,128]{3,2,1,0:T(8,128)(2,1)}, u32[]{:S(2)}, u32[]{:S(2)}) async-start(bf16[16,3,224,128]{3,2,1,0:T(8,128)(2,1)} %gather_fusion), calls=%async_computation | async-start | bytes 5505024 | tf_op jit(solution)/shard_map/all_to_all | solution.py:246
  39.9 63.2 %collective-permute-start = (bf16[128,512]{1,0:T(8,128)(2,1)S(1)}, bf16[128,512]{1,0:T(8,128)(2,1)S(1)}, u32[]{:S(2)}, u32[]{:S(2)}) collective-permute-start(bf16[128,512]{1,0:T(8,128)(2,1)S(1)} %bitcast.71), channel_id=1, source_target_pairs={{0,16},{16,0},{1,17},{17,1},{2,18},{18,2},{3,19},{19,3},{4,20},{20... | collective-permute-start | bytes 393224 | tf_op jit(solution)/shard_map/ppermute | solution.py:216
  103.2 16.5 %collective-permute-start.1 = (bf16[256,512]{1,0:T(8,128)(2,1)S(1)}, bf16[256,512]{1,0:T(8,128)(2,1)S(1)}, u32[]{:S(2)}, u32[]{:S(2)}) collective-permute-start(bf16[256,512]{1,0:T(8,128)(2,1)S(1)} %pad_maximum_fusion), channel_id=1, source_target_pairs={{0,2},{2,4},{4,6},{6,8},{8,10},{10,12},{12,14},{14,0},{1,3},{3,5},... | collective-permute-start | bytes 786440 | tf_op jit(solution)/shard_map/ppermute | solution.py:224
  107.2 14.4 %collective-permute-start.2 = (bf16[256,512]{1,0:T(8,128)(2,1)S(1)}, bf16[256,512]{1,0:T(8,128)(2,1)S(1)}, u32[]{:S(2)}, u32[]{:S(2)}) collective-permute-start(bf16[256,512]{1,0:T(8,128)(2,1)S(1)} %pad_maximum_fusion), channel_id=1, source_target_pairs={{0,14},{2,0},{4,2},{6,4},{8,6},{10,8},{12,10},{14,12},{1,15},{3,1}... | collective-permute-start | bytes 786440 | tf_op jit(solution)/shard_map/ppermute | solution.py:225
  119.6 9.4 %collective-permute-start.3 = (bf16[256,512]{1,0:T(8,128)(2,1)S(1)}, bf16[256,512]{1,0:T(8,128)(2,1)S(1)}, u32[]{:S(2)}, u32[]{:S(2)}) collective-permute-start(bf16[256,512]{1,0:T(8,128)(2,1)S(1)} %collective-permute-done.1), channel_id=1, source_target_pairs={{0,2},{2,4},{4,6},{6,8},{8,10},{10,12},{12,14},{14,0},{1,3},{3,5},... | collective-permute-start | bytes 786440 | tf_op jit(solution)/shard_map/ppermute | solution.py:224
  121.6 9.4 %collective-permute-start.4 = (bf16[256,512]{1,0:T(8,128)(2,1)S(1)}, bf16[256,512]{1,0:T(8,128)(2,1)S(1)}, u32[]{:S(2)}, u32[]{:S(2)}) collective-permute-start(bf16[256,512]{1,0:T(8,128)(2,1)S(1)} %collective-permute-done.2), channel_id=1, source_target_pairs={{0,14},{2,0},{4,2},{6,4},{8,6},{10,8},{12,10},{14,12},{1,15},{3,1}... | collective-permute-start | bytes 786440 | tf_op jit(solution)/shard_map/ppermute | solution.py:225
  126.1 26.3 %copy-start.6 = (s32[16,1]{0,1:T(1,128)S(1)}, s32[16,1]{0,1:T(1,128)}, u32[]{:S(2)}) copy-start(s32[16,1]{0,1:T(1,128)} %param.13) | copy-start | bytes 196
  126.2 29.7 %copy-start.11 = (s32[8]{0:T(128)S(1)}, s32[8]{0:T(128)}, u32[]{:S(2)}) copy-start(s32[8]{0:T(128)} %constant.86.clone) | copy-start | bytes 100
  129.1 8.3 %collective-permute-start.5 = (bf16[256,512]{1,0:T(8,128)(2,1)S(1)}, bf16[256,512]{1,0:T(8,128)(2,1)S(1)}, u32[]{:S(2)}, u32[]{:S(2)}) collective-permute-start(bf16[256,512]{1,0:T(8,128)(2,1)S(1)} %collective-permute-done.3), channel_id=1, source_target_pairs={{0,2},{2,4},{4,6},{6,8},{8,10},{10,12},{12,14},{14,0},{1,3},{3,5},... | collective-permute-start | bytes 786440 | tf_op jit(solution)/shard_map/ppermute | solution.py:224
  131.0 8.3 %collective-permute-start.6 = (bf16[256,512]{1,0:T(8,128)(2,1)S(1)}, bf16[256,512]{1,0:T(8,128)(2,1)S(1)}, u32[]{:S(2)}, u32[]{:S(2)}) collective-permute-start(bf16[256,512]{1,0:T(8,128)(2,1)S(1)} %collective-permute-done.4), channel_id=1, source_target_pairs={{0,14},{2,0},{4,2},{6,4},{8,6},{10,8},{12,10},{14,12},{1,15},{3,1}... | collective-permute-start | bytes 786440 | tf_op jit(solution)/shard_map/ppermute | solution.py:225
  137.4 6.9 %collective-permute-start.7 = (bf16[128,512]{1,0:T(8,128)(2,1)S(1)}, bf16[128,512]{1,0:T(8,128)(2,1)S(1)}, u32[]{:S(2)}, u32[]{:S(2)}) collective-permute-start(bf16[128,512]{1,0:T(8,128)(2,1)S(1)} %slice.14), channel_id=1, source_target_pairs={{0,2},{2,4},{4,6},{6,8},{8,10},{10,12},{12,14},{14,0},{1,3},{3,5},... | collective-permute-start | bytes 393224 | tf_op jit(solution)/shard_map/ppermute | solution.py:230
  139.4 6.5 %collective-permute-start.8 = (bf16[128,512]{1,0:T(8,128)(2,1)S(1)}, bf16[128,512]{1,0:T(8,128)(2,1)S(1)}, u32[]{:S(2)}, u32[]{:S(2)}) collective-permute-start(bf16[128,512]{1,0:T(8,128)(2,1)S(1)} %slice.15), channel_id=1, source_target_pairs={{0,14},{2,0},{4,2},{6,4},{8,6},{10,8},{12,10},{14,12},{1,15},{3,1}... | collective-permute-start | bytes 393224 | tf_op jit(solution)/shard_map/ppermute | solution.py:231
  145.9 10.5 %collective-permute-start.9 = (bf16[2048,512]{1,0:T(8,128)(2,1)S(1)}, bf16[2048,512]{1,0:T(8,128)(2,1)}, u32[]{:S(2)}, u32[]{:S(2)}) collective-permute-start(bf16[2048,512]{1,0:T(8,128)(2,1)S(1)} %constant_dynamic-update-slice_fusion.mine_ref), channel_id=1, source_target_pairs={{0,1},{1,0},{2,3},{3,2},{4,5},{5,4},{6,7},{7,6},{8,9},{9,8},{10,11... | collective-permute-start | bytes 6291464 | tf_op jit(solution)/shard_map/ppermute | solution.py:267
  165.7 0.8 copy-start.3
  166.5 75.2 %all-to-all-start.2 = ((bf16[16,3,224,128]{3,2,1,0:T(8,128)(2,1)}), bf16[16,3,224,128]{3,2,1,0:T(8,128)(2,1)S(1)}, u32[]{:S(2)}, u32[]{:S(2)}) async-start(bf16[16,3,224,128]{3,2,1,0:T(8,128)(2,1)} %get-tuple-element.28), calls=%async_computation.2 | async-start | bytes 5505024 | tf_op jit(solution)/shard_map/all_to_all | solution.py:278
  174.3 1.0 copy-start.4
  181.2 4.8 %collective-permute-start.10 = (bf16[16,64,512]{2,1,0:T(8,128)(2,1)S(1)}, bf16[16,64,512]{2,1,0:T(8,128)(2,1)S(1)}, u32[]{:S(2)}, u32[]{:S(2)}) collective-permute-start(bf16[16,64,512]{2,1,0:T(8,128)(2,1)S(1)} %get-tuple-element.19), channel_id=1, source_target_pairs={{0,1},{1,0},{2,3},{3,2},{4,5},{5,4},{6,7},{7,6},{8,9},{9,8},{10,11... | collective-permute-start | bytes 3145736 | tf_op jit(solution)/shard_map/ppermute | solution.py:281
  187.6 18.3 %collective-permute-start.17 = (bf16[2,64,512]{2,1,0:T(8,128)(2,1)S(1)}, bf16[2,64,512]{2,1,0:T(8,128)(2,1)S(1)}, u32[]{:S(2)}, u32[]{:S(2)}) collective-permute-start(bf16[2,64,512]{2,1,0:T(8,128)(2,1)S(1)} %get-tuple-element.27), channel_id=1, source_target_pairs={{0,14},{2,0},{4,2},{6,4},{8,6},{10,8},{12,10},{14,12},{1,15},{3,1}... | collective-permute-start | bytes 393224 | tf_op jit(solution)/shard_map/ppermute | solution.py:282
  192.9 18.4 %collective-permute-start.16 = (bf16[2,64,512]{2,1,0:T(8,128)(2,1)S(1)}, bf16[2,64,512]{2,1,0:T(8,128)(2,1)S(1)}, u32[]{:S(2)}, u32[]{:S(2)}) collective-permute-start(bf16[2,64,512]{2,1,0:T(8,128)(2,1)S(1)} %get-tuple-element.26), channel_id=1, source_target_pairs={{0,12},{2,14},{4,0},{6,2},{8,4},{10,6},{12,8},{14,10},{1,13},{3,15... | collective-permute-start | bytes 393224 | tf_op jit(solution)/shard_map/ppermute | solution.py:282
  194.8 19.1 %collective-permute-start.15 = (bf16[2,64,512]{2,1,0:T(8,128)(2,1)}, bf16[2,64,512]{2,1,0:T(8,128)(2,1)}, u32[]{:S(2)}, u32[]{:S(2)}) collective-permute-start(bf16[2,64,512]{2,1,0:T(8,128)(2,1)} %get-tuple-element.25), channel_id=1, source_target_pairs={{0,10},{2,12},{4,14},{6,0},{8,2},{10,4},{12,6},{14,8},{1,11},{3,13... | collective-permute-start | bytes 393224 | tf_op jit(solution)/shard_map/ppermute | solution.py:282
  198.7 17.0 %collective-permute-start.14 = (bf16[2,64,512]{2,1,0:T(8,128)(2,1)}, bf16[2,64,512]{2,1,0:T(8,128)(2,1)}, u32[]{:S(2)}, u32[]{:S(2)}) collective-permute-start(bf16[2,64,512]{2,1,0:T(8,128)(2,1)} %get-tuple-element.24), channel_id=1, source_target_pairs={{0,8},{2,10},{4,12},{6,14},{8,0},{10,2},{12,4},{14,6},{1,9},{3,11}... | collective-permute-start | bytes 393224 | tf_op jit(solution)/shard_map/ppermute | solution.py:282
  204.0 18.3 %collective-permute-start.13 = (bf16[2,64,512]{2,1,0:T(8,128)(2,1)}, bf16[2,64,512]{2,1,0:T(8,128)(2,1)}, u32[]{:S(2)}, u32[]{:S(2)}) collective-permute-start(bf16[2,64,512]{2,1,0:T(8,128)(2,1)} %get-tuple-element.23), channel_id=1, source_target_pairs={{0,6},{2,8},{4,10},{6,12},{8,14},{10,0},{12,2},{14,4},{1,7},{3,9},... | collective-permute-start | bytes 393224 | tf_op jit(solution)/shard_map/ppermute | solution.py:282
  206.0 5.4 %copy-start.8 = (bf16[2,64,512]{2,1,0:T(8,128)(2,1)}, bf16[2,64,512]{2,1,0:T(8,128)(2,1)S(1)}, u32[]{:S(2)}) copy-start(bf16[2,64,512]{2,1,0:T(8,128)(2,1)S(1)} %collective-permute-done.17) | copy-start | bytes 393220
  206.0 17.5 %collective-permute-start.12 = (bf16[2,64,512]{2,1,0:T(8,128)(2,1)}, bf16[2,64,512]{2,1,0:T(8,128)(2,1)}, u32[]{:S(2)}, u32[]{:S(2)}) collective-permute-start(bf16[2,64,512]{2,1,0:T(8,128)(2,1)} %get-tuple-element.22), channel_id=1, source_target_pairs={{0,4},{2,6},{4,8},{6,10},{8,12},{10,14},{12,0},{14,2},{1,5},{3,7},... | collective-permute-start | bytes 393224 | tf_op jit(solution)/shard_map/ppermute | solution.py:282
  212.0 15.2 %collective-permute-start.11 = (bf16[2,64,512]{2,1,0:T(8,128)(2,1)}, bf16[2,64,512]{2,1,0:T(8,128)(2,1)}, u32[]{:S(2)}, u32[]{:S(2)}) collective-permute-start(bf16[2,64,512]{2,1,0:T(8,128)(2,1)} %get-tuple-element.21), channel_id=1, source_target_pairs={{0,2},{2,4},{4,6},{6,8},{8,10},{10,12},{12,14},{14,0},{1,3},{3,5},... | collective-permute-start | bytes 393224 | tf_op jit(solution)/shard_map/ppermute | solution.py:282
  228.7 0.7 copy-start.7
  230.1 9.1 %collective-permute-start.18 = (f32[64,512]{1,0:T(8,128)}, f32[64,512]{1,0:T(8,128)}, u32[]{:S(2)}, u32[]{:S(2)}) collective-permute-start(f32[64,512]{1,0:T(8,128)} %dynamic-slice_bitcast_fusion), channel_id=1, source_target_pairs={{0,16},{16,0},{1,17},{17,1},{2,18},{18,2},{3,19},{19,3},{4,20},{20... | collective-permute-start | bytes 393224 | tf_op jit(solution)/shard_map/ppermute | solution.py:287
  241.6 1.3 copy-start.2
  (2 other events, 1.3 us)

commit v3 on v2

--- a/solution.py
+++ b/solution.py
@@ -13,23 +13,28 @@
 
 PATH = ("yh", "x")
 SHARD = ("yl", "z", "c")
-VMEM_LIMIT = 48 * 1024 * 1024
-
-
-def grads_kernel(tile_ref, core_ref, w_ref, mine_ref, other_ref, delta_ref, dgu_ref, xp, yp, g_s, u_s, d_s, h_s):
+VMEM_LIMIT = 24 * 1024 * 1024
+
+
+def place_kernel(place_ref, core_ref, mine_ref, other_ref, xp_ref, yp_ref):
+    owners = place_ref.shape[0]
+    width = mine_ref.shape[0] // owners
+    first = core_ref[0] == 0
+
+    def one(o, carry):
+        here = pl.ds(pl.multiple_of(place_ref[o] * width, width), width)
+        to = pl.ds(pl.multiple_of(o * width, width), width)
+        a = mine_ref[here, :]
+        b = other_ref[here, :]
+        xp_ref[to, :] = jnp.where(first, a, b)
+        yp_ref[to, :] = jnp.where(first, b, a)
+        return carry
+
+    lax.fori_loop(0, owners, one, 0)
+
+
+def grads_kernel(w_ref, xp, yp, delta_ref, dgu_ref, g_s, u_s, d_s, h_s):
     owners, _, units, width = w_ref.shape
-    core = core_ref[0]
-
-    def place(o, carry):
-        j = pl.multiple_of(tile_ref[o] * width, width)
-        to = pl.multiple_of(o * width, width)
-        a = mine_ref[pl.ds(j, width), :]
-        b = other_ref[pl.ds(j, width), :]
-        xp[pl.ds(to, width), :] = jnp.where(core == 0, a, b)
-        yp[pl.ds(to, width), :] = jnp.where(core == 0, b, a)
-        return carry
-
-    lax.fori_loop(0, owners, place, 0)
 
     def matrix(k):
         return jnp.concatenate([w_ref[o, k] for o in range(owners)], axis=1)
@@ -115,10 +120,23 @@
         new_w_ref[m, 0] = weight_ref[m, 0].astype(jnp.float32) - LR_OUTER * (mean + MU * moment)
 
 
-def grads(tile_of, core, w, mine, other):
+def in_owner_order(place, core, mine, other):
+    smem = pl.BlockSpec(memory_space=pltpu.SMEM)
+    vmem = pl.BlockSpec(memory_space=pltpu.VMEM)
+    return pl.pallas_call(
+        place_kernel,
+        out_shape=(jax.ShapeDtypeStruct(mine.shape, mine.dtype),) * 2,
+        in_specs=[smem, smem, vmem, vmem],
+        out_specs=(vmem, vmem),
+        compiler_params=pltpu.CompilerParams(vmem_limit_bytes=VMEM_LIMIT),
+        cost_estimate=pl.CostEstimate(flops=1000, bytes_accessed=1000, transcendentals=0),
+        name="in_owner_order",
+    )(place, core, mine, other)
+
+
+def grads(w, xp, yp):
     owners, _, units, width = w.shape
-    rows = mine.shape[1]
-    smem = pl.BlockSpec(memory_space=pltpu.SMEM)
+    rows = xp.shape[1]
     vmem = pl.BlockSpec(memory_space=pltpu.VMEM)
     return pl.pallas_call(
         grads_kernel,
@@ -126,11 +144,9 @@
             jax.ShapeDtypeStruct(w.shape, jnp.bfloat16),
             jax.ShapeDtypeStruct((2 * units, rows), jnp.bfloat16),
         ),
-        in_specs=[smem, smem, vmem, vmem, vmem],
+        in_specs=[vmem, vmem, vmem],
         out_specs=(vmem, vmem),
         scratch_shapes=[
-            pltpu.VMEM(mine.shape, jnp.bfloat16),
-            pltpu.VMEM(mine.shape, jnp.bfloat16),
             pltpu.VMEM((units, rows), jnp.float32),
             pltpu.VMEM((units, rows), jnp.float32),
             pltpu.VMEM((units, rows), jnp.float32),
@@ -141,7 +157,7 @@
             flops=12 * units * rows * owners * width, bytes_accessed=12 * 2**20, transcendentals=units * rows
         ),
         name="grads",
-    )(tile_of, core, w, mine, other)
+    )(w, xp, yp)
 
 
 def input_partial(slot_of, core, w, dgu):
@@ -211,9 +227,8 @@
     return [(i, (i + k) % size) for i in range(size)]
 
 
-def ring_gather(piece):
+def ring_gather(piece, beside):
     depth = lax.axis_size("z")
-    beside = lax.ppermute(piece, "yl", [(0, 1), (1, 0)])
     first = lax.axis_index("yl") == 0
     pair = jnp.concatenate([jnp.where(first, piece, beside), jnp.where(first, beside, piece)], axis=0)
     half = piece.shape[0]
@@ -242,9 +257,6 @@
     cols = tokens.shape[1]
     owned = weights[0]
 
-    send_w = pick(owned, modules_of)
-    recv_w = lax.all_to_all(send_w, PATH, split_axis=0, concat_axis=0, tiled=True)
-
     def feature_major(array):
         return array.reshape(blocks, BLK, cols).transpose(0, 2, 1)
 
@@ -262,7 +274,10 @@
     sources = jnp.sum(jnp.where(comes, path_ids[None, :], 0), axis=1)
     piece = pick(recv_x, sources).transpose(1, 2, 0, 3).reshape(2 * cols, blocks * BLK)
 
-    mine, at = ring_gather(piece)
+    beside = lax.ppermute(piece, "yl", [(0, 1), (1, 0)])
+    send_w, piece, beside = lax.optimization_barrier((pick(owned, modules_of), piece, beside))
+    recv_w = lax.all_to_all(send_w, PATH, split_axis=0, concat_axis=0, tiled=True)
+    mine, at = ring_gather(piece, beside)
     swap = [(0, 1), (1, 0)]
     other = lax.ppermute(mine, "c", swap)
 
@@ -274,7 +289,8 @@
     side = tile_of // depth
     place = jnp.sum(jnp.where(away[:, None] == jnp.arange(depth)[None, :], jnp.array(at, jnp.int32)[None, :], 0), axis=1)
     core_id = core.reshape(1)
-    delta, dgu = grads(place * 2 + side, core_id, recv_w, mine, other)
+    xp, yp = in_owner_order(place * 2 + side, core_id, mine, other)
+    delta, dgu = grads(recv_w, xp, yp)
     recv_delta = lax.all_to_all(delta, PATH, split_axis=0, concat_axis=0, tiled=True)
 
     keep, give = input_partial(away * 2 + side, core_id, recv_w, dgu)
@@ -284,6 +300,7 @@
     for part in came:
         total = total + part.astype(jnp.float32)
     yl = lax.axis_index("yl")
+    total, recv_delta = lax.optimization_barrier((total, recv_delta))
     theirs = lax.ppermute(lax.dynamic_index_in_dim(total, 1 - yl, 0, keepdims=False), "yl", swap)
     total = lax.dynamic_index_in_dim(total, yl, 0, keepdims=False) + theirs
     input_grad = total.astype(jnp.bfloat16).T

time: 249 us -> 207 us (0.83)
  waiting for transfers between devices: 111 us -> 58.2 us
  local copies, waits for them, and re-layouts: 13.6 us -> 23.1 us
  starting transfers between devices: 94.2 us -> 97 us
    ppermute x1, waiting for transfers between devices: 61.3 us -> 2.09 us  [body(): beside = lax.ppermute(piece, 'yl', [(0, 1), (1, 0)])]
    unnamed x32 -> x38, local copies, waits for them, and re-layouts: 5.34 us -> 14.9 us
    all_to_all x1, waiting for transfers between devices: 0.8 us -> 9.33 us  [body(): lax.all_to_all(delta, PATH, split_axis=0, concat_axis=0, tiled=True)]
    ppermute x1, waiting for transfers between devices: 6.97 us -> 0.01 us  [body(): lax.ppermute(lax.dynamic_index_in_dim(total, 1 - yl, 0, keepdims=False),...]
    all_to_all x1, waiting for transfers between devices: 0.01 us -> 5.37 us  [body(): lax.all_to_all(send_w, PATH, split_axis=0, concat_axis=0, tiled=True)]
    ppermute x7, starting transfers between devices: 25.6 us -> 30.5 us  [body(): came = [lax.ppermute(sums[k], 'z', turn(depth, k)) for k in range(1, depth)]]
    pallas_call x1, Pallas kernels: 9.37 us -> 5.01 us  [grads(): pl.pallas_call(grads_kernel, out_shape=(jax.ShapeDtypeStruct(w.shape, jnp...]
    ppermute x3, waiting for transfers between devices: 8.46 us -> 4.89 us  [ring_gather(): up = lax.ppermute(up, 'z', turn(depth, 1))]
  transfers between devices with their start and end apart: 22 -> 22, of which waited for: 15 -> 11; matrix products, arithmetic and copies ran while one was open for 4% -> 7% of each run, Pallas kernels for 3% -> 6%
where the time goes in v3:
time: 207 us; the launch traced here: 206 us
  starting transfers between devices  97 us (47%)
  waiting for transfers between devices  58.2 us (28%)
  local copies, waits for them, and re-layouts  23.1 us (11%)
  Pallas kernels  18 us (9%)
  other arithmetic  6.63 us (3%)
  between operations  3.08 us (1%)
    ppermute x7, starting transfers between devices, body(): came = [lax.ppermute(sums[k], 'z', turn(depth, k)) for k in range(1, depth)]  30.5 us
    all_to_all x1, waiting for transfers between devices, body(): lax.all_to_all(send_x.reshape(paths * 2, cols, BLK), PATH + ('c',), split...  17.9 us
    ppermute x3, starting transfers between devices, ring_gather(): down = lax.ppermute(down, 'z', turn(depth, -1))  17.7 us
    ppermute x7, waiting for transfers between devices, body(): came = [lax.ppermute(sums[k], 'z', turn(depth, k)) for k in range(1, depth)]  15.7 us
    unnamed x38, local copies, waits for them, and re-layouts  14.9 us
    all_to_all x1, starting transfers between devices, body(): lax.all_to_all(send_x.reshape(paths * 2, cols, BLK), PATH + ('c',), split...  11.2 us
    all_to_all x1, waiting for transfers between devices, body(): lax.all_to_all(delta, PATH, split_axis=0, concat_axis=0, tiled=True)  9.33 us
    ppermute x3, starting transfers between devices, ring_gather(): up = lax.ppermute(up, 'z', turn(depth, 1))  7.82 us
  transfers between devices with their start and end apart: 22, of which 11 were waited for; matrix products, arithmetic and copies ran while one was open for 7% of the time, Pallas kernels for 6%

profile of v3, /device:TPU:1, one launch (start us, length us, event | category | flops | bytes accessed | tf_op | source)
XLA Modules:
  0.0 206.1 jit_solution(7690801809826434484)
XLA Ops:
  4.5 11.2 %all-to-all-start = ((bf16[32,64,128]{2,1,0:T(8,128)(2,1)}), bf16[32,64,128]{2,1,0:T(8,128)(2,1)S(1)}, u32[]{:S(2)}, u32[]{:S(2)}) async-start(bf16[32,64,128]{2,1,0:T(8,128)(2,1)} %bitcast.11), calls=%async_computation | async-start | bytes 1048576 | tf_op jit(solution)/shard_map/all_to_all | solution.py:268
  16.3 17.9 %all-to-all-done = bf16[32,64,128]{2,1,0:T(8,128)(2,1)S(1)} async-done(((bf16[32,64,128]{2,1,0:T(8,128)(2,1)}), bf16[32,64,128]{2,1,0:T(8,128)(2,1)S(1)}, u32[]{:S(2)}, u32[]{:S(2)}) %all-to-all-start) | async-done | bytes 524320 | tf_op jit(solution)/shard_map/all_to_all | solution.py:268
  34.9 1.9 collective-permute-start
  36.9 2.4 %gather_fusion = bf16[16,3,224,128]{3,2,1,0:T(8,128)(2,1)} fusion(bf16[4,3,224,128]{3,2,1,0:T(8,128)(2,1)S(1)} %bitcast.55, s32[1024]{0:T(1024)S(1)} %pad_clamp_fusion.2), kind=kCustom, calls=%fused_computation | custom fusion | bytes 5505088 | tf_op jit(solution)/shard_map/gather | solution.py:223
  39.3 2.1 %collective-permute-done = bf16[128,512]{1,0:T(8,128)(2,1)S(1)} collective-permute-done((bf16[128,512]{1,0:T(8,128)(2,1)S(1)}, bf16[128,512]{1,0:T(8,128)(2,1)S(1)}, u32[]{:S(2)}, u32[]{:S(2)}) %collective-permute-start) | collective-permute-done | bytes 131104 | tf_op jit(solution)/shard_map/ppermute | solution.py:277
  42.0 3.9 %all-to-all-start.1 = ((bf16[16,3,224,128]{3,2,1,0:T(8,128)(2,1)}), bf16[16,3,224,128]{3,2,1,0:T(8,128)(2,1)S(1)}, u32[]{:S(2)}, u32[]{:S(2)}) async-start(bf16[16,3,224,128]{3,2,1,0:T(8,128)(2,1)} %gather_fusion), calls=%async_computation.1 | async-start | bytes 5505024 | tf_op jit(solution)/shard_map/all_to_all | solution.py:279
  49.2 4.0 %collective-permute-start.1 = (bf16[256,512]{1,0:T(8,128)(2,1)S(1)}, bf16[256,512]{1,0:T(8,128)(2,1)S(1)}, u32[]{:S(2)}, u32[]{:S(2)}) collective-permute-start(bf16[256,512]{1,0:T(8,128)(2,1)S(1)} %pad_maximum_fusion), channel_id=1, source_target_pairs={{0,2},{2,4},{4,6},{6,8},{8,10},{10,12},{12,14},{14,0},{1,3},{3,5},... | collective-permute-start | bytes 786440 | tf_op jit(solution)/shard_map/ppermute | solution.py:239
  53.2 8.6 %collective-permute-start.2 = (bf16[256,512]{1,0:T(8,128)(2,1)S(1)}, bf16[256,512]{1,0:T(8,128)(2,1)S(1)}, u32[]{:S(2)}, u32[]{:S(2)}) collective-permute-start(bf16[256,512]{1,0:T(8,128)(2,1)S(1)} %pad_maximum_fusion), channel_id=1, source_target_pairs={{0,14},{2,0},{4,2},{6,4},{8,6},{10,8},{12,10},{14,12},{1,15},{3,1}... | collective-permute-start | bytes 786440 | tf_op jit(solution)/shard_map/ppermute | solution.py:240
  61.8 3.3 %collective-permute-done.1 = bf16[256,512]{1,0:T(8,128)(2,1)S(1)} collective-permute-done((bf16[256,512]{1,0:T(8,128)(2,1)S(1)}, bf16[256,512]{1,0:T(8,128)(2,1)S(1)}, u32[]{:S(2)}, u32[]{:S(2)}) %collective-permute-start.1) | collective-permute-done | bytes 262176 | tf_op jit(solution)/shard_map/ppermute | solution.py:239
  67.0 4.6 %collective-permute-start.4 = (bf16[256,512]{1,0:T(8,128)(2,1)S(1)}, bf16[256,512]{1,0:T(8,128)(2,1)S(1)}, u32[]{:S(2)}, u32[]{:S(2)}) collective-permute-start(bf16[256,512]{1,0:T(8,128)(2,1)S(1)} %collective-permute-done.2), channel_id=1, source_target_pairs={{0,14},{2,0},{4,2},{6,4},{8,6},{10,8},{12,10},{14,12},{1,15},{3,1}... | collective-permute-start | bytes 786440 | tf_op jit(solution)/shard_map/ppermute | solution.py:240
  75.9 4.6 %collective-permute-start.6 = (bf16[256,512]{1,0:T(8,128)(2,1)S(1)}, bf16[256,512]{1,0:T(8,128)(2,1)S(1)}, u32[]{:S(2)}, u32[]{:S(2)}) collective-permute-start(bf16[256,512]{1,0:T(8,128)(2,1)S(1)} %collective-permute-done.4), channel_id=1, source_target_pairs={{0,14},{2,0},{4,2},{6,4},{8,6},{10,8},{12,10},{14,12},{1,15},{3,1}... | collective-permute-start | bytes 786440 | tf_op jit(solution)/shard_map/ppermute | solution.py:240
  84.6 4.6 %collective-permute-start.8 = (bf16[128,512]{1,0:T(8,128)(2,1)S(1)}, bf16[128,512]{1,0:T(8,128)(2,1)S(1)}, u32[]{:S(2)}, u32[]{:S(2)}) collective-permute-start(bf16[128,512]{1,0:T(8,128)(2,1)S(1)} %slice.15), channel_id=1, source_target_pairs={{0,14},{2,0},{4,2},{6,4},{8,6},{10,8},{12,10},{14,12},{1,15},{3,1}... | collective-permute-start | bytes 393224 | tf_op jit(solution)/shard_map/ppermute | solution.py:246
  92.0 6.6 %collective-permute-start.9 = (bf16[2048,512]{1,0:T(8,128)(2,1)}, bf16[2048,512]{1,0:T(8,128)(2,1)}, u32[]{:S(2)}, u32[]{:S(2)}) collective-permute-start(bf16[2048,512]{1,0:T(8,128)(2,1)} %constant_dynamic-update-slice_fusion.mine_ref), channel_id=1, source_target_pairs={{0,1},{1,0},{2,3},{3,2},{4,5},{5,4},{6,7},{7,6},{8,9},{9,8},{10,11... | collective-permute-start | bytes 6291464 | tf_op jit(solution)/shard_map/ppermute | solution.py:282
  102.7 2.6 %in_owner_order.1 = (bf16[2048,512]{1,0:T(8,128)(2,1)S(1)}, bf16[2048,512]{1,0:T(8,128)(2,1)S(1)}) custom-call(s32[16]{0:T(128)S(1)} %get-tuple-element.49.place_ref, s32[1]{0:T(128)} %bitcast.2.core_ref, bf16[2048,512]{1,0:T(8,128)(2,1)} %constant_dynamic-update-slice_fusion.mine_ref, bf16[2048,512]{1,0:T(8,128)(2,1)} %collective-permute-done.9.other_ref), custom_call_target="tpu_custom_call" | custom-call | flops 1000 | bytes 1000 | tf_op jit(solution)/shard_map/in_owner_order/pallas_call | solution.py:126
  108.0 5.4 %all-to-all-done.1.w_ref = bf16[16,3,224,128]{3,2,1,0:T(8,128)(2,1)S(1)} async-done(((bf16[16,3,224,128]{3,2,1,0:T(8,128)(2,1)}), bf16[16,3,224,128]{3,2,1,0:T(8,128)(2,1)S(1)}, u32[]{:S(2)}, u32[]{:S(2)}) %all-to-all-start.1) | async-done | bytes 2752544 | tf_op jit(solution)/shard_map/all_to_all | solution.py:279
  116.6 5.0 %grads.1 = (bf16[16,3,224,128]{3,2,1,0:T(8,128)(2,1)S(1)}, bf16[448,512]{1,0:T(8,128)(2,1)S(1)}) custom-call(bf16[16,3,224,128]{3,2,1,0:T(8,128)(2,1)S(1)} %all-to-all-done.1.w_ref, bf16[2048,512]{1,0:T(8,128)(2,1)S(1)} %copy-done.8, bf16[2048,512]{1,0:T(8,128)(2,1)S(1)} %copy-done.10), custom_call_target="tpu_custom_call" | custom-call | flops 2818572288 | bytes 12582912 | tf_op jit(solution)/shard_map/grads/pallas_call | solution.py:141
  123.9 5.7 %all-to-all-start.2 = ((bf16[16,3,224,128]{3,2,1,0:T(8,128)(2,1)}), bf16[16,3,224,128]{3,2,1,0:T(8,128)(2,1)}, u32[]{:S(2)}, u32[]{:S(2)}) async-start(bf16[16,3,224,128]{3,2,1,0:T(8,128)(2,1)} %copy-done.2), calls=%async_computation.2 | async-start | bytes 5505024 | tf_op jit(solution)/shard_map/all_to_all | solution.py:294
  130.7 4.6 %input_partial.1 = (f32[16,64,512]{2,1,0:T(8,128)S(1)}, bf16[16,64,512]{2,1,0:T(8,128)(2,1)S(1)}) custom-call(s32[16]{0:T(128)S(1)} %multiply_add_fusion.1.slot_ref, s32[1]{0:T(128)} %bitcast.2.core_ref, bf16[16,3,224,128]{3,2,1,0:T(8,128)(2,1)S(1)} %all-to-all-done.1.w_ref, bf16[448,512]{1,0:T(8,128)(2,1)S(1)} %copy-done.5), custom_call_target="tpu_custom_call" | custom-call | flops 1000 | bytes 1000 | tf_op jit(solution)/shard_map/input_partial/pallas_call | solution.py:169
  135.2 3.1 %collective-permute-start.10 = (bf16[16,64,512]{2,1,0:T(8,128)(2,1)S(1)}, bf16[16,64,512]{2,1,0:T(8,128)(2,1)S(1)}, u32[]{:S(2)}, u32[]{:S(2)}) collective-permute-start(bf16[16,64,512]{2,1,0:T(8,128)(2,1)S(1)} %get-tuple-element.31), channel_id=1, source_target_pairs={{0,1},{1,0},{2,3},{3,2},{4,5},{5,4},{6,7},{7,6},{8,9},{9,8},{10,11... | collective-permute-start | bytes 3145736 | tf_op jit(solution)/shard_map/ppermute | solution.py:297
  138.3 2.3 %collective-permute-done.10.came_ref = bf16[16,64,512]{2,1,0:T(8,128)(2,1)S(1)} collective-permute-done((bf16[16,64,512]{2,1,0:T(8,128)(2,1)S(1)}, bf16[16,64,512]{2,1,0:T(8,128)(2,1)S(1)}, u32[]{:S(2)}, u32[]{:S(2)}) %collective-permute-start.10) | collective-permute-done | bytes 1048608 | tf_op jit(solution)/shard_map/ppermute | solution.py:297
  140.8 10.8 %collective-permute-start.17 = (bf16[2,64,512]{2,1,0:T(8,128)(2,1)S(1)}, bf16[2,64,512]{2,1,0:T(8,128)(2,1)S(1)}, u32[]{:S(2)}, u32[]{:S(2)}) collective-permute-start(bf16[2,64,512]{2,1,0:T(8,128)(2,1)S(1)} %get-tuple-element.39), channel_id=1, source_target_pairs={{0,14},{2,0},{4,2},{6,4},{8,6},{10,8},{12,10},{14,12},{1,15},{3,1}... | collective-permute-start | bytes 393224 | tf_op jit(solution)/shard_map/ppermute | solution.py:298
  151.6 2.2 %collective-permute-start.16 = (bf16[2,64,512]{2,1,0:T(8,128)(2,1)S(1)}, bf16[2,64,512]{2,1,0:T(8,128)(2,1)S(1)}, u32[]{:S(2)}, u32[]{:S(2)}) collective-permute-start(bf16[2,64,512]{2,1,0:T(8,128)(2,1)S(1)} %get-tuple-element.38), channel_id=1, source_target_pairs={{0,12},{2,14},{4,0},{6,2},{8,4},{10,6},{12,8},{14,10},{1,13},{3,15... | collective-permute-start | bytes 393224 | tf_op jit(solution)/shard_map/ppermute | solution.py:298
  153.8 1.9 collective-permute-start.15
  155.7 7.3 %collective-permute-start.14 = (bf16[2,64,512]{2,1,0:T(8,128)(2,1)S(1)}, bf16[2,64,512]{2,1,0:T(8,128)(2,1)}, u32[]{:S(2)}, u32[]{:S(2)}) collective-permute-start(bf16[2,64,512]{2,1,0:T(8,128)(2,1)S(1)} %get-tuple-element.36), channel_id=1, source_target_pairs={{0,8},{2,10},{4,12},{6,14},{8,0},{10,2},{12,4},{14,6},{1,9},{3,11}... | collective-permute-start | bytes 393224 | tf_op jit(solution)/shard_map/ppermute | solution.py:298
  163.0 1.9 collective-permute-start.13
  164.9 3.1 %collective-permute-start.12 = (bf16[2,64,512]{2,1,0:T(8,128)(2,1)S(1)}, bf16[2,64,512]{2,1,0:T(8,128)(2,1)}, u32[]{:S(2)}, u32[]{:S(2)}) collective-permute-start(bf16[2,64,512]{2,1,0:T(8,128)(2,1)S(1)} %get-tuple-element.34), channel_id=1, source_target_pairs={{0,4},{2,6},{4,8},{6,10},{8,12},{10,14},{12,0},{14,2},{1,5},{3,7},... | collective-permute-start | bytes 393224 | tf_op jit(solution)/shard_map/ppermute | solution.py:298
  168.0 3.3 %collective-permute-start.11 = (bf16[2,64,512]{2,1,0:T(8,128)(2,1)S(1)}, bf16[2,64,512]{2,1,0:T(8,128)(2,1)}, u32[]{:S(2)}, u32[]{:S(2)}) collective-permute-start(bf16[2,64,512]{2,1,0:T(8,128)(2,1)S(1)} %get-tuple-element.33), channel_id=1, source_target_pairs={{0,2},{2,4},{4,6},{6,8},{8,10},{10,12},{12,14},{14,0},{1,3},{3,5},... | collective-permute-start | bytes 393224 | tf_op jit(solution)/shard_map/ppermute | solution.py:298
  171.4 6.1 %collective-permute-done.13 = bf16[2,64,512]{2,1,0:T(8,128)(2,1)} collective-permute-done((bf16[2,64,512]{2,1,0:T(8,128)(2,1)S(1)}, bf16[2,64,512]{2,1,0:T(8,128)(2,1)}, u32[]{:S(2)}, u32[]{:S(2)}) %collective-permute-start.13) | collective-permute-done | bytes 131104 | tf_op jit(solution)/shard_map/ppermute | solution.py:298
  177.5 5.5 %collective-permute-done.12 = bf16[2,64,512]{2,1,0:T(8,128)(2,1)} collective-permute-done((bf16[2,64,512]{2,1,0:T(8,128)(2,1)S(1)}, bf16[2,64,512]{2,1,0:T(8,128)(2,1)}, u32[]{:S(2)}, u32[]{:S(2)}) %collective-permute-start.12) | collective-permute-done | bytes 131104 | tf_op jit(solution)/shard_map/ppermute | solution.py:298
  183.1 4.0 %collective-permute-done.11 = bf16[2,64,512]{2,1,0:T(8,128)(2,1)} collective-permute-done((bf16[2,64,512]{2,1,0:T(8,128)(2,1)S(1)}, bf16[2,64,512]{2,1,0:T(8,128)(2,1)}, u32[]{:S(2)}, u32[]{:S(2)}) %collective-permute-start.11) | collective-permute-done | bytes 131104 | tf_op jit(solution)/shard_map/ppermute | solution.py:298
  188.4 9.3 %all-to-all-done.2.delta_ref = bf16[16,3,224,128]{3,2,1,0:T(8,128)(2,1)} async-done(((bf16[16,3,224,128]{3,2,1,0:T(8,128)(2,1)}), bf16[16,3,224,128]{3,2,1,0:T(8,128)(2,1)}, u32[]{:S(2)}, u32[]{:S(2)}) %all-to-all-start.2) | async-done | bytes 2752544 | tf_op jit(solution)/shard_map/all_to_all | solution.py:294
  199.8 5.6 %update.1 = (f32[4,3,224,128]{3,2,1,0:T(8,128)}, f32[4,3,224,128]{3,2,1,0:T(8,128)}) custom-call(s32[16]{0:T(128)S(1)} %bitcast.59, f32[4]{0:T(128)S(1)} %convert_reduce_fusion.1.count_ref, bf16[16,3,224,128]{3,2,1,0:T(8,128)(2,1)} %all-to-all-done.2.delta_ref, bf16[4,3,224,128]{3,2,1,0:T(8,128)(2,1)S(1)} %bitcast.56, f32[4,3,224,128]{3,2,1,0:T(8,128)S(1)} %bitcast.57), custom_call_target="tpu_custom_call" | custom-call | flops 1000000 | bytes 8388608 | tf_op jit(solution)/shard_map/update/pallas_call | solution.py:203
  (90 shorter events, 37.4 us)
Async XLA Ops:
  0.6 1.6 copy-start
  0.6 15.1 %copy-start.13 = (s32[64]{0:T(128)S(1)}, s32[64]{0:T(128)}, u32[]{:S(2)}) copy-start(s32[64]{0:T(128)} %param.12) | copy-start | bytes 772
  0.7 36.2 %copy-start.1 = (bf16[1,4,3,224,128]{4,3,2,1,0:T(8,128)(2,1)S(1)}, bf16[1,4,3,224,128]{4,3,2,1,0:T(8,128)(2,1)}, u32[]{:S(2)}) copy-start(bf16[1,4,3,224,128]{4,3,2,1,0:T(8,128)(2,1)} %param.10) | copy-start | bytes 2064388
  4.5 29.6 %all-to-all-start = ((bf16[32,64,128]{2,1,0:T(8,128)(2,1)}), bf16[32,64,128]{2,1,0:T(8,128)(2,1)S(1)}, u32[]{:S(2)}, u32[]{:S(2)}) async-start(bf16[32,64,128]{2,1,0:T(8,128)(2,1)} %bitcast.11), calls=%async_computation | async-start | bytes 1048576 | tf_op jit(solution)/shard_map/all_to_all | solution.py:268
  34.9 4.4 %copy-start.11 = (bf16[16,8,4,128]{3,1,2,0:T(8,128)(2,1)}, bf16[16,8,4,128]{3,1,2,0:T(8,128)(2,1)S(1)}, u32[]{:S(2)}) copy-start(bf16[16,8,4,128]{3,1,2,0:T(8,128)(2,1)S(1)} %copy.24) | copy-start | bytes 393220
  34.9 6.5 %collective-permute-start = (bf16[128,512]{1,0:T(8,128)(2,1)S(1)}, bf16[128,512]{1,0:T(8,128)(2,1)S(1)}, u32[]{:S(2)}, u32[]{:S(2)}) collective-permute-start(bf16[128,512]{1,0:T(8,128)(2,1)S(1)} %bitcast.60), channel_id=1, source_target_pairs={{0,16},{16,0},{1,17},{17,1},{2,18},{18,2},{3,19},{19,3},{4,20},{20... | collective-permute-start | bytes 393224 | tf_op jit(solution)/shard_map/ppermute | solution.py:277
  42.0 71.3 %all-to-all-start.1 = ((bf16[16,3,224,128]{3,2,1,0:T(8,128)(2,1)}), bf16[16,3,224,128]{3,2,1,0:T(8,128)(2,1)S(1)}, u32[]{:S(2)}, u32[]{:S(2)}) async-start(bf16[16,3,224,128]{3,2,1,0:T(8,128)(2,1)} %gather_fusion), calls=%async_computation.1 | async-start | bytes 5505024 | tf_op jit(solution)/shard_map/all_to_all | solution.py:279
  49.2 15.9 %collective-permute-start.1 = (bf16[256,512]{1,0:T(8,128)(2,1)S(1)}, bf16[256,512]{1,0:T(8,128)(2,1)S(1)}, u32[]{:S(2)}, u32[]{:S(2)}) collective-permute-start(bf16[256,512]{1,0:T(8,128)(2,1)S(1)} %pad_maximum_fusion), channel_id=1, source_target_pairs={{0,2},{2,4},{4,6},{6,8},{8,10},{10,12},{12,14},{14,0},{1,3},{3,5},... | collective-permute-start | bytes 786440 | tf_op jit(solution)/shard_map/ppermute | solution.py:239
  53.2 13.8 %collective-permute-start.2 = (bf16[256,512]{1,0:T(8,128)(2,1)S(1)}, bf16[256,512]{1,0:T(8,128)(2,1)S(1)}, u32[]{:S(2)}, u32[]{:S(2)}) collective-permute-start(bf16[256,512]{1,0:T(8,128)(2,1)S(1)} %pad_maximum_fusion), channel_id=1, source_target_pairs={{0,14},{2,0},{4,2},{6,4},{8,6},{10,8},{12,10},{14,12},{1,15},{3,1}... | collective-permute-start | bytes 786440 | tf_op jit(solution)/shard_map/ppermute | solution.py:240
  65.1 8.9 %collective-permute-start.3 = (bf16[256,512]{1,0:T(8,128)(2,1)S(1)}, bf16[256,512]{1,0:T(8,128)(2,1)S(1)}, u32[]{:S(2)}, u32[]{:S(2)}) collective-permute-start(bf16[256,512]{1,0:T(8,128)(2,1)S(1)} %collective-permute-done.1), channel_id=1, source_target_pairs={{0,2},{2,4},{4,6},{6,8},{8,10},{10,12},{12,14},{14,0},{1,3},{3,5},... | collective-permute-start | bytes 786440 | tf_op jit(solution)/shard_map/ppermute | solution.py:239
  67.0 8.8 %collective-permute-start.4 = (bf16[256,512]{1,0:T(8,128)(2,1)S(1)}, bf16[256,512]{1,0:T(8,128)(2,1)S(1)}, u32[]{:S(2)}, u32[]{:S(2)}) collective-permute-start(bf16[256,512]{1,0:T(8,128)(2,1)S(1)} %collective-permute-done.2), channel_id=1, source_target_pairs={{0,14},{2,0},{4,2},{6,4},{8,6},{10,8},{12,10},{14,12},{1,15},{3,1}... | collective-permute-start | bytes 786440 | tf_op jit(solution)/shard_map/ppermute | solution.py:240
  71.6 27.0 %copy-start.6 = (s32[16,1]{0,1:T(1,128)S(1)}, s32[16,1]{0,1:T(1,128)}, u32[]{:S(2)}) copy-start(s32[16,1]{0,1:T(1,128)} %param.13) | copy-start | bytes 196
  71.6 30.3 %copy-start.14 = (s32[8]{0:T(128)S(1)}, s32[8]{0:T(128)}, u32[]{:S(2)}) copy-start(s32[8]{0:T(128)} %constant.86.clone) | copy-start | bytes 100
  73.9 8.6 %collective-permute-start.5 = (bf16[256,512]{1,0:T(8,128)(2,1)S(1)}, bf16[256,512]{1,0:T(8,128)(2,1)S(1)}, u32[]{:S(2)}, u32[]{:S(2)}) collective-permute-start(bf16[256,512]{1,0:T(8,128)(2,1)S(1)} %collective-permute-done.3), channel_id=1, source_target_pairs={{0,2},{2,4},{4,6},{6,8},{8,10},{10,12},{12,14},{14,0},{1,3},{3,5},... | collective-permute-start | bytes 786440 | tf_op jit(solution)/shard_map/ppermute | solution.py:239
  75.9 8.7 %collective-permute-start.6 = (bf16[256,512]{1,0:T(8,128)(2,1)S(1)}, bf16[256,512]{1,0:T(8,128)(2,1)S(1)}, u32[]{:S(2)}, u32[]{:S(2)}) collective-permute-start(bf16[256,512]{1,0:T(8,128)(2,1)S(1)} %collective-permute-done.4), channel_id=1, source_target_pairs={{0,14},{2,0},{4,2},{6,4},{8,6},{10,8},{12,10},{14,12},{1,15},{3,1}... | collective-permute-start | bytes 786440 | tf_op jit(solution)/shard_map/ppermute | solution.py:240
  82.6 8.0 %collective-permute-start.7 = (bf16[128,512]{1,0:T(8,128)(2,1)S(1)}, bf16[128,512]{1,0:T(8,128)(2,1)S(1)}, u32[]{:S(2)}, u32[]{:S(2)}) collective-permute-start(bf16[128,512]{1,0:T(8,128)(2,1)S(1)} %slice.14), channel_id=1, source_target_pairs={{0,2},{2,4},{4,6},{6,8},{8,10},{10,12},{12,14},{14,0},{1,3},{3,5},... | collective-permute-start | bytes 393224 | tf_op jit(solution)/shard_map/ppermute | solution.py:245
  84.6 6.7 %collective-permute-start.8 = (bf16[128,512]{1,0:T(8,128)(2,1)S(1)}, bf16[128,512]{1,0:T(8,128)(2,1)S(1)}, u32[]{:S(2)}, u32[]{:S(2)}) collective-permute-start(bf16[128,512]{1,0:T(8,128)(2,1)S(1)} %slice.15), channel_id=1, source_target_pairs={{0,14},{2,0},{4,2},{6,4},{8,6},{10,8},{12,10},{14,12},{1,15},{3,1}... | collective-permute-start | bytes 393224 | tf_op jit(solution)/shard_map/ppermute | solution.py:246
  92.0 10.7 %collective-permute-start.9 = (bf16[2048,512]{1,0:T(8,128)(2,1)}, bf16[2048,512]{1,0:T(8,128)(2,1)}, u32[]{:S(2)}, u32[]{:S(2)}) collective-permute-start(bf16[2048,512]{1,0:T(8,128)(2,1)} %constant_dynamic-update-slice_fusion.mine_ref), channel_id=1, source_target_pairs={{0,1},{1,0},{2,3},{3,2},{4,5},{5,4},{6,7},{7,6},{8,9},{9,8},{10,11... | collective-permute-start | bytes 6291464 | tf_op jit(solution)/shard_map/ppermute | solution.py:282
  113.4 1.6 copy-start.8
  115.0 1.6 copy-start.10
  121.6 1.5 copy-start.2
  123.9 73.8 %all-to-all-start.2 = ((bf16[16,3,224,128]{3,2,1,0:T(8,128)(2,1)}), bf16[16,3,224,128]{3,2,1,0:T(8,128)(2,1)}, u32[]{:S(2)}, u32[]{:S(2)}) async-start(bf16[16,3,224,128]{3,2,1,0:T(8,128)(2,1)} %copy-done.2), calls=%async_computation.2 | async-start | bytes 5505024 | tf_op jit(solution)/shard_map/all_to_all | solution.py:294
  135.2 5.4 %collective-permute-start.10 = (bf16[16,64,512]{2,1,0:T(8,128)(2,1)S(1)}, bf16[16,64,512]{2,1,0:T(8,128)(2,1)S(1)}, u32[]{:S(2)}, u32[]{:S(2)}) collective-permute-start(bf16[16,64,512]{2,1,0:T(8,128)(2,1)S(1)} %get-tuple-element.31), channel_id=1, source_target_pairs={{0,1},{1,0},{2,3},{3,2},{4,5},{5,4},{6,7},{7,6},{8,9},{9,8},{10,11... | collective-permute-start | bytes 3145736 | tf_op jit(solution)/shard_map/ppermute | solution.py:297
  140.6 59.2 %copy-start.3 = (f32[1,4,3,224,128]{4,3,2,1,0:T(8,128)S(1)}, f32[1,4,3,224,128]{4,3,2,1,0:T(8,128)}, u32[]{:S(2)}) copy-start(f32[1,4,3,224,128]{4,3,2,1,0:T(8,128)} %param.11) | copy-start | bytes 4128772
  140.8 24.1 %collective-permute-start.17 = (bf16[2,64,512]{2,1,0:T(8,128)(2,1)S(1)}, bf16[2,64,512]{2,1,0:T(8,128)(2,1)S(1)}, u32[]{:S(2)}, u32[]{:S(2)}) collective-permute-start(bf16[2,64,512]{2,1,0:T(8,128)(2,1)S(1)} %get-tuple-element.39), channel_id=1, source_target_pairs={{0,14},{2,0},{4,2},{6,4},{8,6},{10,8},{12,10},{14,12},{1,15},{3,1}... | collective-permute-start | bytes 393224 | tf_op jit(solution)/shard_map/ppermute | solution.py:298
  151.6 16.4 %collective-permute-start.16 = (bf16[2,64,512]{2,1,0:T(8,128)(2,1)S(1)}, bf16[2,64,512]{2,1,0:T(8,128)(2,1)S(1)}, u32[]{:S(2)}, u32[]{:S(2)}) collective-permute-start(bf16[2,64,512]{2,1,0:T(8,128)(2,1)S(1)} %get-tuple-element.38), channel_id=1, source_target_pairs={{0,12},{2,14},{4,0},{6,2},{8,4},{10,6},{12,8},{14,10},{1,13},{3,15... | collective-permute-start | bytes 393224 | tf_op jit(solution)/shard_map/ppermute | solution.py:298
  153.8 17.6 %collective-permute-start.15 = (bf16[2,64,512]{2,1,0:T(8,128)(2,1)S(1)}, bf16[2,64,512]{2,1,0:T(8,128)(2,1)S(1)}, u32[]{:S(2)}, u32[]{:S(2)}) collective-permute-start(bf16[2,64,512]{2,1,0:T(8,128)(2,1)S(1)} %get-tuple-element.37), channel_id=1, source_target_pairs={{0,10},{2,12},{4,14},{6,0},{8,2},{10,4},{12,6},{14,8},{1,11},{3,13... | collective-permute-start | bytes 393224 | tf_op jit(solution)/shard_map/ppermute | solution.py:298
  155.7 15.7 %collective-permute-start.14 = (bf16[2,64,512]{2,1,0:T(8,128)(2,1)S(1)}, bf16[2,64,512]{2,1,0:T(8,128)(2,1)}, u32[]{:S(2)}, u32[]{:S(2)}) collective-permute-start(bf16[2,64,512]{2,1,0:T(8,128)(2,1)S(1)} %get-tuple-element.36), channel_id=1, source_target_pairs={{0,8},{2,10},{4,12},{6,14},{8,0},{10,2},{12,4},{14,6},{1,9},{3,11}... | collective-permute-start | bytes 393224 | tf_op jit(solution)/shard_map/ppermute | solution.py:298
  163.0 14.6 %collective-permute-start.13 = (bf16[2,64,512]{2,1,0:T(8,128)(2,1)S(1)}, bf16[2,64,512]{2,1,0:T(8,128)(2,1)}, u32[]{:S(2)}, u32[]{:S(2)}) collective-permute-start(bf16[2,64,512]{2,1,0:T(8,128)(2,1)S(1)} %get-tuple-element.35), channel_id=1, source_target_pairs={{0,6},{2,8},{4,10},{6,12},{8,14},{10,0},{12,2},{14,4},{1,7},{3,9},... | collective-permute-start | bytes 393224 | tf_op jit(solution)/shard_map/ppermute | solution.py:298
  164.9 18.1 %collective-permute-start.12 = (bf16[2,64,512]{2,1,0:T(8,128)(2,1)S(1)}, bf16[2,64,512]{2,1,0:T(8,128)(2,1)}, u32[]{:S(2)}, u32[]{:S(2)}) collective-permute-start(bf16[2,64,512]{2,1,0:T(8,128)(2,1)S(1)} %get-tuple-element.34), channel_id=1, source_target_pairs={{0,4},{2,6},{4,8},{6,10},{8,12},{10,14},{12,0},{14,2},{1,5},{3,7},... | collective-permute-start | bytes 393224 | tf_op jit(solution)/shard_map/ppermute | solution.py:298
  168.0 19.1 %collective-permute-start.11 = (bf16[2,64,512]{2,1,0:T(8,128)(2,1)S(1)}, bf16[2,64,512]{2,1,0:T(8,128)(2,1)}, u32[]{:S(2)}, u32[]{:S(2)}) collective-permute-start(bf16[2,64,512]{2,1,0:T(8,128)(2,1)S(1)} %get-tuple-element.33), channel_id=1, source_target_pairs={{0,2},{2,4},{4,6},{6,8},{8,10},{10,12},{12,14},{14,0},{1,3},{3,5},... | collective-permute-start | bytes 393224 | tf_op jit(solution)/shard_map/ppermute | solution.py:298
  197.7 7.7 %collective-permute-start.18 = (f32[64,512]{1,0:T(8,128)S(1)}, f32[64,512]{1,0:T(8,128)S(1)}, u32[]{:S(2)}, u32[]{:S(2)}) collective-permute-start(f32[64,512]{1,0:T(8,128)S(1)} %dynamic-slice_bitcast_fusion), channel_id=1, source_target_pairs={{0,16},{16,0},{1,17},{17,1},{2,18},{18,2},{3,19},{19,3},{4,20},{20... | collective-permute-start | bytes 393224 | tf_op jit(solution)/shard_map/ppermute | solution.py:304
  (5 other events, 5.2 us)

commit v4 on v2

v4 whole, which is shorter than its diff:
```python
import jax
import jax.numpy as jnp
from jax import lax
from jax.experimental import pallas as pl
from jax.experimental.pallas import tpu as pltpu
from jax.sharding import Mesh, PartitionSpec as P

MODULES = 4
BLK = 128
MU = 0.9
LR_INNER = 0.05
LR_OUTER = 0.02

PATH = ("yh", "x")
SHARD = ("yl", "z", "c")
BIG = ("x", "yh")
VMEM_LIMIT = 24 * 1024 * 1024


def pack_kernel(cluster_ref, here_ref, tokens_hbm, cotangent_hbm, send_ref, tokens_ref, cotangent_ref, sem):
    load_t = pltpu.make_async_copy(tokens_hbm, tokens_ref, sem.at[0])
    load_c = pltpu.make_async_copy(cotangent_hbm, cotangent_ref, sem.at[1])
    load_t.start()
    load_c.start()
    load_t.wait()
    load_c.wait()
    blocks = tokens_ref.shape[1] // BLK

    def block(b):
        lanes = slice(b * BLK, (b + 1) * BLK)
        return jnp.stack([tokens_ref[:, lanes], cotangent_ref[:, lanes]])

    def fill(d, carry):
        send_ref[d] = block(0)
        return carry

    lax.fori_loop(0, send_ref.shape[0], fill, 0)
    for b in range(blocks):
        send_ref[cluster_ref[here_ref[0] * blocks + b]] = block(b)


def grads_kernel(
    place_ref, core_ref, w_ref, mine_hbm, other_hbm, delta_hbm, dgu_hbm, xp, yp, delta, dgu, g_s, u_s, d_s, h_s, in_sem, out_sem
):
    owners, _, units, width = w_ref.shape

    def fetch(source, target, base):
        for o in range(owners):
            here = pl.ds(pl.multiple_of(place_ref[o] * width, width), width)
            pltpu.make_async_copy(source.at[here], target.at[pl.ds(o * width, width)], in_sem.at[base + o]).start()

    @pl.when(core_ref[0] == 0)
    def _():
        fetch(mine_hbm, xp, 0)
        fetch(other_hbm, yp, owners)

    @pl.when(core_ref[0] != 0)
    def _():
        fetch(other_hbm, xp, 0)
        fetch(mine_hbm, yp, owners)

    def arrived(target, base, some):
        for o in some:
            rows = pl.ds(o * width, width)
            pltpu.make_async_copy(mine_hbm.at[rows], target.at[rows], in_sem.at[base + o]).wait()

    def product(k, tokens, some):
        left = jnp.concatenate([w_ref[o, k] for o in some], axis=1)
        right = tokens[some[0] * width : (some[-1] + 1) * width, :]
        return jnp.dot(left, right, preferred_element_type=jnp.float32)

    early, late = range(owners // 2), range(owners // 2, owners)
    arrived(xp, 0, early)
    g_s[...] = product(0, xp, early)
    u_s[...] = product(1, xp, early)
    arrived(xp, 0, late)
    g_s[...] += product(0, xp, late)
    u_s[...] += product(1, xp, late)
    arrived(yp, owners, range(owners))
    d_s[...] = product(2, yp, range(owners))
    step = 32

    def act(i, carry):
        at = pl.multiple_of(i * step, step)
        rows = pl.ds(at, step)
        gate = g_s[rows, :]
        up = u_s[rows, :]
        dh = d_s[rows, :]
        sig = jax.nn.sigmoid(gate)
        silu = gate * sig
        h_s[rows, :] = (silu * up).astype(jnp.bfloat16)
        dgu[rows, :] = (dh * up * sig * (1.0 + gate * (1.0 - sig))).astype(jnp.bfloat16)
        dgu[pl.ds(pl.multiple_of(units + at, step), step), :] = (dh * silu).astype(jnp.bfloat16)
        return carry

    lax.fori_loop(0, units // step, act, 0)
    save_dgu = pltpu.make_async_copy(dgu, dgu_hbm, out_sem.at[owners // 2])
    save_dgu.start()
    nt = (((1,), (1,)), ((), ()))
    saves = []
    for p in range(owners // 2):
        rows = slice(p * 2 * width, (p + 1) * 2 * width)
        gu = LR_INNER * lax.dot_general(dgu[...], xp[rows, :], nt, preferred_element_type=jnp.float32)
        dn = LR_INNER * lax.dot_general(h_s[...], yp[rows, :], nt, preferred_element_type=jnp.float32)
        gu = gu.astype(jnp.bfloat16)
        dn = dn.astype(jnp.bfloat16)
        for half in range(2):
            lanes = slice(half * width, (half + 1) * width)
            delta[2 * p + half, 0] = gu[:units, lanes]
            delta[2 * p + half, 1] = gu[units:, lanes]
            delta[2 * p + half, 2] = dn[:, lanes]
        pair = slice(2 * p, 2 * p + 2)
        save = pltpu.make_async_copy(delta.at[pair], delta_hbm.at[pair], out_sem.at[p])
        save.start()
        saves.append(save)
    for save in saves:
        save.wait()
    save_dgu.wait()


def input_kernel(slot_ref, core_ref, w_ref, dgu_ref, keep_ref, give_ref):
    owners, _, units, width = w_ref.shape
    half = width // 2
    core = core_ref[0]

    def one(o, carry):
        w = w_ref[o, 0:2].reshape(2 * units, width)
        part = lax.dot_general(w, dgu_ref[...], (((0,), (0,)), ((), ())), preferred_element_type=jnp.float32)
        j = slot_ref[o]
        low, high = part[:half], part[half:]
        keep_ref[j] = jnp.where(core == 0, low, high)
        give_ref[j] = jnp.where(core == 0, high, low).astype(jnp.bfloat16)
        return carry

    lax.fori_loop(0, owners, one, 0)


def pair_kernel(keep_ref, came_ref, own_ref, *out_refs):
    for k in range(len(out_refs) + 1):
        at = slice(2 * k, 2 * k + 2)
        total = keep_ref[at] + came_ref[at].astype(jnp.float32)
        if k == 0:
            own_ref[...] = total
        else:
            out_refs[k - 1][...] = total.astype(jnp.bfloat16)


def update_kernel(module_ref, scale_ref, delta_ref, w_ref, m_ref, new_w_hbm, new_m_hbm, new_w, new_m, acc, out_sem):
    modules, mats, units, width = w_ref.shape
    paths = delta_ref.shape[0]
    step = acc.shape[1]
    saves = []
    for k in range(mats):
        for i in range(units // step):
            rows = slice(i * step, (i + 1) * step)
            acc[...] = jnp.zeros_like(acc)
            for q in range(paths):
                acc[module_ref[q]] += delta_ref[q, k, rows, :].astype(jnp.float32)
            for m in range(modules):
                mean = acc[m] * scale_ref[m]
                moment = MU * m_ref[m, k, rows, :] + mean
                new_m[m, k, rows, :] = moment
                new_w[m, k, rows, :] = w_ref[m, k, rows, :].astype(jnp.float32) - LR_OUTER * (mean + MU * moment)
            for here, there in ((new_w, new_w_hbm), (new_m, new_m_hbm)):
                part = (slice(None), k, rows)
                save = pltpu.make_async_copy(here.at[part], there.at[part], out_sem.at[len(saves)])
                save.start()
                saves.append(save)
    for save in saves:
        save.wait()


def in_hbm(array):
    return pltpu.with_memory_space_constraint(array, pltpu.HBM)


def pack(cluster, here, tokens, cotangent):
    cols, rows = tokens.shape
    paths = cluster.shape[0] * BLK // rows
    smem = pl.BlockSpec(memory_space=pltpu.SMEM)
    vmem = pl.BlockSpec(memory_space=pltpu.VMEM)
    hbm = pl.BlockSpec(memory_space=pltpu.HBM)
    return pl.pallas_call(
        pack_kernel,
        out_shape=jax.ShapeDtypeStruct((paths, 2, cols, BLK), tokens.dtype),
        in_specs=[smem, smem, hbm, hbm],
        out_specs=vmem,
        scratch_shapes=[pltpu.VMEM(tokens.shape, tokens.dtype)] * 2 + [pltpu.SemaphoreType.DMA((2,))],
        compiler_params=pltpu.CompilerParams(vmem_limit_bytes=VMEM_LIMIT),
        cost_estimate=pl.CostEstimate(flops=1000, bytes_accessed=1000, transcendentals=0),
        name="pack",
    )(cluster, here, in_hbm(tokens), in_hbm(cotangent))


def grads(place, core, w, mine, other):
    owners, _, units, width = w.shape
    rows = mine.shape[1]
    smem = pl.BlockSpec(memory_space=pltpu.SMEM)
    vmem = pl.BlockSpec(memory_space=pltpu.VMEM)
    hbm = pl.BlockSpec(memory_space=pltpu.HBM)
    return pl.pallas_call(
        grads_kernel,
        out_shape=(
            pltpu.HBM(w.shape, jnp.bfloat16),
            pltpu.HBM((2 * units, rows), jnp.bfloat16),
        ),
        in_specs=[smem, smem, vmem, hbm, hbm],
        out_specs=(hbm, hbm),
        scratch_shapes=[
            pltpu.VMEM(mine.shape, jnp.bfloat16),
            pltpu.VMEM(mine.shape, jnp.bfloat16),
            pltpu.VMEM(w.shape, jnp.bfloat16),
            pltpu.VMEM((2 * units, rows), jnp.bfloat16),
            pltpu.VMEM((units, rows), jnp.float32),
            pltpu.VMEM((units, rows), jnp.float32),
            pltpu.VMEM((units, rows), jnp.float32),
            pltpu.VMEM((units, rows), jnp.bfloat16),
            pltpu.SemaphoreType.DMA((2 * owners,)),
            pltpu.SemaphoreType.DMA((owners // 2 + 1,)),
        ],
        compiler_params=pltpu.CompilerParams(vmem_limit_bytes=VMEM_LIMIT),
        cost_estimate=pl.CostEstimate(
            flops=12 * units * rows * owners * width, bytes_accessed=12 * 2**20, transcendentals=units * rows
        ),
        name="grads",
    )(place, core, w, in_hbm(mine), in_hbm(other))


def input_partial(slot_of, core, w, dgu):
    owners, _, units, width = w.shape
    rows = dgu.shape[1]
    smem = pl.BlockSpec(memory_space=pltpu.SMEM)
    vmem = pl.BlockSpec(memory_space=pltpu.VMEM)
    shape = (owners, width // 2, rows)
    return pl.pallas_call(
        input_kernel,
        out_shape=(jax.ShapeDtypeStruct(shape, jnp.float32), jax.ShapeDtypeStruct(shape, jnp.bfloat16)),
        in_specs=[smem, smem, vmem, vmem],
        out_specs=(vmem, vmem),
        compiler_params=pltpu.CompilerParams(vmem_limit_bytes=VMEM_LIMIT),
        cost_estimate=pl.CostEstimate(flops=1000, bytes_accessed=1000, transcendentals=0),
        name="input_partial",
    )(slot_of, core, w, dgu)


def pair_sums(keep, came):
    tiles, feats, rows = keep.shape
    vmem = pl.BlockSpec(memory_space=pltpu.VMEM)
    part = (2, feats, rows)
    steps = tiles // 2
    return pl.pallas_call(
        pair_kernel,
        out_shape=(jax.ShapeDtypeStruct(part, jnp.float32),)
        + (jax.ShapeDtypeStruct(part, jnp.bfloat16),) * (steps - 1),
        in_specs=[vmem, vmem],
        out_specs=(vmem,) * steps,
        compiler_params=pltpu.CompilerParams(vmem_limit_bytes=VMEM_LIMIT),
        cost_estimate=pl.CostEstimate(flops=1000, bytes_accessed=1000, transcendentals=0),
        name="pair_sums",
    )(keep, came)


def update(modules_of, scale, delta, owned, momentum):
    modules, mats, units, width = owned.shape
    smem = pl.BlockSpec(memory_space=pltpu.SMEM)
    vmem = pl.BlockSpec(memory_space=pltpu.VMEM)
    hbm = pl.BlockSpec(memory_space=pltpu.HBM)
    return pl.pallas_call(
        update_kernel,
        out_shape=(jax.ShapeDtypeStruct(momentum.shape, jnp.float32),) * 2,
        in_specs=[smem, smem, vmem, vmem, vmem],
        out_specs=(hbm, hbm),
        scratch_shapes=[
            pltpu.VMEM(momentum.shape, jnp.float32),
            pltpu.VMEM(momentum.shape, jnp.float32),
            pltpu.VMEM((modules, units // 2, width), jnp.float32),
            pltpu.SemaphoreType.DMA((4 * mats,)),
        ],
        compiler_params=pltpu.CompilerParams(vmem_limit_bytes=VMEM_LIMIT // 2),
        cost_estimate=pl.CostEstimate(flops=10**6, bytes_accessed=8 * 2**20, transcendentals=0),
        name="update",
    )(modules_of, scale, delta, owned, momentum)


def pick(array, index):
    return array.at[index].get(mode="promise_in_bounds")


def transposed(per_path):
    lead = per_path.shape[:-1]
    grid = per_path.reshape(lead + tuple(lax.axis_size(name) for name in PATH))
    return jnp.swapaxes(grid, -1, -2).reshape(per_path.shape)


def turn(size, k):
    return [(i, (i + k) % size) for i in range(size)]


def ring_gather(piece, beside):
    depth = lax.axis_size("z")
    first = lax.axis_index("yl") == 0
    pair = jnp.concatenate([jnp.where(first, piece, beside), jnp.where(first, beside, piece)], axis=0)
    half = piece.shape[0]
    up = down = pair
    parts = [pair]
    at = [0] * depth
    for k in range(1, depth // 2):
        up = lax.ppermute(up, "z", turn(depth, 1))
        down = lax.ppermute(down, "z", turn(depth, -1))
        at[depth - k] = len(parts)
        at[k] = len(parts) + 1
        parts += [up, down]
    at[depth // 2] = len(parts)
    parts.append(lax.ppermute(up[:half], "z", turn(depth, 1)))
    parts.append(lax.ppermute(down[half:], "z", turn(depth, -1)))
    return jnp.concatenate(parts, axis=0), at


def body(tokens, cotangent, weights, momentum, cluster, path_module, owner):
    paths = lax.axis_size(PATH)
    here = lax.axis_index(PATH)
    core = lax.axis_index("c")
    modules_of = path_module[:, 0]
    path_ids = jnp.arange(paths, dtype=jnp.int32)
    blocks = tokens.shape[0] // BLK
    cols = tokens.shape[1]
    owned = weights[0]

    block_ids = jnp.arange(blocks, dtype=jnp.int32)
    send_x = pack(cluster, here.reshape(1), tokens.T, cotangent.T)
    recv_x = lax.all_to_all(
        send_x.reshape(paths * 2, cols, BLK), PATH + ("c",), split_axis=0, concat_axis=0, tiled=True
    ).reshape(paths, 2, cols, BLK)
    has = jnp.any(cluster.reshape(paths, blocks) == here, axis=1)
    before = jnp.sum((has[None, :] & (path_ids[None, :] < path_ids[:, None])).astype(jnp.int32), axis=1)
    comes = has[None, :] & (before[None, :] == block_ids[:, None])
    sources = jnp.sum(jnp.where(comes, path_ids[None, :], 0), axis=1)
    piece = pick(recv_x, sources).transpose(1, 2, 0, 3).reshape(2 * cols, blocks * BLK)

    beside = lax.ppermute(piece, "yl", [(0, 1), (1, 0)])
    send_w, piece, beside = lax.optimization_barrier((pick(owned, transposed(modules_of)), piece, beside))
    recv_w = lax.all_to_all(send_w, BIG, split_axis=0, concat_axis=0, tiled=True)
    mine, at = ring_gather(piece, beside)
    swap = [(0, 1), (1, 0)]
    other = lax.ppermute(mine, "c", swap)

    owner_row = owner[modules_of[here]]
    tile_of = jnp.sum(jnp.where(owner_row[None, :] == transposed(path_ids)[:, None], path_ids[None, :], 0), axis=1)
    z = lax.axis_index("z")
    depth = lax.axis_size("z")
    away = (tile_of % depth - z) % depth
    side = tile_of // depth
    place = jnp.sum(jnp.where(away[:, None] == jnp.arange(depth)[None, :], jnp.array(at, jnp.int32)[None, :], 0), axis=1)
    core_id = core.reshape(1)
    delta, dgu = grads(place * 2 + side, core_id, recv_w, mine, other)
    recv_delta = lax.all_to_all(delta, BIG, split_axis=0, concat_axis=0, tiled=True)

    keep, give = input_partial(away * 2 + side, core_id, recv_w, dgu)
    sums = pair_sums(keep, lax.ppermute(give, "c", swap))
    came = [lax.ppermute(sums[k], "z", turn(depth, k)) for k in range(1, depth)]
    total = sums[0]
    for part in came:
        total = total + part.astype(jnp.float32)
    yl = lax.axis_index("yl")
    theirs = lax.ppermute(lax.dynamic_index_in_dim(total, 1 - yl, 0, keepdims=False), "yl", swap)
    member = modules_of[None, :] == jnp.arange(MODULES, dtype=jnp.int32)[:, None]
    counts = jnp.sum(member.astype(jnp.float32), axis=1)
    new_tiles, new_moment = update(transposed(modules_of), 1.0 / counts, recv_delta, owned, momentum[0])
    total, new_moment = lax.optimization_barrier((lax.dynamic_index_in_dim(total, yl, 0, keepdims=False), new_moment))
    input_grad = (total + theirs).astype(jnp.bfloat16).T
    return (input_grad, new_tiles[None], new_moment[None])


def solution(mesh):
    fine = Mesh(mesh.devices.reshape(4, 4, 2, 8, 2), PATH + SHARD)
    tiles = P(PATH, None, None, SHARD, None)
    return jax.shard_map(
        body,
        mesh=fine,
        in_specs=(P(PATH, SHARD), P(PATH, SHARD), tiles, tiles, P(), P(), P()),
        out_specs=(P(PATH, SHARD), tiles, tiles),
        check_vma=False,
    )
```

time: 249 us -> 196 us (0.79)
  the two profiles are of different devices: /device:TPU:1 before, /device:TPU:401 now
where the time goes in v4:
time: 196 us; the launch traced here: 194 us
  starting transfers between devices  81.7 us (42%)
  waiting for transfers between devices  71.3 us (36%)
  Pallas kernels  17.7 us (9%)
  local copies, waits for them, and re-layouts  12.9 us (7%)
  other arithmetic  7.83 us (4%)
  between operations  3.05 us (2%)
    ppermute x7, starting transfers between devices, body(): came = [lax.ppermute(sums[k], 'z', turn(depth, k)) for k in range(1, depth)]  23 us
    all_to_all x1, waiting for transfers between devices, body(): lax.all_to_all(send_w, BIG, split_axis=0, concat_axis=0, tiled=True)  17.5 us
    all_to_all x1, waiting for transfers between devices, body(): lax.all_to_all(send_x.reshape(paths * 2, cols, BLK), PATH + ('c',), split...  14.7 us
    ppermute x7, waiting for transfers between devices, body(): came = [lax.ppermute(sums[k], 'z', turn(depth, k)) for k in range(1, depth)]  14.6 us
    all_to_all x1, waiting for transfers between devices, body(): lax.all_to_all(delta, BIG, split_axis=0, concat_axis=0, tiled=True)  14.2 us
    ppermute x3, starting transfers between devices, ring_gather(): up = lax.ppermute(up, 'z', turn(depth, 1))  11.7 us
    all_to_all x1, starting transfers between devices, body(): lax.all_to_all(send_x.reshape(paths * 2, cols, BLK), PATH + ('c',), split...  10.4 us
    unnamed x27, local copies, waits for them, and re-layouts  7.96 us
  transfers between devices with their start and end apart: 22, of which 12 were waited for; matrix products, arithmetic and copies ran while one was open for 9% of the time, Pallas kernels for 4%

profile of v4, /device:TPU:401, one launch (start us, length us, event | category | flops | bytes accessed | tf_op | source)
XLA Modules:
  0.0 194.5 jit_solution(4944464749748164774)
XLA Ops:
  1.4 2.4 %pack.1 = bf16[16,2,64,128]{3,2,1,0:T(8,128)(2,1)} custom-call(s32[64]{0:T(128)S(1)} %copy-done.4, s32[1]{0:T(128)} %bitcast.6.here_ref, bf16[64,512]{1,0:T(8,128)(2,1)} %bitcast.43, bf16[64,512]{1,0:T(8,128)(2,1)} %bitcast.44), custom_call_target="tpu_custom_call" | custom-call | flops 1000 | bytes 1000 | tf_op jit(solution)/shard_map/pack/pallas_call | solution.py:183
  3.8 10.4 %all-to-all-start = ((bf16[32,64,128]{2,1,0:T(8,128)(2,1)}), bf16[32,64,128]{2,1,0:T(8,128)(2,1)S(1)}, u32[]{:S(2)}, u32[]{:S(2)}) async-start(bf16[32,64,128]{2,1,0:T(8,128)(2,1)} %bitcast.9), calls=%async_computation | async-start | bytes 1048576 | tf_op jit(solution)/shard_map/all_to_all | solution.py:331
  17.4 14.7 %all-to-all-done = bf16[32,64,128]{2,1,0:T(8,128)(2,1)S(1)} async-done(((bf16[32,64,128]{2,1,0:T(8,128)(2,1)}), bf16[32,64,128]{2,1,0:T(8,128)(2,1)S(1)}, u32[]{:S(2)}, u32[]{:S(2)}) %all-to-all-start) | async-done | bytes 524320 | tf_op jit(solution)/shard_map/all_to_all | solution.py:331
  32.9 1.9 collective-permute-start
  34.9 2.5 %gather_fusion = bf16[16,3,224,128]{3,2,1,0:T(8,128)(2,1)} fusion(bf16[4,3,224,128]{3,2,1,0:T(8,128)(2,1)S(1)} %bitcast.34, s32[1024]{0:T(1024)S(1)} %pad_clamp_fusion.1), kind=kCustom, calls=%fused_computation | custom fusion | bytes 5505088 | tf_op jit(solution)/shard_map/gather | solution.py:286
  37.3 2.3 %collective-permute-done = bf16[128,512]{1,0:T(8,128)(2,1)S(1)} collective-permute-done((bf16[128,512]{1,0:T(8,128)(2,1)S(1)}, bf16[128,512]{1,0:T(8,128)(2,1)S(1)}, u32[]{:S(2)}, u32[]{:S(2)}) %collective-permute-start) | collective-permute-done | bytes 131104 | tf_op jit(solution)/shard_map/ppermute | solution.py:340
  40.3 4.1 %all-to-all-start.1 = ((bf16[16,3,224,128]{3,2,1,0:T(8,128)(2,1)}), bf16[16,3,224,128]{3,2,1,0:T(8,128)(2,1)S(1)}, u32[]{:S(2)}, u32[]{:S(2)}) async-start(bf16[16,3,224,128]{3,2,1,0:T(8,128)(2,1)} %gather_fusion), calls=%async_computation.1 | async-start | bytes 5505024 | tf_op jit(solution)/shard_map/all_to_all | solution.py:342
  47.6 2.2 %collective-permute-start.2 = (bf16[256,512]{1,0:T(8,128)(2,1)S(1)}, bf16[256,512]{1,0:T(8,128)(2,1)S(1)}, u32[]{:S(2)}, u32[]{:S(2)}) collective-permute-start(bf16[256,512]{1,0:T(8,128)(2,1)S(1)} %pad_maximum_fusion), channel_id=1, source_target_pairs={{0,14},{2,0},{4,2},{6,4},{8,6},{10,8},{12,10},{14,12},{1,15},{3,1}... | collective-permute-start | bytes 786440 | tf_op jit(solution)/shard_map/ppermute | solution.py:309
  49.8 3.1 %collective-permute-start.1 = (bf16[256,512]{1,0:T(8,128)(2,1)S(1)}, bf16[256,512]{1,0:T(8,128)(2,1)S(1)}, u32[]{:S(2)}, u32[]{:S(2)}) collective-permute-start(bf16[256,512]{1,0:T(8,128)(2,1)S(1)} %pad_maximum_fusion), channel_id=1, source_target_pairs={{0,2},{2,4},{4,6},{6,8},{8,10},{10,12},{12,14},{14,0},{1,3},{3,5},... | collective-permute-start | bytes 786440 | tf_op jit(solution)/shard_map/ppermute | solution.py:308
  52.9 2.7 %collective-permute-done.2 = bf16[256,512]{1,0:T(8,128)(2,1)S(1)} collective-permute-done((bf16[256,512]{1,0:T(8,128)(2,1)S(1)}, bf16[256,512]{1,0:T(8,128)(2,1)S(1)}, u32[]{:S(2)}, u32[]{:S(2)}) %collective-permute-start.2) | collective-permute-done | bytes 262176 | tf_op jit(solution)/shard_map/ppermute | solution.py:309
  55.6 2.2 %collective-permute-start.4 = (bf16[256,512]{1,0:T(8,128)(2,1)S(1)}, bf16[256,512]{1,0:T(8,128)(2,1)S(1)}, u32[]{:S(2)}, u32[]{:S(2)}) collective-permute-start(bf16[256,512]{1,0:T(8,128)(2,1)S(1)} %collective-permute-done.2), channel_id=1, source_target_pairs={{0,14},{2,0},{4,2},{6,4},{8,6},{10,8},{12,10},{14,12},{1,15},{3,1}... | collective-permute-start | bytes 786440 | tf_op jit(solution)/shard_map/ppermute | solution.py:309
  57.8 4.1 %collective-permute-start.3 = (bf16[256,512]{1,0:T(8,128)(2,1)S(1)}, bf16[256,512]{1,0:T(8,128)(2,1)S(1)}, u32[]{:S(2)}, u32[]{:S(2)}) collective-permute-start(bf16[256,512]{1,0:T(8,128)(2,1)S(1)} %collective-permute-done.1), channel_id=1, source_target_pairs={{0,2},{2,4},{4,6},{6,8},{8,10},{10,12},{12,14},{14,0},{1,3},{3,5},... | collective-permute-start | bytes 786440 | tf_op jit(solution)/shard_map/ppermute | solution.py:308
  65.9 4.6 %collective-permute-start.5 = (bf16[256,512]{1,0:T(8,128)(2,1)S(1)}, bf16[256,512]{1,0:T(8,128)(2,1)S(1)}, u32[]{:S(2)}, u32[]{:S(2)}) collective-permute-start(bf16[256,512]{1,0:T(8,128)(2,1)S(1)} %collective-permute-done.3), channel_id=1, source_target_pairs={{0,2},{2,4},{4,6},{6,8},{8,10},{10,12},{12,14},{14,0},{1,3},{3,5},... | collective-permute-start | bytes 786440 | tf_op jit(solution)/shard_map/ppermute | solution.py:308
  72.7 1.9 collective-permute-start.8
  74.6 4.6 %collective-permute-start.7 = (bf16[128,512]{1,0:T(8,128)(2,1)S(1)}, bf16[128,512]{1,0:T(8,128)(2,1)S(1)}, u32[]{:S(2)}, u32[]{:S(2)}) collective-permute-start(bf16[128,512]{1,0:T(8,128)(2,1)S(1)} %slice.12), channel_id=1, source_target_pairs={{0,2},{2,4},{4,6},{6,8},{8,10},{10,12},{12,14},{14,0},{1,3},{3,5},... | collective-permute-start | bytes 393224 | tf_op jit(solution)/shard_map/ppermute | solution.py:314
  82.4 7.0 %collective-permute-start.9 = (bf16[2048,512]{1,0:T(8,128)(2,1)}, bf16[2048,512]{1,0:T(8,128)(2,1)}, u32[]{:S(2)}, u32[]{:S(2)}) collective-permute-start(bf16[2048,512]{1,0:T(8,128)(2,1)} %constant_dynamic-update-slice_fusion.mine_hbm), channel_id=1, source_target_pairs={{0,1},{1,0},{2,3},{3,2},{4,5},{5,4},{6,7},{7,6},{8,9},{9,8},{10,11... | collective-permute-start | bytes 6291464 | tf_op jit(solution)/shard_map/ppermute | solution.py:345
  93.5 17.5 %all-to-all-done.1.w_ref = bf16[16,3,224,128]{3,2,1,0:T(8,128)(2,1)S(1)} async-done(((bf16[16,3,224,128]{3,2,1,0:T(8,128)(2,1)}), bf16[16,3,224,128]{3,2,1,0:T(8,128)(2,1)S(1)}, u32[]{:S(2)}, u32[]{:S(2)}) %all-to-all-start.1) | async-done | bytes 2752544 | tf_op jit(solution)/shard_map/all_to_all | solution.py:342
  111.1 6.8 %grads.1 = (bf16[16,3,224,128]{3,2,1,0:T(8,128)(2,1)}, bf16[448,512]{1,0:T(8,128)(2,1)}) custom-call(s32[16]{0:T(128)S(1)} %get-tuple-element.45.place_ref, s32[1]{0:T(128)} %bitcast.2.core_ref, bf16[16,3,224,128]{3,2,1,0:T(8,128)(2,1)S(1)} %all-to-all-done.1.w_ref, bf16[2048,512]{1,0:T(8,128)(2,1)} %constant_dynamic-update-slice_fusion.mine_hbm, ...), custom_call_target="tpu_custom_call" | custom-call | flops 2818572288 | bytes 12582912 | tf_op jit(solution)/shard_map/grads/pallas_call | solution.py:201
  117.8 5.6 %all-to-all-start.2 = ((bf16[16,3,224,128]{3,2,1,0:T(8,128)(2,1)}), bf16[16,3,224,128]{3,2,1,0:T(8,128)(2,1)}, u32[]{:S(2)}, u32[]{:S(2)}) async-start(bf16[16,3,224,128]{3,2,1,0:T(8,128)(2,1)} %get-tuple-element.36), calls=%async_computation.2 | async-start | bytes 5505024 | tf_op jit(solution)/shard_map/all_to_all | solution.py:356
  124.5 4.6 %input_partial.1 = (f32[16,64,512]{2,1,0:T(8,128)S(1)}, bf16[16,64,512]{2,1,0:T(8,128)(2,1)S(1)}) custom-call(s32[16]{0:T(128)S(1)} %multiply_add_fusion.2.slot_ref, s32[1]{0:T(128)} %bitcast.2.core_ref, bf16[16,3,224,128]{3,2,1,0:T(8,128)(2,1)S(1)} %all-to-all-done.1.w_ref, bf16[448,512]{1,0:T(8,128)(2,1)S(1)} %copy-done.3), custom_call_target="tpu_custom_call" | custom-call | flops 1000 | bytes 1000 | tf_op jit(solution)/shard_map/input_partial/pallas_call | solution.py:235
  129.1 3.3 %collective-permute-start.10 = (bf16[16,64,512]{2,1,0:T(8,128)(2,1)S(1)}, bf16[16,64,512]{2,1,0:T(8,128)(2,1)S(1)}, u32[]{:S(2)}, u32[]{:S(2)}) collective-permute-start(bf16[16,64,512]{2,1,0:T(8,128)(2,1)S(1)} %get-tuple-element.27), channel_id=1, source_target_pairs={{0,1},{1,0},{2,3},{3,2},{4,5},{5,4},{6,7},{7,6},{8,9},{9,8},{10,11... | collective-permute-start | bytes 3145736 | tf_op jit(solution)/shard_map/ppermute | solution.py:359
  132.4 2.3 %collective-permute-done.10.came_ref = bf16[16,64,512]{2,1,0:T(8,128)(2,1)S(1)} collective-permute-done((bf16[16,64,512]{2,1,0:T(8,128)(2,1)S(1)}, bf16[16,64,512]{2,1,0:T(8,128)(2,1)S(1)}, u32[]{:S(2)}, u32[]{:S(2)}) %collective-permute-start.10) | collective-permute-done | bytes 1048608 | tf_op jit(solution)/shard_map/ppermute | solution.py:359
  134.8 3.2 %collective-permute-start.11 = (bf16[2,64,512]{2,1,0:T(8,128)(2,1)S(1)}, bf16[2,64,512]{2,1,0:T(8,128)(2,1)S(1)}, u32[]{:S(2)}, u32[]{:S(2)}) collective-permute-start(bf16[2,64,512]{2,1,0:T(8,128)(2,1)S(1)} %get-tuple-element.29), channel_id=1, source_target_pairs={{0,2},{2,4},{4,6},{6,8},{8,10},{10,12},{12,14},{14,0},{1,3},{3,5},... | collective-permute-start | bytes 393224 | tf_op jit(solution)/shard_map/ppermute | solution.py:360
  140.0 4.6 %collective-permute-start.13 = (bf16[2,64,512]{2,1,0:T(8,128)(2,1)S(1)}, bf16[2,64,512]{2,1,0:T(8,128)(2,1)S(1)}, u32[]{:S(2)}, u32[]{:S(2)}) collective-permute-start(bf16[2,64,512]{2,1,0:T(8,128)(2,1)S(1)} %get-tuple-element.31), channel_id=1, source_target_pairs={{0,6},{2,8},{4,10},{6,12},{8,14},{10,0},{12,2},{14,4},{1,7},{3,9},... | collective-permute-start | bytes 393224 | tf_op jit(solution)/shard_map/ppermute | solution.py:360
  144.6 4.6 %collective-permute-start.14 = (bf16[2,64,512]{2,1,0:T(8,128)(2,1)S(1)}, bf16[2,64,512]{2,1,0:T(8,128)(2,1)S(1)}, u32[]{:S(2)}, u32[]{:S(2)}) collective-permute-start(bf16[2,64,512]{2,1,0:T(8,128)(2,1)S(1)} %get-tuple-element.32), channel_id=1, source_target_pairs={{0,8},{2,10},{4,12},{6,14},{8,0},{10,2},{12,4},{14,6},{1,9},{3,11}... | collective-permute-start | bytes 393224 | tf_op jit(solution)/shard_map/ppermute | solution.py:360
  149.2 4.6 %collective-permute-start.15 = (bf16[2,64,512]{2,1,0:T(8,128)(2,1)S(1)}, bf16[2,64,512]{2,1,0:T(8,128)(2,1)}, u32[]{:S(2)}, u32[]{:S(2)}) collective-permute-start(bf16[2,64,512]{2,1,0:T(8,128)(2,1)S(1)} %get-tuple-element.33), channel_id=1, source_target_pairs={{0,10},{2,12},{4,14},{6,0},{8,2},{10,4},{12,6},{14,8},{1,11},{3,13... | collective-permute-start | bytes 393224 | tf_op jit(solution)/shard_map/ppermute | solution.py:360
  153.8 1.9 collective-permute-start.16
  155.7 2.2 %collective-permute-start.17 = (bf16[2,64,512]{2,1,0:T(8,128)(2,1)S(1)}, bf16[2,64,512]{2,1,0:T(8,128)(2,1)}, u32[]{:S(2)}, u32[]{:S(2)}) collective-permute-start(bf16[2,64,512]{2,1,0:T(8,128)(2,1)S(1)} %get-tuple-element.35), channel_id=1, source_target_pairs={{0,14},{2,0},{4,2},{6,4},{8,6},{10,8},{12,10},{14,12},{1,15},{3,1}... | collective-permute-start | bytes 393224 | tf_op jit(solution)/shard_map/ppermute | solution.py:360
  158.1 5.7 %collective-permute-done.14 = bf16[2,64,512]{2,1,0:T(8,128)(2,1)S(1)} collective-permute-done((bf16[2,64,512]{2,1,0:T(8,128)(2,1)S(1)}, bf16[2,64,512]{2,1,0:T(8,128)(2,1)S(1)}, u32[]{:S(2)}, u32[]{:S(2)}) %collective-permute-start.14) | collective-permute-done | bytes 131104 | tf_op jit(solution)/shard_map/ppermute | solution.py:360
  163.8 8.0 %collective-permute-done.16 = bf16[2,64,512]{2,1,0:T(8,128)(2,1)} collective-permute-done((bf16[2,64,512]{2,1,0:T(8,128)(2,1)S(1)}, bf16[2,64,512]{2,1,0:T(8,128)(2,1)}, u32[]{:S(2)}, u32[]{:S(2)}) %collective-permute-start.16) | collective-permute-done | bytes 131104 | tf_op jit(solution)/shard_map/ppermute | solution.py:360
  175.9 14.2 %all-to-all-done.2.delta_ref = bf16[16,3,224,128]{3,2,1,0:T(8,128)(2,1)} async-done(((bf16[16,3,224,128]{3,2,1,0:T(8,128)(2,1)}), bf16[16,3,224,128]{3,2,1,0:T(8,128)(2,1)}, u32[]{:S(2)}, u32[]{:S(2)}) %all-to-all-start.2) | async-done | bytes 2752544 | tf_op jit(solution)/shard_map/all_to_all | solution.py:356
  190.0 3.8 %update.1 = (f32[4,3,224,128]{3,2,1,0:T(8,128)}, f32[4,3,224,128]{3,2,1,0:T(8,128)}) custom-call(s32[16]{0:T(128)S(1)} %reshape.141.module_ref, f32[4]{0:T(128)S(1)} %broadcast_divide_fusion.scale_ref, bf16[16,3,224,128]{3,2,1,0:T(8,128)(2,1)} %all-to-all-done.2.delta_ref, bf16[4,3,224,128]{3,2,1,0:T(8,128)(2,1)S(1)} %bitcast.35, f32[4,3,224,128]{3,2,1,0:T(8,128)S(1)} %bitcast.36), custom_call_target="tpu_custom_call" | custom-call | flops 1000000 | bytes 8388608 | tf_op jit(solution)/shard_map/update/pallas_call | solution.py:268
  (81 shorter events, 28.1 us)
Async XLA Ops:
  0.6 91.5 %copy-start = (s32[4,16]{1,0:T(4,128)S(1)}, s32[4,16]{1,0:T(4,128)}, u32[]{:S(2)}) copy-start(s32[4,16]{1,0:T(4,128)} %param.14) | copy-start | bytes 772
  0.6 34.2 %copy-start.1 = (bf16[1,4,3,224,128]{4,3,2,1,0:T(8,128)(2,1)S(1)}, bf16[1,4,3,224,128]{4,3,2,1,0:T(8,128)(2,1)}, u32[]{:S(2)}) copy-start(bf16[1,4,3,224,128]{4,3,2,1,0:T(8,128)(2,1)} %param.10) | copy-start | bytes 2064388
  0.7 0.7 copy-start.4
  3.8 28.4 %all-to-all-start = ((bf16[32,64,128]{2,1,0:T(8,128)(2,1)}), bf16[32,64,128]{2,1,0:T(8,128)(2,1)S(1)}, u32[]{:S(2)}, u32[]{:S(2)}) async-start(bf16[32,64,128]{2,1,0:T(8,128)(2,1)} %bitcast.9), calls=%async_computation | async-start | bytes 1048576 | tf_op jit(solution)/shard_map/all_to_all | solution.py:331
  32.9 4.4 %copy-start.5 = (bf16[16,8,4,128]{3,1,2,0:T(8,128)(2,1)}, bf16[16,8,4,128]{3,1,2,0:T(8,128)(2,1)S(1)}, u32[]{:S(2)}) copy-start(bf16[16,8,4,128]{3,1,2,0:T(8,128)(2,1)S(1)} %copy.21) | copy-start | bytes 393220
  32.9 6.8 %collective-permute-start = (bf16[128,512]{1,0:T(8,128)(2,1)S(1)}, bf16[128,512]{1,0:T(8,128)(2,1)S(1)}, u32[]{:S(2)}, u32[]{:S(2)}) collective-permute-start(bf16[128,512]{1,0:T(8,128)(2,1)S(1)} %bitcast.37), channel_id=1, source_target_pairs={{0,16},{16,0},{1,17},{17,1},{2,18},{18,2},{3,19},{19,3},{4,20},{20... | collective-permute-start | bytes 393224 | tf_op jit(solution)/shard_map/ppermute | solution.py:340
  39.7 0.7 copy-start.6
  40.3 70.7 %all-to-all-start.1 = ((bf16[16,3,224,128]{3,2,1,0:T(8,128)(2,1)}), bf16[16,3,224,128]{3,2,1,0:T(8,128)(2,1)S(1)}, u32[]{:S(2)}, u32[]{:S(2)}) async-start(bf16[16,3,224,128]{3,2,1,0:T(8,128)(2,1)} %gather_fusion), calls=%async_computation.1 | async-start | bytes 5505024 | tf_op jit(solution)/shard_map/all_to_all | solution.py:342
  47.6 8.0 %collective-permute-start.2 = (bf16[256,512]{1,0:T(8,128)(2,1)S(1)}, bf16[256,512]{1,0:T(8,128)(2,1)S(1)}, u32[]{:S(2)}, u32[]{:S(2)}) collective-permute-start(bf16[256,512]{1,0:T(8,128)(2,1)S(1)} %pad_maximum_fusion), channel_id=1, source_target_pairs={{0,14},{2,0},{4,2},{6,4},{8,6},{10,8},{12,10},{14,12},{1,15},{3,1}... | collective-permute-start | bytes 786440 | tf_op jit(solution)/shard_map/ppermute | solution.py:309
  49.8 8.0 %collective-permute-start.1 = (bf16[256,512]{1,0:T(8,128)(2,1)S(1)}, bf16[256,512]{1,0:T(8,128)(2,1)S(1)}, u32[]{:S(2)}, u32[]{:S(2)}) collective-permute-start(bf16[256,512]{1,0:T(8,128)(2,1)S(1)} %pad_maximum_fusion), channel_id=1, source_target_pairs={{0,2},{2,4},{4,6},{6,8},{8,10},{10,12},{12,14},{14,0},{1,3},{3,5},... | collective-permute-start | bytes 786440 | tf_op jit(solution)/shard_map/ppermute | solution.py:308
  55.6 8.3 %collective-permute-start.4 = (bf16[256,512]{1,0:T(8,128)(2,1)S(1)}, bf16[256,512]{1,0:T(8,128)(2,1)S(1)}, u32[]{:S(2)}, u32[]{:S(2)}) collective-permute-start(bf16[256,512]{1,0:T(8,128)(2,1)S(1)} %collective-permute-done.2), channel_id=1, source_target_pairs={{0,14},{2,0},{4,2},{6,4},{8,6},{10,8},{12,10},{14,12},{1,15},{3,1}... | collective-permute-start | bytes 786440 | tf_op jit(solution)/shard_map/ppermute | solution.py:309
  57.8 8.1 %collective-permute-start.3 = (bf16[256,512]{1,0:T(8,128)(2,1)S(1)}, bf16[256,512]{1,0:T(8,128)(2,1)S(1)}, u32[]{:S(2)}, u32[]{:S(2)}) collective-permute-start(bf16[256,512]{1,0:T(8,128)(2,1)S(1)} %collective-permute-done.1), channel_id=1, source_target_pairs={{0,2},{2,4},{4,6},{6,8},{8,10},{10,12},{12,14},{14,0},{1,3},{3,5},... | collective-permute-start | bytes 786440 | tf_op jit(solution)/shard_map/ppermute | solution.py:308
  61.9 27.6 %copy-start.7 = (s32[16,1]{0,1:T(1,128)S(1)}, s32[16,1]{0,1:T(1,128)}, u32[]{:S(2)}) copy-start(s32[16,1]{0,1:T(1,128)} %param.13) | copy-start | bytes 196
  61.9 30.4 %copy-start.8 = (s32[8]{0:T(128)S(1)}, s32[8]{0:T(128)}, u32[]{:S(2)}) copy-start(s32[8]{0:T(128)} %constant.87.clone) | copy-start | bytes 100
  64.0 8.7 %collective-permute-start.6 = (bf16[256,512]{1,0:T(8,128)(2,1)S(1)}, bf16[256,512]{1,0:T(8,128)(2,1)S(1)}, u32[]{:S(2)}, u32[]{:S(2)}) collective-permute-start(bf16[256,512]{1,0:T(8,128)(2,1)S(1)} %collective-permute-done.4), channel_id=1, source_target_pairs={{0,14},{2,0},{4,2},{6,4},{8,6},{10,8},{12,10},{14,12},{1,15},{3,1}... | collective-permute-start | bytes 786440 | tf_op jit(solution)/shard_map/ppermute | solution.py:309
  65.9 8.7 %collective-permute-start.5 = (bf16[256,512]{1,0:T(8,128)(2,1)S(1)}, bf16[256,512]{1,0:T(8,128)(2,1)S(1)}, u32[]{:S(2)}, u32[]{:S(2)}) collective-permute-start(bf16[256,512]{1,0:T(8,128)(2,1)S(1)} %collective-permute-done.3), channel_id=1, source_target_pairs={{0,2},{2,4},{4,6},{6,8},{8,10},{10,12},{12,14},{14,0},{1,3},{3,5},... | collective-permute-start | bytes 786440 | tf_op jit(solution)/shard_map/ppermute | solution.py:308
  72.7 9.1 %collective-permute-start.8 = (bf16[128,512]{1,0:T(8,128)(2,1)S(1)}, bf16[128,512]{1,0:T(8,128)(2,1)S(1)}, u32[]{:S(2)}, u32[]{:S(2)}) collective-permute-start(bf16[128,512]{1,0:T(8,128)(2,1)S(1)} %slice.13), channel_id=1, source_target_pairs={{0,14},{2,0},{4,2},{6,4},{8,6},{10,8},{12,10},{14,12},{1,15},{3,1}... | collective-permute-start | bytes 393224 | tf_op jit(solution)/shard_map/ppermute | solution.py:315
  74.6 6.5 %collective-permute-start.7 = (bf16[128,512]{1,0:T(8,128)(2,1)S(1)}, bf16[128,512]{1,0:T(8,128)(2,1)S(1)}, u32[]{:S(2)}, u32[]{:S(2)}) collective-permute-start(bf16[128,512]{1,0:T(8,128)(2,1)S(1)} %slice.12), channel_id=1, source_target_pairs={{0,2},{2,4},{4,6},{6,8},{8,10},{10,12},{12,14},{14,0},{1,3},{3,5},... | collective-permute-start | bytes 393224 | tf_op jit(solution)/shard_map/ppermute | solution.py:314
  82.4 11.1 %collective-permute-start.9 = (bf16[2048,512]{1,0:T(8,128)(2,1)}, bf16[2048,512]{1,0:T(8,128)(2,1)}, u32[]{:S(2)}, u32[]{:S(2)}) collective-permute-start(bf16[2048,512]{1,0:T(8,128)(2,1)} %constant_dynamic-update-slice_fusion.mine_hbm), channel_id=1, source_target_pairs={{0,1},{1,0},{2,3},{3,2},{4,5},{5,4},{6,7},{7,6},{8,9},{9,8},{10,11... | collective-permute-start | bytes 6291464 | tf_op jit(solution)/shard_map/ppermute | solution.py:345
  117.8 72.2 %all-to-all-start.2 = ((bf16[16,3,224,128]{3,2,1,0:T(8,128)(2,1)}), bf16[16,3,224,128]{3,2,1,0:T(8,128)(2,1)}, u32[]{:S(2)}, u32[]{:S(2)}) async-start(bf16[16,3,224,128]{3,2,1,0:T(8,128)(2,1)} %get-tuple-element.36), calls=%async_computation.2 | async-start | bytes 5505024 | tf_op jit(solution)/shard_map/all_to_all | solution.py:356
  123.5 1.0 copy-start.3
  129.1 5.6 %collective-permute-start.10 = (bf16[16,64,512]{2,1,0:T(8,128)(2,1)S(1)}, bf16[16,64,512]{2,1,0:T(8,128)(2,1)S(1)}, u32[]{:S(2)}, u32[]{:S(2)}) collective-permute-start(bf16[16,64,512]{2,1,0:T(8,128)(2,1)S(1)} %get-tuple-element.27), channel_id=1, source_target_pairs={{0,1},{1,0},{2,3},{3,2},{4,5},{5,4},{6,7},{7,6},{8,9},{9,8},{10,11... | collective-permute-start | bytes 3145736 | tf_op jit(solution)/shard_map/ppermute | solution.py:359
  134.7 55.4 %copy-start.2 = (f32[1,4,3,224,128]{4,3,2,1,0:T(8,128)S(1)}, f32[1,4,3,224,128]{4,3,2,1,0:T(8,128)}, u32[]{:S(2)}) copy-start(f32[1,4,3,224,128]{4,3,2,1,0:T(8,128)} %param.11) | copy-start | bytes 4128772
  134.8 18.9 %collective-permute-start.11 = (bf16[2,64,512]{2,1,0:T(8,128)(2,1)S(1)}, bf16[2,64,512]{2,1,0:T(8,128)(2,1)S(1)}, u32[]{:S(2)}, u32[]{:S(2)}) collective-permute-start(bf16[2,64,512]{2,1,0:T(8,128)(2,1)S(1)} %get-tuple-element.29), channel_id=1, source_target_pairs={{0,2},{2,4},{4,6},{6,8},{8,10},{10,12},{12,14},{14,0},{1,3},{3,5},... | collective-permute-start | bytes 393224 | tf_op jit(solution)/shard_map/ppermute | solution.py:360
  138.1 17.7 %collective-permute-start.12 = (bf16[2,64,512]{2,1,0:T(8,128)(2,1)S(1)}, bf16[2,64,512]{2,1,0:T(8,128)(2,1)S(1)}, u32[]{:S(2)}, u32[]{:S(2)}) collective-permute-start(bf16[2,64,512]{2,1,0:T(8,128)(2,1)S(1)} %get-tuple-element.30), channel_id=1, source_target_pairs={{0,4},{2,6},{4,8},{6,10},{8,12},{10,14},{12,0},{14,2},{1,5},{3,7},... | collective-permute-start | bytes 393224 | tf_op jit(solution)/shard_map/ppermute | solution.py:360
  140.0 18.1 %collective-permute-start.13 = (bf16[2,64,512]{2,1,0:T(8,128)(2,1)S(1)}, bf16[2,64,512]{2,1,0:T(8,128)(2,1)S(1)}, u32[]{:S(2)}, u32[]{:S(2)}) collective-permute-start(bf16[2,64,512]{2,1,0:T(8,128)(2,1)S(1)} %get-tuple-element.31), channel_id=1, source_target_pairs={{0,6},{2,8},{4,10},{6,12},{8,14},{10,0},{12,2},{14,4},{1,7},{3,9},... | collective-permute-start | bytes 393224 | tf_op jit(solution)/shard_map/ppermute | solution.py:360
  144.6 19.2 %collective-permute-start.14 = (bf16[2,64,512]{2,1,0:T(8,128)(2,1)S(1)}, bf16[2,64,512]{2,1,0:T(8,128)(2,1)S(1)}, u32[]{:S(2)}, u32[]{:S(2)}) collective-permute-start(bf16[2,64,512]{2,1,0:T(8,128)(2,1)S(1)} %get-tuple-element.32), channel_id=1, source_target_pairs={{0,8},{2,10},{4,12},{6,14},{8,0},{10,2},{12,4},{14,6},{1,9},{3,11}... | collective-permute-start | bytes 393224 | tf_op jit(solution)/shard_map/ppermute | solution.py:360
  149.2 14.6 %collective-permute-start.15 = (bf16[2,64,512]{2,1,0:T(8,128)(2,1)S(1)}, bf16[2,64,512]{2,1,0:T(8,128)(2,1)}, u32[]{:S(2)}, u32[]{:S(2)}) collective-permute-start(bf16[2,64,512]{2,1,0:T(8,128)(2,1)S(1)} %get-tuple-element.33), channel_id=1, source_target_pairs={{0,10},{2,12},{4,14},{6,0},{8,2},{10,4},{12,6},{14,8},{1,11},{3,13... | collective-permute-start | bytes 393224 | tf_op jit(solution)/shard_map/ppermute | solution.py:360
  153.8 18.0 %collective-permute-start.16 = (bf16[2,64,512]{2,1,0:T(8,128)(2,1)S(1)}, bf16[2,64,512]{2,1,0:T(8,128)(2,1)}, u32[]{:S(2)}, u32[]{:S(2)}) collective-permute-start(bf16[2,64,512]{2,1,0:T(8,128)(2,1)S(1)} %get-tuple-element.34), channel_id=1, source_target_pairs={{0,12},{2,14},{4,0},{6,2},{8,4},{10,6},{12,8},{14,10},{1,13},{3,15... | collective-permute-start | bytes 393224 | tf_op jit(solution)/shard_map/ppermute | solution.py:360
  155.7 17.0 %collective-permute-start.17 = (bf16[2,64,512]{2,1,0:T(8,128)(2,1)S(1)}, bf16[2,64,512]{2,1,0:T(8,128)(2,1)}, u32[]{:S(2)}, u32[]{:S(2)}) collective-permute-start(bf16[2,64,512]{2,1,0:T(8,128)(2,1)S(1)} %get-tuple-element.35), channel_id=1, source_target_pairs={{0,14},{2,0},{4,2},{6,4},{8,6},{10,8},{12,10},{14,12},{1,15},{3,1}... | collective-permute-start | bytes 393224 | tf_op jit(solution)/shard_map/ppermute | solution.py:360
  173.9 19.9 %collective-permute-start.18 = (f32[64,512]{1,0:T(8,128)S(1)}, f32[64,512]{1,0:T(8,128)S(1)}, u32[]{:S(2)}, u32[]{:S(2)}) collective-permute-start(f32[64,512]{1,0:T(8,128)S(1)} %get-tuple-element.47), channel_id=1, source_target_pairs={{0,16},{16,0},{1,17},{17,1},{2,18},{18,2},{3,19},{19,3},{4,20},{20... | collective-permute-start | bytes 393224 | tf_op jit(solution)/shard_map/ppermute | solution.py:365

commit v5 on v4

--- a/solution.py
+++ b/solution.py
@@ -17,26 +17,23 @@
 VMEM_LIMIT = 24 * 1024 * 1024
 
 
-def pack_kernel(cluster_ref, here_ref, tokens_hbm, cotangent_hbm, send_ref, tokens_ref, cotangent_ref, sem):
-    load_t = pltpu.make_async_copy(tokens_hbm, tokens_ref, sem.at[0])
-    load_c = pltpu.make_async_copy(cotangent_hbm, cotangent_ref, sem.at[1])
-    load_t.start()
-    load_c.start()
-    load_t.wait()
-    load_c.wait()
+def pack_kernel(here_ref, cluster_hbm, tokens_hbm, cotangent_hbm, send_hbm, cluster_ref, tokens_ref, cotangent_ref, in_sem, out_sem):
     blocks = tokens_ref.shape[1] // BLK
-
-    def block(b):
-        lanes = slice(b * BLK, (b + 1) * BLK)
-        return jnp.stack([tokens_ref[:, lanes], cotangent_ref[:, lanes]])
-
-    def fill(d, carry):
-        send_ref[d] = block(0)
-        return carry
-
-    lax.fori_loop(0, send_ref.shape[0], fill, 0)
+    pairs = ((cluster_hbm, cluster_ref), (tokens_hbm, tokens_ref), (cotangent_hbm, cotangent_ref))
+    loads = [pltpu.make_async_copy(there, here, in_sem.at[i]) for i, (there, here) in enumerate(pairs)]
+    for load in loads:
+        load.start()
+    for load in loads:
+        load.wait()
+    saves = []
     for b in range(blocks):
-        send_ref[cluster_ref[here_ref[0] * blocks + b]] = block(b)
+        to = cluster_ref[here_ref[0] * blocks + b]
+        for i, source in enumerate((tokens_ref, cotangent_ref)):
+            lanes = source.at[:, pl.ds(b * BLK, BLK)]
+            saves.append(pltpu.make_async_copy(lanes, send_hbm.at[to, i], out_sem.at[2 * b + i]))
+            saves[-1].start()
+    for save in saves:
+        save.wait()
 
 
 def grads_kernel(
@@ -76,8 +73,10 @@
     arrived(xp, 0, late)
     g_s[...] += product(0, xp, late)
     u_s[...] += product(1, xp, late)
-    arrived(yp, owners, range(owners))
-    d_s[...] = product(2, yp, range(owners))
+    arrived(yp, owners, early)
+    d_s[...] = product(2, yp, early)
+    arrived(yp, owners, late)
+    d_s[...] += product(2, yp, late)
     step = 32
 
     def act(i, carry):
@@ -123,16 +122,13 @@
     half = width // 2
     core = core_ref[0]
 
-    def one(o, carry):
+    for o in range(owners):
         w = w_ref[o, 0:2].reshape(2 * units, width)
         part = lax.dot_general(w, dgu_ref[...], (((0,), (0,)), ((), ())), preferred_element_type=jnp.float32)
         j = slot_ref[o]
         low, high = part[:half], part[half:]
         keep_ref[j] = jnp.where(core == 0, low, high)
         give_ref[j] = jnp.where(core == 0, high, low).astype(jnp.bfloat16)
-        return carry
-
-    lax.fori_loop(0, owners, one, 0)
 
 
 def pair_kernel(keep_ref, came_ref, own_ref, *out_refs):
@@ -145,27 +141,34 @@
             out_refs[k - 1][...] = total.astype(jnp.bfloat16)
 
 
-def update_kernel(module_ref, scale_ref, delta_ref, w_ref, m_ref, new_w_hbm, new_m_hbm, new_w, new_m, acc, out_sem):
+def update_kernel(
+    module_ref, scale_ref, delta_hbm, w_ref, m_ref, new_w_hbm, new_m_hbm, delta_ref, new_w, new_m, acc, in_sem, out_sem
+):
     modules, mats, units, width = w_ref.shape
     paths = delta_ref.shape[0]
     step = acc.shape[1]
+    parts = [(k, slice(i * step, (i + 1) * step)) for k in range(mats) for i in range(units // step)]
+    loads = []
+    for k, rows in parts:
+        part = (slice(None), k, rows)
+        loads.append(pltpu.make_async_copy(delta_hbm.at[part], delta_ref.at[part], in_sem.at[len(loads)]))
+        loads[-1].start()
     saves = []
-    for k in range(mats):
-        for i in range(units // step):
-            rows = slice(i * step, (i + 1) * step)
-            acc[...] = jnp.zeros_like(acc)
-            for q in range(paths):
-                acc[module_ref[q]] += delta_ref[q, k, rows, :].astype(jnp.float32)
-            for m in range(modules):
-                mean = acc[m] * scale_ref[m]
-                moment = MU * m_ref[m, k, rows, :] + mean
-                new_m[m, k, rows, :] = moment
-                new_w[m, k, rows, :] = w_ref[m, k, rows, :].astype(jnp.float32) - LR_OUTER * (mean + MU * moment)
-            for here, there in ((new_w, new_w_hbm), (new_m, new_m_hbm)):
-                part = (slice(None), k, rows)
-                save = pltpu.make_async_copy(here.at[part], there.at[part], out_sem.at[len(saves)])
-                save.start()
-                saves.append(save)
+    for load, (k, rows) in zip(loads, parts):
+        load.wait()
+        acc[...] = jnp.zeros_like(acc)
+        for q in range(paths):
+            acc[module_ref[q]] += delta_ref[q, k, rows, :].astype(jnp.float32)
+        for m in range(modules):
+            mean = acc[m] * scale_ref[m]
+            moment = MU * m_ref[m, k, rows, :] + mean
+            new_m[m, k, rows, :] = moment
+            new_w[m, k, rows, :] = w_ref[m, k, rows, :].astype(jnp.float32) - LR_OUTER * (mean + MU * moment)
+        for here, there in ((new_w, new_w_hbm), (new_m, new_m_hbm)):
+            part = (slice(None), k, rows)
+            save = pltpu.make_async_copy(here.at[part], there.at[part], out_sem.at[len(saves)])
+            save.start()
+            saves.append(save)
     for save in saves:
         save.wait()
 
@@ -174,22 +177,28 @@
     return pltpu.with_memory_space_constraint(array, pltpu.HBM)
 
 
-def pack(cluster, here, tokens, cotangent):
+def pack(here, cluster, tokens, cotangent):
     cols, rows = tokens.shape
-    paths = cluster.shape[0] * BLK // rows
+    blocks = rows // BLK
+    paths = cluster.shape[0] // blocks
     smem = pl.BlockSpec(memory_space=pltpu.SMEM)
-    vmem = pl.BlockSpec(memory_space=pltpu.VMEM)
     hbm = pl.BlockSpec(memory_space=pltpu.HBM)
     return pl.pallas_call(
         pack_kernel,
-        out_shape=jax.ShapeDtypeStruct((paths, 2, cols, BLK), tokens.dtype),
-        in_specs=[smem, smem, hbm, hbm],
-        out_specs=vmem,
-        scratch_shapes=[pltpu.VMEM(tokens.shape, tokens.dtype)] * 2 + [pltpu.SemaphoreType.DMA((2,))],
+        out_shape=pltpu.HBM((paths, 2, cols, BLK), tokens.dtype),
+        in_specs=[smem, hbm, hbm, hbm],
+        out_specs=hbm,
+        scratch_shapes=[
+            pltpu.SMEM(cluster.shape, cluster.dtype),
+            pltpu.VMEM(tokens.shape, tokens.dtype),
+            pltpu.VMEM(tokens.shape, tokens.dtype),
+            pltpu.SemaphoreType.DMA((3,)),
+            pltpu.SemaphoreType.DMA((2 * blocks,)),
+        ],
         compiler_params=pltpu.CompilerParams(vmem_limit_bytes=VMEM_LIMIT),
         cost_estimate=pl.CostEstimate(flops=1000, bytes_accessed=1000, transcendentals=0),
         name="pack",
-    )(cluster, here, in_hbm(tokens), in_hbm(cotangent))
+    )(here, in_hbm(cluster), in_hbm(tokens), in_hbm(cotangent))
 
 
 def grads(place, core, w, mine, other):
@@ -268,18 +277,20 @@
     return pl.pallas_call(
         update_kernel,
         out_shape=(jax.ShapeDtypeStruct(momentum.shape, jnp.float32),) * 2,
-        in_specs=[smem, smem, vmem, vmem, vmem],
+        in_specs=[smem, smem, hbm, vmem, vmem],
         out_specs=(hbm, hbm),
         scratch_shapes=[
+            pltpu.VMEM(delta.shape, delta.dtype),
             pltpu.VMEM(momentum.shape, jnp.float32),
             pltpu.VMEM(momentum.shape, jnp.float32),
             pltpu.VMEM((modules, units // 2, width), jnp.float32),
+            pltpu.SemaphoreType.DMA((2 * mats,)),
             pltpu.SemaphoreType.DMA((4 * mats,)),
         ],
         compiler_params=pltpu.CompilerParams(vmem_limit_bytes=VMEM_LIMIT // 2),
         cost_estimate=pl.CostEstimate(flops=10**6, bytes_accessed=8 * 2**20, transcendentals=0),
         name="update",
-    )(modules_of, scale, delta, owned, momentum)
+    )(modules_of, scale, in_hbm(delta), owned, momentum)
 
 
 def pick(array, index):
@@ -327,7 +338,7 @@
     owned = weights[0]
 
     block_ids = jnp.arange(blocks, dtype=jnp.int32)
-    send_x = pack(cluster, here.reshape(1), tokens.T, cotangent.T)
+    send_x = pack(here.reshape(1), cluster, tokens.T, cotangent.T)
     recv_x = lax.all_to_all(
         send_x.reshape(paths * 2, cols, BLK), PATH + ("c",), split_axis=0, concat_axis=0, tiled=True
     ).reshape(paths, 2, cols, BLK)

time: 196 us -> 194 us (0.990)
  the two profiles are of different devices: /device:TPU:401 before, /device:TPU:320 now
where the time goes in v5:
time: 194 us; the launch traced here: 193 us
  starting transfers between devices  82.3 us (42%)
  waiting for transfers between devices  73.6 us (38%)
  Pallas kernels  14.2 us (7%)
  local copies, waits for them, and re-layouts  12.2 us (6%)
  other arithmetic  7.86 us (4%)
  between operations  3.05 us (2%)
    ppermute x7, starting transfers between devices, body(): came = [lax.ppermute(sums[k], 'z', turn(depth, k)) for k in range(1, depth)]  26.5 us
    all_to_all x1, waiting for transfers between devices, body(): lax.all_to_all(delta, BIG, split_axis=0, concat_axis=0, tiled=True)  16.1 us
    all_to_all x1, waiting for transfers between devices, body(): lax.all_to_all(send_w, BIG, split_axis=0, concat_axis=0, tiled=True)  15.3 us
    all_to_all x1, waiting for transfers between devices, body(): lax.all_to_all(send_x.reshape(paths * 2, cols, BLK), PATH + ('c',), split...  13.8 us
    ppermute x7, waiting for transfers between devices, body(): came = [lax.ppermute(sums[k], 'z', turn(depth, k)) for k in range(1, depth)]  12.6 us
    ppermute x3, starting transfers between devices, ring_gather(): up = lax.ppermute(up, 'z', turn(depth, 1))  10.6 us
    all_to_all x1, starting transfers between devices, body(): lax.all_to_all(send_x.reshape(paths * 2, cols, BLK), PATH + ('c',), split...  9.96 us
    all_to_all x1, starting transfers between devices, body(): lax.all_to_all(delta, BIG, split_axis=0, concat_axis=0, tiled=True)  8.43 us
  transfers between devices with their start and end apart: 22, of which 15 were waited for; matrix products, arithmetic and copies ran while one was open for 9% of the time, Pallas kernels for 3%

profile of v5, /device:TPU:320, one launch (start us, length us, event | category | flops | bytes accessed | tf_op | source)
XLA Modules:
  0.0 193.2 jit_solution(6258353593975190449)
XLA Ops:
  2.4 10.0 %all-to-all-start = ((bf16[32,64,128]{2,1,0:T(8,128)(2,1)}), bf16[32,64,128]{2,1,0:T(8,128)(2,1)S(1)}, u32[]{:S(2)}, u32[]{:S(2)}) async-start(bf16[32,64,128]{2,1,0:T(8,128)(2,1)} %bitcast.37), calls=%async_computation | async-start | bytes 1048576 | tf_op jit(solution)/shard_map/all_to_all | solution.py:342
  15.6 13.8 %all-to-all-done = bf16[32,64,128]{2,1,0:T(8,128)(2,1)S(1)} async-done(((bf16[32,64,128]{2,1,0:T(8,128)(2,1)}), bf16[32,64,128]{2,1,0:T(8,128)(2,1)S(1)}, u32[]{:S(2)}, u32[]{:S(2)}) %all-to-all-start) | async-done | bytes 524320 | tf_op jit(solution)/shard_map/all_to_all | solution.py:342
  30.1 1.9 collective-permute-start
  32.1 2.4 %gather_fusion = bf16[16,3,224,128]{3,2,1,0:T(8,128)(2,1)} fusion(bf16[4,3,224,128]{3,2,1,0:T(8,128)(2,1)S(1)} %bitcast.34, s32[1024]{0:T(1024)S(1)} %pad_clamp_fusion.1), kind=kCustom, calls=%fused_computation | custom fusion | bytes 5505088 | tf_op jit(solution)/shard_map/gather | solution.py:297
  34.6 3.3 %collective-permute-done = bf16[128,512]{1,0:T(8,128)(2,1)S(1)} collective-permute-done((bf16[128,512]{1,0:T(8,128)(2,1)S(1)}, bf16[128,512]{1,0:T(8,128)(2,1)S(1)}, u32[]{:S(2)}, u32[]{:S(2)}) %collective-permute-start) | collective-permute-done | bytes 131104 | tf_op jit(solution)/shard_map/ppermute | solution.py:351
  38.5 5.2 %all-to-all-start.1 = ((bf16[16,3,224,128]{3,2,1,0:T(8,128)(2,1)}), bf16[16,3,224,128]{3,2,1,0:T(8,128)(2,1)S(1)}, u32[]{:S(2)}, u32[]{:S(2)}) async-start(bf16[16,3,224,128]{3,2,1,0:T(8,128)(2,1)} %gather_fusion), calls=%async_computation.1 | async-start | bytes 5505024 | tf_op jit(solution)/shard_map/all_to_all | solution.py:353
  47.0 2.5 %collective-permute-start.2 = (bf16[256,512]{1,0:T(8,128)(2,1)S(1)}, bf16[256,512]{1,0:T(8,128)(2,1)S(1)}, u32[]{:S(2)}, u32[]{:S(2)}) collective-permute-start(bf16[256,512]{1,0:T(8,128)(2,1)S(1)} %pad_maximum_fusion), channel_id=1, source_target_pairs={{0,14},{2,0},{4,2},{6,4},{8,6},{10,8},{12,10},{14,12},{1,15},{3,1}... | collective-permute-start | bytes 786440 | tf_op jit(solution)/shard_map/ppermute | solution.py:320
  49.4 3.4 %collective-permute-start.1 = (bf16[256,512]{1,0:T(8,128)(2,1)S(1)}, bf16[256,512]{1,0:T(8,128)(2,1)S(1)}, u32[]{:S(2)}, u32[]{:S(2)}) collective-permute-start(bf16[256,512]{1,0:T(8,128)(2,1)S(1)} %pad_maximum_fusion), channel_id=1, source_target_pairs={{0,2},{2,4},{4,6},{6,8},{8,10},{10,12},{12,14},{14,0},{1,3},{3,5},... | collective-permute-start | bytes 786440 | tf_op jit(solution)/shard_map/ppermute | solution.py:319
  52.8 3.4 %collective-permute-done.2 = bf16[256,512]{1,0:T(8,128)(2,1)S(1)} collective-permute-done((bf16[256,512]{1,0:T(8,128)(2,1)S(1)}, bf16[256,512]{1,0:T(8,128)(2,1)S(1)}, u32[]{:S(2)}, u32[]{:S(2)}) %collective-permute-start.2) | collective-permute-done | bytes 262176 | tf_op jit(solution)/shard_map/ppermute | solution.py:320
  56.2 2.4 %collective-permute-start.4 = (bf16[256,512]{1,0:T(8,128)(2,1)S(1)}, bf16[256,512]{1,0:T(8,128)(2,1)S(1)}, u32[]{:S(2)}, u32[]{:S(2)}) collective-permute-start(bf16[256,512]{1,0:T(8,128)(2,1)S(1)} %collective-permute-done.2), channel_id=1, source_target_pairs={{0,14},{2,0},{4,2},{6,4},{8,6},{10,8},{12,10},{14,12},{1,15},{3,1}... | collective-permute-start | bytes 786440 | tf_op jit(solution)/shard_map/ppermute | solution.py:320
  58.6 3.4 %collective-permute-start.3 = (bf16[256,512]{1,0:T(8,128)(2,1)S(1)}, bf16[256,512]{1,0:T(8,128)(2,1)S(1)}, u32[]{:S(2)}, u32[]{:S(2)}) collective-permute-start(bf16[256,512]{1,0:T(8,128)(2,1)S(1)} %collective-permute-done.1), channel_id=1, source_target_pairs={{0,2},{2,4},{4,6},{6,8},{8,10},{10,12},{12,14},{14,0},{1,3},{3,5},... | collective-permute-start | bytes 786440 | tf_op jit(solution)/shard_map/ppermute | solution.py:319
  64.5 2.4 %collective-permute-start.6 = (bf16[256,512]{1,0:T(8,128)(2,1)S(1)}, bf16[256,512]{1,0:T(8,128)(2,1)S(1)}, u32[]{:S(2)}, u32[]{:S(2)}) collective-permute-start(bf16[256,512]{1,0:T(8,128)(2,1)S(1)} %collective-permute-done.4), channel_id=1, source_target_pairs={{0,14},{2,0},{4,2},{6,4},{8,6},{10,8},{12,10},{14,12},{1,15},{3,1}... | collective-permute-start | bytes 786440 | tf_op jit(solution)/shard_map/ppermute | solution.py:320
  66.9 3.8 %collective-permute-start.5 = (bf16[256,512]{1,0:T(8,128)(2,1)S(1)}, bf16[256,512]{1,0:T(8,128)(2,1)S(1)}, u32[]{:S(2)}, u32[]{:S(2)}) collective-permute-start(bf16[256,512]{1,0:T(8,128)(2,1)S(1)} %collective-permute-done.3), channel_id=1, source_target_pairs={{0,2},{2,4},{4,6},{6,8},{8,10},{10,12},{12,14},{14,0},{1,3},{3,5},... | collective-permute-start | bytes 786440 | tf_op jit(solution)/shard_map/ppermute | solution.py:319
  73.1 2.8 %collective-permute-start.8 = (bf16[128,512]{1,0:T(8,128)(2,1)S(1)}, bf16[128,512]{1,0:T(8,128)(2,1)S(1)}, u32[]{:S(2)}, u32[]{:S(2)}) collective-permute-start(bf16[128,512]{1,0:T(8,128)(2,1)S(1)} %slice.13), channel_id=1, source_target_pairs={{0,14},{2,0},{4,2},{6,4},{8,6},{10,8},{12,10},{14,12},{1,15},{3,1}... | collective-permute-start | bytes 393224 | tf_op jit(solution)/shard_map/ppermute | solution.py:326
  76.2 3.8 %collective-permute-start.7 = (bf16[128,512]{1,0:T(8,128)(2,1)S(1)}, bf16[128,512]{1,0:T(8,128)(2,1)S(1)}, u32[]{:S(2)}, u32[]{:S(2)}) collective-permute-start(bf16[128,512]{1,0:T(8,128)(2,1)S(1)} %slice.12), channel_id=1, source_target_pairs={{0,2},{2,4},{4,6},{6,8},{8,10},{10,12},{12,14},{14,0},{1,3},{3,5},... | collective-permute-start | bytes 393224 | tf_op jit(solution)/shard_map/ppermute | solution.py:325
  81.4 2.9 %collective-permute-done.7 = bf16[128,512]{1,0:T(8,128)(2,1)S(1)} collective-permute-done((bf16[128,512]{1,0:T(8,128)(2,1)S(1)}, bf16[128,512]{1,0:T(8,128)(2,1)S(1)}, u32[]{:S(2)}, u32[]{:S(2)}) %collective-permute-start.7) | collective-permute-done | bytes 131104 | tf_op jit(solution)/shard_map/ppermute | solution.py:325
  92.0 15.3 %all-to-all-done.1.w_ref = bf16[16,3,224,128]{3,2,1,0:T(8,128)(2,1)S(1)} async-done(((bf16[16,3,224,128]{3,2,1,0:T(8,128)(2,1)}), bf16[16,3,224,128]{3,2,1,0:T(8,128)(2,1)S(1)}, u32[]{:S(2)}, u32[]{:S(2)}) %all-to-all-start.1) | async-done | bytes 2752544 | tf_op jit(solution)/shard_map/all_to_all | solution.py:353
  107.3 6.8 %grads.1 = (bf16[16,3,224,128]{3,2,1,0:T(8,128)(2,1)}, bf16[448,512]{1,0:T(8,128)(2,1)}) custom-call(s32[16]{0:T(128)S(1)} %get-tuple-element.45.place_ref, s32[1]{0:T(128)} %bitcast.2.core_ref, bf16[16,3,224,128]{3,2,1,0:T(8,128)(2,1)S(1)} %all-to-all-done.1.w_ref, bf16[2048,512]{1,0:T(8,128)(2,1)} %constant_dynamic-update-slice_fusion.mine_hbm, ...), custom_call_target="tpu_custom_call" | custom-call | flops 2818572288 | bytes 12582912 | tf_op jit(solution)/shard_map/grads/pallas_call | solution.py:210
  114.2 8.4 %all-to-all-start.2 = ((bf16[16,3,224,128]{3,2,1,0:T(8,128)(2,1)}), bf16[16,3,224,128]{3,2,1,0:T(8,128)(2,1)}, u32[]{:S(2)}, u32[]{:S(2)}) async-start(bf16[16,3,224,128]{3,2,1,0:T(8,128)(2,1)} %get-tuple-element.36), calls=%async_computation.2 | async-start | bytes 5505024 | tf_op jit(solution)/shard_map/all_to_all | solution.py:367
  127.4 2.6 %collective-permute-done.10.came_ref = bf16[16,64,512]{2,1,0:T(8,128)(2,1)S(1)} collective-permute-done((bf16[16,64,512]{2,1,0:T(8,128)(2,1)S(1)}, bf16[16,64,512]{2,1,0:T(8,128)(2,1)S(1)}, u32[]{:S(2)}, u32[]{:S(2)}) %collective-permute-start.10) | collective-permute-done | bytes 1048608 | tf_op jit(solution)/shard_map/ppermute | solution.py:370
  130.2 3.5 %collective-permute-start.11 = (bf16[2,64,512]{2,1,0:T(8,128)(2,1)S(1)}, bf16[2,64,512]{2,1,0:T(8,128)(2,1)S(1)}, u32[]{:S(2)}, u32[]{:S(2)}) collective-permute-start(bf16[2,64,512]{2,1,0:T(8,128)(2,1)S(1)} %get-tuple-element.29), channel_id=1, source_target_pairs={{0,2},{2,4},{4,6},{6,8},{8,10},{10,12},{12,14},{14,0},{1,3},{3,5},... | collective-permute-start | bytes 393224 | tf_op jit(solution)/shard_map/ppermute | solution.py:371
  133.7 2.8 %collective-permute-start.12 = (bf16[2,64,512]{2,1,0:T(8,128)(2,1)S(1)}, bf16[2,64,512]{2,1,0:T(8,128)(2,1)S(1)}, u32[]{:S(2)}, u32[]{:S(2)}) collective-permute-start(bf16[2,64,512]{2,1,0:T(8,128)(2,1)S(1)} %get-tuple-element.30), channel_id=1, source_target_pairs={{0,4},{2,6},{4,8},{6,10},{8,12},{10,14},{12,0},{14,2},{1,5},{3,7},... | collective-permute-start | bytes 393224 | tf_op jit(solution)/shard_map/ppermute | solution.py:371
  136.6 2.1 %collective-permute-start.13 = (bf16[2,64,512]{2,1,0:T(8,128)(2,1)S(1)}, bf16[2,64,512]{2,1,0:T(8,128)(2,1)S(1)}, u32[]{:S(2)}, u32[]{:S(2)}) collective-permute-start(bf16[2,64,512]{2,1,0:T(8,128)(2,1)S(1)} %get-tuple-element.31), channel_id=1, source_target_pairs={{0,6},{2,8},{4,10},{6,12},{8,14},{10,0},{12,2},{14,4},{1,7},{3,9},... | collective-permute-start | bytes 393224 | tf_op jit(solution)/shard_map/ppermute | solution.py:371
  138.7 8.2 %collective-permute-start.14 = (bf16[2,64,512]{2,1,0:T(8,128)(2,1)S(1)}, bf16[2,64,512]{2,1,0:T(8,128)(2,1)S(1)}, u32[]{:S(2)}, u32[]{:S(2)}) collective-permute-start(bf16[2,64,512]{2,1,0:T(8,128)(2,1)S(1)} %get-tuple-element.32), channel_id=1, source_target_pairs={{0,8},{2,10},{4,12},{6,14},{8,0},{10,2},{12,4},{14,6},{1,9},{3,11}... | collective-permute-start | bytes 393224 | tf_op jit(solution)/shard_map/ppermute | solution.py:371
  146.9 3.6 %collective-permute-start.15 = (bf16[2,64,512]{2,1,0:T(8,128)(2,1)S(1)}, bf16[2,64,512]{2,1,0:T(8,128)(2,1)}, u32[]{:S(2)}, u32[]{:S(2)}) collective-permute-start(bf16[2,64,512]{2,1,0:T(8,128)(2,1)S(1)} %get-tuple-element.33), channel_id=1, source_target_pairs={{0,10},{2,12},{4,14},{6,0},{8,2},{10,4},{12,6},{14,8},{1,11},{3,13... | collective-permute-start | bytes 393224 | tf_op jit(solution)/shard_map/ppermute | solution.py:371
  150.5 1.9 %collective-permute-start.16 = (bf16[2,64,512]{2,1,0:T(8,128)(2,1)S(1)}, bf16[2,64,512]{2,1,0:T(8,128)(2,1)}, u32[]{:S(2)}, u32[]{:S(2)}) collective-permute-start(bf16[2,64,512]{2,1,0:T(8,128)(2,1)S(1)} %get-tuple-element.34), channel_id=1, source_target_pairs={{0,12},{2,14},{4,0},{6,2},{8,4},{10,6},{12,8},{14,10},{1,13},{3,15... | collective-permute-start | bytes 393224 | tf_op jit(solution)/shard_map/ppermute | solution.py:371
  152.5 4.3 %collective-permute-start.17 = (bf16[2,64,512]{2,1,0:T(8,128)(2,1)S(1)}, bf16[2,64,512]{2,1,0:T(8,128)(2,1)}, u32[]{:S(2)}, u32[]{:S(2)}) collective-permute-start(bf16[2,64,512]{2,1,0:T(8,128)(2,1)S(1)} %get-tuple-element.35), channel_id=1, source_target_pairs={{0,14},{2,0},{4,2},{6,4},{8,6},{10,8},{12,10},{14,12},{1,15},{3,1}... | collective-permute-start | bytes 393224 | tf_op jit(solution)/shard_map/ppermute | solution.py:371
  157.9 6.3 %collective-permute-done.15 = bf16[2,64,512]{2,1,0:T(8,128)(2,1)} collective-permute-done((bf16[2,64,512]{2,1,0:T(8,128)(2,1)S(1)}, bf16[2,64,512]{2,1,0:T(8,128)(2,1)}, u32[]{:S(2)}, u32[]{:S(2)}) %collective-permute-start.15) | collective-permute-done | bytes 131104 | tf_op jit(solution)/shard_map/ppermute | solution.py:371
  164.2 2.0 %collective-permute-done.16 = bf16[2,64,512]{2,1,0:T(8,128)(2,1)} collective-permute-done((bf16[2,64,512]{2,1,0:T(8,128)(2,1)S(1)}, bf16[2,64,512]{2,1,0:T(8,128)(2,1)}, u32[]{:S(2)}, u32[]{:S(2)}) %collective-permute-start.16) | collective-permute-done | bytes 131104 | tf_op jit(solution)/shard_map/ppermute | solution.py:371
  166.2 3.4 %collective-permute-done.17 = bf16[2,64,512]{2,1,0:T(8,128)(2,1)} collective-permute-done((bf16[2,64,512]{2,1,0:T(8,128)(2,1)S(1)}, bf16[2,64,512]{2,1,0:T(8,128)(2,1)}, u32[]{:S(2)}, u32[]{:S(2)}) %collective-permute-start.17) | collective-permute-done | bytes 131104 | tf_op jit(solution)/shard_map/ppermute | solution.py:371
  172.8 16.1 %all-to-all-done.2.delta_hbm = bf16[16,3,224,128]{3,2,1,0:T(8,128)(2,1)} async-done(((bf16[16,3,224,128]{3,2,1,0:T(8,128)(2,1)}), bf16[16,3,224,128]{3,2,1,0:T(8,128)(2,1)}, u32[]{:S(2)}, u32[]{:S(2)}) %all-to-all-start.2) | async-done | bytes 2752544 | tf_op jit(solution)/shard_map/all_to_all | solution.py:367
  188.9 3.7 %update.1 = (f32[4,3,224,128]{3,2,1,0:T(8,128)}, f32[4,3,224,128]{3,2,1,0:T(8,128)}) custom-call(s32[16]{0:T(128)S(1)} %reshape.141.module_ref, f32[4]{0:T(128)S(1)} %broadcast_divide_fusion.scale_ref, bf16[16,3,224,128]{3,2,1,0:T(8,128)(2,1)} %all-to-all-done.2.delta_hbm, bf16[4,3,224,128]{3,2,1,0:T(8,128)(2,1)S(1)} %bitcast.35, f32[4,3,224,128]{3,2,1,0:T(8,128)S(1)} %bitcast.36), custom_call_target="tpu_custom_call" | custom-call | flops 1000000 | bytes 8388608 | tf_op jit(solution)/shard_map/update/pallas_call | solution.py:277
  (79 shorter events, 31.5 us)
Async XLA Ops:
  0.6 89.5 %copy-start = (s32[4,16]{1,0:T(4,128)S(1)}, s32[4,16]{1,0:T(4,128)}, u32[]{:S(2)}) copy-start(s32[4,16]{1,0:T(4,128)} %param.14) | copy-start | bytes 772
  0.6 31.4 %copy-start.1 = (bf16[1,4,3,224,128]{4,3,2,1,0:T(8,128)(2,1)S(1)}, bf16[1,4,3,224,128]{4,3,2,1,0:T(8,128)(2,1)}, u32[]{:S(2)}) copy-start(bf16[1,4,3,224,128]{4,3,2,1,0:T(8,128)(2,1)} %param.10) | copy-start | bytes 2064388
  2.4 27.1 %all-to-all-start = ((bf16[32,64,128]{2,1,0:T(8,128)(2,1)}), bf16[32,64,128]{2,1,0:T(8,128)(2,1)S(1)}, u32[]{:S(2)}, u32[]{:S(2)}) async-start(bf16[32,64,128]{2,1,0:T(8,128)(2,1)} %bitcast.37), calls=%async_computation | async-start | bytes 1048576 | tf_op jit(solution)/shard_map/all_to_all | solution.py:342
  30.1 4.4 %copy-start.4 = (bf16[16,8,4,128]{3,1,2,0:T(8,128)(2,1)}, bf16[16,8,4,128]{3,1,2,0:T(8,128)(2,1)S(1)}, u32[]{:S(2)}) copy-start(bf16[16,8,4,128]{3,1,2,0:T(8,128)(2,1)S(1)} %copy.21) | copy-start | bytes 393220
  30.1 7.7 %collective-permute-start = (bf16[128,512]{1,0:T(8,128)(2,1)S(1)}, bf16[128,512]{1,0:T(8,128)(2,1)S(1)}, u32[]{:S(2)}, u32[]{:S(2)}) collective-permute-start(bf16[128,512]{1,0:T(8,128)(2,1)S(1)} %bitcast.38), channel_id=1, source_target_pairs={{0,16},{16,0},{1,17},{17,1},{2,18},{18,2},{3,19},{19,3},{4,20},{20... | collective-permute-start | bytes 393224 | tf_op jit(solution)/shard_map/ppermute | solution.py:351
  37.8 0.7 copy-start.5
  38.5 68.9 %all-to-all-start.1 = ((bf16[16,3,224,128]{3,2,1,0:T(8,128)(2,1)}), bf16[16,3,224,128]{3,2,1,0:T(8,128)(2,1)S(1)}, u32[]{:S(2)}, u32[]{:S(2)}) async-start(bf16[16,3,224,128]{3,2,1,0:T(8,128)(2,1)} %gather_fusion), calls=%async_computation.1 | async-start | bytes 5505024 | tf_op jit(solution)/shard_map/all_to_all | solution.py:353
  47.0 9.2 %collective-permute-start.2 = (bf16[256,512]{1,0:T(8,128)(2,1)S(1)}, bf16[256,512]{1,0:T(8,128)(2,1)S(1)}, u32[]{:S(2)}, u32[]{:S(2)}) collective-permute-start(bf16[256,512]{1,0:T(8,128)(2,1)S(1)} %pad_maximum_fusion), channel_id=1, source_target_pairs={{0,14},{2,0},{4,2},{6,4},{8,6},{10,8},{12,10},{14,12},{1,15},{3,1}... | collective-permute-start | bytes 786440 | tf_op jit(solution)/shard_map/ppermute | solution.py:320
  49.4 9.2 %collective-permute-start.1 = (bf16[256,512]{1,0:T(8,128)(2,1)S(1)}, bf16[256,512]{1,0:T(8,128)(2,1)S(1)}, u32[]{:S(2)}, u32[]{:S(2)}) collective-permute-start(bf16[256,512]{1,0:T(8,128)(2,1)S(1)} %pad_maximum_fusion), channel_id=1, source_target_pairs={{0,2},{2,4},{4,6},{6,8},{8,10},{10,12},{12,14},{14,0},{1,3},{3,5},... | collective-permute-start | bytes 786440 | tf_op jit(solution)/shard_map/ppermute | solution.py:319
  56.2 8.3 %collective-permute-start.4 = (bf16[256,512]{1,0:T(8,128)(2,1)S(1)}, bf16[256,512]{1,0:T(8,128)(2,1)S(1)}, u32[]{:S(2)}, u32[]{:S(2)}) collective-permute-start(bf16[256,512]{1,0:T(8,128)(2,1)S(1)} %collective-permute-done.2), channel_id=1, source_target_pairs={{0,14},{2,0},{4,2},{6,4},{8,6},{10,8},{12,10},{14,12},{1,15},{3,1}... | collective-permute-start | bytes 786440 | tf_op jit(solution)/shard_map/ppermute | solution.py:320
  58.6 8.3 %collective-permute-start.3 = (bf16[256,512]{1,0:T(8,128)(2,1)S(1)}, bf16[256,512]{1,0:T(8,128)(2,1)S(1)}, u32[]{:S(2)}, u32[]{:S(2)}) collective-permute-start(bf16[256,512]{1,0:T(8,128)(2,1)S(1)} %collective-permute-done.1), channel_id=1, source_target_pairs={{0,2},{2,4},{4,6},{6,8},{8,10},{10,12},{12,14},{14,0},{1,3},{3,5},... | collective-permute-start | bytes 786440 | tf_op jit(solution)/shard_map/ppermute | solution.py:319
  62.0 25.5 %copy-start.6 = (s32[16,1]{0,1:T(1,128)S(1)}, s32[16,1]{0,1:T(1,128)}, u32[]{:S(2)}) copy-start(s32[16,1]{0,1:T(1,128)} %param.13) | copy-start | bytes 196
  62.0 28.4 %copy-start.7 = (s32[8]{0:T(128)S(1)}, s32[8]{0:T(128)}, u32[]{:S(2)}) copy-start(s32[8]{0:T(128)} %constant.87.clone) | copy-start | bytes 100
  64.5 8.7 %collective-permute-start.6 = (bf16[256,512]{1,0:T(8,128)(2,1)S(1)}, bf16[256,512]{1,0:T(8,128)(2,1)S(1)}, u32[]{:S(2)}, u32[]{:S(2)}) collective-permute-start(bf16[256,512]{1,0:T(8,128)(2,1)S(1)} %collective-permute-done.4), channel_id=1, source_target_pairs={{0,14},{2,0},{4,2},{6,4},{8,6},{10,8},{12,10},{14,12},{1,15},{3,1}... | collective-permute-start | bytes 786440 | tf_op jit(solution)/shard_map/ppermute | solution.py:320
  66.9 9.2 %collective-permute-start.5 = (bf16[256,512]{1,0:T(8,128)(2,1)S(1)}, bf16[256,512]{1,0:T(8,128)(2,1)S(1)}, u32[]{:S(2)}, u32[]{:S(2)}) collective-permute-start(bf16[256,512]{1,0:T(8,128)(2,1)S(1)} %collective-permute-done.3), channel_id=1, source_target_pairs={{0,2},{2,4},{4,6},{6,8},{8,10},{10,12},{12,14},{14,0},{1,3},{3,5},... | collective-permute-start | bytes 786440 | tf_op jit(solution)/shard_map/ppermute | solution.py:319
  73.1 11.8 %collective-permute-start.8 = (bf16[128,512]{1,0:T(8,128)(2,1)S(1)}, bf16[128,512]{1,0:T(8,128)(2,1)S(1)}, u32[]{:S(2)}, u32[]{:S(2)}) collective-permute-start(bf16[128,512]{1,0:T(8,128)(2,1)S(1)} %slice.13), channel_id=1, source_target_pairs={{0,14},{2,0},{4,2},{6,4},{8,6},{10,8},{12,10},{14,12},{1,15},{3,1}... | collective-permute-start | bytes 393224 | tf_op jit(solution)/shard_map/ppermute | solution.py:326
  76.2 8.1 %collective-permute-start.7 = (bf16[128,512]{1,0:T(8,128)(2,1)S(1)}, bf16[128,512]{1,0:T(8,128)(2,1)S(1)}, u32[]{:S(2)}, u32[]{:S(2)}) collective-permute-start(bf16[128,512]{1,0:T(8,128)(2,1)S(1)} %slice.12), channel_id=1, source_target_pairs={{0,2},{2,4},{4,6},{6,8},{8,10},{10,12},{12,14},{14,0},{1,3},{3,5},... | collective-permute-start | bytes 393224 | tf_op jit(solution)/shard_map/ppermute | solution.py:325
  85.6 6.4 %collective-permute-start.9 = (bf16[2048,512]{1,0:T(8,128)(2,1)}, bf16[2048,512]{1,0:T(8,128)(2,1)}, u32[]{:S(2)}, u32[]{:S(2)}) collective-permute-start(bf16[2048,512]{1,0:T(8,128)(2,1)} %constant_dynamic-update-slice_fusion.mine_hbm), channel_id=1, source_target_pairs={{0,1},{1,0},{2,3},{3,2},{4,5},{5,4},{6,7},{7,6},{8,9},{9,8},{10,11... | collective-permute-start | bytes 6291464 | tf_op jit(solution)/shard_map/ppermute | solution.py:356
  114.2 74.7 %all-to-all-start.2 = ((bf16[16,3,224,128]{3,2,1,0:T(8,128)(2,1)}), bf16[16,3,224,128]{3,2,1,0:T(8,128)(2,1)}, u32[]{:S(2)}, u32[]{:S(2)}) async-start(bf16[16,3,224,128]{3,2,1,0:T(8,128)(2,1)} %get-tuple-element.36), calls=%async_computation.2 | async-start | bytes 5505024 | tf_op jit(solution)/shard_map/all_to_all | solution.py:367
  122.6 1.0 copy-start.3
  125.5 4.6 %collective-permute-start.10 = (bf16[16,64,512]{2,1,0:T(8,128)(2,1)S(1)}, bf16[16,64,512]{2,1,0:T(8,128)(2,1)S(1)}, u32[]{:S(2)}, u32[]{:S(2)}) collective-permute-start(bf16[16,64,512]{2,1,0:T(8,128)(2,1)S(1)} %get-tuple-element.27), channel_id=1, source_target_pairs={{0,1},{1,0},{2,3},{3,2},{4,5},{5,4},{6,7},{7,6},{8,9},{9,8},{10,11... | collective-permute-start | bytes 3145736 | tf_op jit(solution)/shard_map/ppermute | solution.py:370
  130.0 58.8 %copy-start.2 = (f32[1,4,3,224,128]{4,3,2,1,0:T(8,128)S(1)}, f32[1,4,3,224,128]{4,3,2,1,0:T(8,128)}, u32[]{:S(2)}) copy-start(f32[1,4,3,224,128]{4,3,2,1,0:T(8,128)} %param.11) | copy-start | bytes 4128772
  130.2 20.3 %collective-permute-start.11 = (bf16[2,64,512]{2,1,0:T(8,128)(2,1)S(1)}, bf16[2,64,512]{2,1,0:T(8,128)(2,1)S(1)}, u32[]{:S(2)}, u32[]{:S(2)}) collective-permute-start(bf16[2,64,512]{2,1,0:T(8,128)(2,1)S(1)} %get-tuple-element.29), channel_id=1, source_target_pairs={{0,2},{2,4},{4,6},{6,8},{8,10},{10,12},{12,14},{14,0},{1,3},{3,5},... | collective-permute-start | bytes 393224 | tf_op jit(solution)/shard_map/ppermute | solution.py:371
  133.7 18.8 %collective-permute-start.12 = (bf16[2,64,512]{2,1,0:T(8,128)(2,1)S(1)}, bf16[2,64,512]{2,1,0:T(8,128)(2,1)S(1)}, u32[]{:S(2)}, u32[]{:S(2)}) collective-permute-start(bf16[2,64,512]{2,1,0:T(8,128)(2,1)S(1)} %get-tuple-element.30), channel_id=1, source_target_pairs={{0,4},{2,6},{4,8},{6,10},{8,12},{10,14},{12,0},{14,2},{1,5},{3,7},... | collective-permute-start | bytes 393224 | tf_op jit(solution)/shard_map/ppermute | solution.py:371
  136.6 21.3 %collective-permute-start.13 = (bf16[2,64,512]{2,1,0:T(8,128)(2,1)S(1)}, bf16[2,64,512]{2,1,0:T(8,128)(2,1)S(1)}, u32[]{:S(2)}, u32[]{:S(2)}) collective-permute-start(bf16[2,64,512]{2,1,0:T(8,128)(2,1)S(1)} %get-tuple-element.31), channel_id=1, source_target_pairs={{0,6},{2,8},{4,10},{6,12},{8,14},{10,0},{12,2},{14,4},{1,7},{3,9},... | collective-permute-start | bytes 393224 | tf_op jit(solution)/shard_map/ppermute | solution.py:371
  138.7 19.2 %collective-permute-start.14 = (bf16[2,64,512]{2,1,0:T(8,128)(2,1)S(1)}, bf16[2,64,512]{2,1,0:T(8,128)(2,1)S(1)}, u32[]{:S(2)}, u32[]{:S(2)}) collective-permute-start(bf16[2,64,512]{2,1,0:T(8,128)(2,1)S(1)} %get-tuple-element.32), channel_id=1, source_target_pairs={{0,8},{2,10},{4,12},{6,14},{8,0},{10,2},{12,4},{14,6},{1,9},{3,11}... | collective-permute-start | bytes 393224 | tf_op jit(solution)/shard_map/ppermute | solution.py:371
  146.9 17.3 %collective-permute-start.15 = (bf16[2,64,512]{2,1,0:T(8,128)(2,1)S(1)}, bf16[2,64,512]{2,1,0:T(8,128)(2,1)}, u32[]{:S(2)}, u32[]{:S(2)}) collective-permute-start(bf16[2,64,512]{2,1,0:T(8,128)(2,1)S(1)} %get-tuple-element.33), channel_id=1, source_target_pairs={{0,10},{2,12},{4,14},{6,0},{8,2},{10,4},{12,6},{14,8},{1,11},{3,13... | collective-permute-start | bytes 393224 | tf_op jit(solution)/shard_map/ppermute | solution.py:371
  150.5 15.7 %collective-permute-start.16 = (bf16[2,64,512]{2,1,0:T(8,128)(2,1)S(1)}, bf16[2,64,512]{2,1,0:T(8,128)(2,1)}, u32[]{:S(2)}, u32[]{:S(2)}) collective-permute-start(bf16[2,64,512]{2,1,0:T(8,128)(2,1)S(1)} %get-tuple-element.34), channel_id=1, source_target_pairs={{0,12},{2,14},{4,0},{6,2},{8,4},{10,6},{12,8},{14,10},{1,13},{3,15... | collective-permute-start | bytes 393224 | tf_op jit(solution)/shard_map/ppermute | solution.py:371
  152.5 17.1 %collective-permute-start.17 = (bf16[2,64,512]{2,1,0:T(8,128)(2,1)S(1)}, bf16[2,64,512]{2,1,0:T(8,128)(2,1)}, u32[]{:S(2)}, u32[]{:S(2)}) collective-permute-start(bf16[2,64,512]{2,1,0:T(8,128)(2,1)S(1)} %get-tuple-element.35), channel_id=1, source_target_pairs={{0,14},{2,0},{4,2},{6,4},{8,6},{10,8},{12,10},{14,12},{1,15},{3,1}... | collective-permute-start | bytes 393224 | tf_op jit(solution)/shard_map/ppermute | solution.py:371
  170.8 21.7 %collective-permute-start.18 = (f32[64,512]{1,0:T(8,128)S(1)}, f32[64,512]{1,0:T(8,128)S(1)}, u32[]{:S(2)}, u32[]{:S(2)}) collective-permute-start(f32[64,512]{1,0:T(8,128)S(1)} %get-tuple-element.47), channel_id=1, source_target_pairs={{0,16},{16,0},{1,17},{17,1},{2,18},{18,2},{3,19},{19,3},{4,20},{20... | collective-permute-start | bytes 393224 | tf_op jit(solution)/shard_map/ppermute | solution.py:376

commit v6 on v5

--- a/solution.py
+++ b/solution.py
@@ -142,7 +142,22 @@
 
 
 def update_kernel(
-    module_ref, scale_ref, delta_hbm, w_ref, m_ref, new_w_hbm, new_m_hbm, delta_ref, new_w, new_m, acc, in_sem, out_sem
+    module_ref,
+    scale_ref,
+    delta_hbm,
+    w_ref,
+    m_ref,
+    ours_ref,
+    theirs_ref,
+    new_w_hbm,
+    new_m_hbm,
+    grad_ref,
+    delta_ref,
+    new_w,
+    new_m,
+    acc,
+    in_sem,
+    out_sem,
 ):
     modules, mats, units, width = w_ref.shape
     paths = delta_ref.shape[0]
@@ -153,6 +168,7 @@
         part = (slice(None), k, rows)
         loads.append(pltpu.make_async_copy(delta_hbm.at[part], delta_ref.at[part], in_sem.at[len(loads)]))
         loads[-1].start()
+    grad_ref[...] = (ours_ref[...] + theirs_ref[...]).astype(grad_ref.dtype)
     saves = []
     for load, (k, rows) in zip(loads, parts):
         load.wait()
@@ -269,16 +285,17 @@
     )(keep, came)
 
 
-def update(modules_of, scale, delta, owned, momentum):
+def update(modules_of, scale, delta, owned, momentum, ours, theirs):
     modules, mats, units, width = owned.shape
     smem = pl.BlockSpec(memory_space=pltpu.SMEM)
     vmem = pl.BlockSpec(memory_space=pltpu.VMEM)
     hbm = pl.BlockSpec(memory_space=pltpu.HBM)
     return pl.pallas_call(
         update_kernel,
-        out_shape=(jax.ShapeDtypeStruct(momentum.shape, jnp.float32),) * 2,
-        in_specs=[smem, smem, hbm, vmem, vmem],
-        out_specs=(hbm, hbm),
+        out_shape=(jax.ShapeDtypeStruct(momentum.shape, jnp.float32),) * 2
+        + (jax.ShapeDtypeStruct(ours.shape, jnp.bfloat16),),
+        in_specs=[smem, smem, hbm, vmem, vmem, vmem, vmem],
+        out_specs=(hbm, hbm, vmem),
         scratch_shapes=[
             pltpu.VMEM(delta.shape, delta.dtype),
             pltpu.VMEM(momentum.shape, jnp.float32),
@@ -290,7 +307,7 @@
         compiler_params=pltpu.CompilerParams(vmem_limit_bytes=VMEM_LIMIT // 2),
         cost_estimate=pl.CostEstimate(flops=10**6, bytes_accessed=8 * 2**20, transcendentals=0),
         name="update",
-    )(modules_of, scale, in_hbm(delta), owned, momentum)
+    )(modules_of, scale, in_hbm(delta), owned, momentum, ours, theirs)
 
 
 def pick(array, index):
@@ -376,9 +393,11 @@
     theirs = lax.ppermute(lax.dynamic_index_in_dim(total, 1 - yl, 0, keepdims=False), "yl", swap)
     member = modules_of[None, :] == jnp.arange(MODULES, dtype=jnp.int32)[:, None]
     counts = jnp.sum(member.astype(jnp.float32), axis=1)
-    new_tiles, new_moment = update(transposed(modules_of), 1.0 / counts, recv_delta, owned, momentum[0])
-    total, new_moment = lax.optimization_barrier((lax.dynamic_index_in_dim(total, yl, 0, keepdims=False), new_moment))
-    input_grad = (total + theirs).astype(jnp.bfloat16).T
+    ours = lax.dynamic_index_in_dim(total, yl, 0, keepdims=False)
+    new_tiles, new_moment, grad = update(
+        transposed(modules_of), 1.0 / counts, recv_delta, owned, momentum[0], ours, theirs
+    )
+    input_grad = grad.T
     return (input_grad, new_tiles[None], new_moment[None])
 
 

time: 194 us -> 194 us (level)
  the two profiles are of different devices: /device:TPU:320 before, /device:TPU:1 now
where the time goes in v6:
time: 194 us; the launch traced here: 192 us
  starting transfers between devices  99.8 us (51%)
  waiting for transfers between devices  55.3 us (29%)
  Pallas kernels  14.8 us (8%)
  local copies, waits for them, and re-layouts  12.2 us (6%)
  other arithmetic  7.18 us (4%)
  between operations  3.07 us (2%)
    ppermute x7, starting transfers between devices, body(): came = [lax.ppermute(sums[k], 'z', turn(depth, k)) for k in range(1, depth)]  30.5 us
    ppermute x3, starting transfers between devices, ring_gather(): down = lax.ppermute(down, 'z', turn(depth, -1))  17.7 us
    ppermute x7, waiting for transfers between devices, body(): came = [lax.ppermute(sums[k], 'z', turn(depth, k)) for k in range(1, depth)]  15.5 us
    all_to_all x1, waiting for transfers between devices, body(): lax.all_to_all(send_x.reshape(paths * 2, cols, BLK), PATH + ('c',), split...  15.2 us
    all_to_all x1, starting transfers between devices, body(): lax.all_to_all(send_x.reshape(paths * 2, cols, BLK), PATH + ('c',), split...  11.2 us
    all_to_all x1, starting transfers between devices, body(): lax.all_to_all(delta, BIG, split_axis=0, concat_axis=0, tiled=True)  8.63 us
    ppermute x3, starting transfers between devices, ring_gather(): up = lax.ppermute(up, 'z', turn(depth, 1))  7.82 us
    ppermute x1, waiting for transfers between devices, body(): lax.ppermute(lax.dynamic_index_in_dim(total, 1 - yl, 0, keepdims=False),...  7.29 us
  transfers between devices with their start and end apart: 22, of which 11 were waited for; matrix products, arithmetic and copies ran while one was open for 9% of the time, Pallas kernels for 1%

profile of v6, /device:TPU:1, one launch (start us, length us, event | category | flops | bytes accessed | tf_op | source)
XLA Modules:
  0.0 192.4 jit_solution(56011686613926393)
XLA Ops:
  2.4 11.2 %all-to-all-start = ((bf16[32,64,128]{2,1,0:T(8,128)(2,1)}), bf16[32,64,128]{2,1,0:T(8,128)(2,1)S(1)}, u32[]{:S(2)}, u32[]{:S(2)}) async-start(bf16[32,64,128]{2,1,0:T(8,128)(2,1)} %bitcast.36), calls=%async_computation | async-start | bytes 1048576 | tf_op jit(solution)/shard_map/all_to_all | solution.py:359
  16.8 15.2 %all-to-all-done = bf16[32,64,128]{2,1,0:T(8,128)(2,1)S(1)} async-done(((bf16[32,64,128]{2,1,0:T(8,128)(2,1)}), bf16[32,64,128]{2,1,0:T(8,128)(2,1)S(1)}, u32[]{:S(2)}, u32[]{:S(2)}) %all-to-all-start) | async-done | bytes 524320 | tf_op jit(solution)/shard_map/all_to_all | solution.py:359
  32.7 1.9 collective-permute-start
  34.7 2.4 %gather_fusion = bf16[16,3,224,128]{3,2,1,0:T(8,128)(2,1)} fusion(bf16[4,3,224,128]{3,2,1,0:T(8,128)(2,1)S(1)} %bitcast.33, s32[1024]{0:T(1024)S(1)} %pad_clamp_fusion.1), kind=kCustom, calls=%fused_computation | custom fusion | bytes 5505088 | tf_op jit(solution)/shard_map/gather | solution.py:314
  37.1 2.1 %collective-permute-done = bf16[128,512]{1,0:T(8,128)(2,1)S(1)} collective-permute-done((bf16[128,512]{1,0:T(8,128)(2,1)S(1)}, bf16[128,512]{1,0:T(8,128)(2,1)S(1)}, u32[]{:S(2)}, u32[]{:S(2)}) %collective-permute-start) | collective-permute-done | bytes 131104 | tf_op jit(solution)/shard_map/ppermute | solution.py:368
  39.9 3.9 %all-to-all-start.1 = ((bf16[16,3,224,128]{3,2,1,0:T(8,128)(2,1)}), bf16[16,3,224,128]{3,2,1,0:T(8,128)(2,1)S(1)}, u32[]{:S(2)}, u32[]{:S(2)}) async-start(bf16[16,3,224,128]{3,2,1,0:T(8,128)(2,1)} %gather_fusion), calls=%async_computation.1 | async-start | bytes 5505024 | tf_op jit(solution)/shard_map/all_to_all | solution.py:370
  47.1 4.0 %collective-permute-start.1 = (bf16[256,512]{1,0:T(8,128)(2,1)S(1)}, bf16[256,512]{1,0:T(8,128)(2,1)S(1)}, u32[]{:S(2)}, u32[]{:S(2)}) collective-permute-start(bf16[256,512]{1,0:T(8,128)(2,1)S(1)} %pad_maximum_fusion), channel_id=1, source_target_pairs={{0,2},{2,4},{4,6},{6,8},{8,10},{10,12},{12,14},{14,0},{1,3},{3,5},... | collective-permute-start | bytes 786440 | tf_op jit(solution)/shard_map/ppermute | solution.py:336
  51.1 8.6 %collective-permute-start.2 = (bf16[256,512]{1,0:T(8,128)(2,1)S(1)}, bf16[256,512]{1,0:T(8,128)(2,1)S(1)}, u32[]{:S(2)}, u32[]{:S(2)}) collective-permute-start(bf16[256,512]{1,0:T(8,128)(2,1)S(1)} %pad_maximum_fusion), channel_id=1, source_target_pairs={{0,14},{2,0},{4,2},{6,4},{8,6},{10,8},{12,10},{14,12},{1,15},{3,1}... | collective-permute-start | bytes 786440 | tf_op jit(solution)/shard_map/ppermute | solution.py:337
  59.7 3.3 %collective-permute-done.1 = bf16[256,512]{1,0:T(8,128)(2,1)S(1)} collective-permute-done((bf16[256,512]{1,0:T(8,128)(2,1)S(1)}, bf16[256,512]{1,0:T(8,128)(2,1)S(1)}, u32[]{:S(2)}, u32[]{:S(2)}) %collective-permute-start.1) | collective-permute-done | bytes 262176 | tf_op jit(solution)/shard_map/ppermute | solution.py:336
  64.9 4.6 %collective-permute-start.4 = (bf16[256,512]{1,0:T(8,128)(2,1)S(1)}, bf16[256,512]{1,0:T(8,128)(2,1)S(1)}, u32[]{:S(2)}, u32[]{:S(2)}) collective-permute-start(bf16[256,512]{1,0:T(8,128)(2,1)S(1)} %collective-permute-done.2), channel_id=1, source_target_pairs={{0,14},{2,0},{4,2},{6,4},{8,6},{10,8},{12,10},{14,12},{1,15},{3,1}... | collective-permute-start | bytes 786440 | tf_op jit(solution)/shard_map/ppermute | solution.py:337
  73.7 4.6 %collective-permute-start.6 = (bf16[256,512]{1,0:T(8,128)(2,1)S(1)}, bf16[256,512]{1,0:T(8,128)(2,1)S(1)}, u32[]{:S(2)}, u32[]{:S(2)}) collective-permute-start(bf16[256,512]{1,0:T(8,128)(2,1)S(1)} %collective-permute-done.4), channel_id=1, source_target_pairs={{0,14},{2,0},{4,2},{6,4},{8,6},{10,8},{12,10},{14,12},{1,15},{3,1}... | collective-permute-start | bytes 786440 | tf_op jit(solution)/shard_map/ppermute | solution.py:337
  80.5 1.9 collective-permute-start.7
  82.5 4.6 %collective-permute-start.8 = (bf16[128,512]{1,0:T(8,128)(2,1)S(1)}, bf16[128,512]{1,0:T(8,128)(2,1)S(1)}, u32[]{:S(2)}, u32[]{:S(2)}) collective-permute-start(bf16[128,512]{1,0:T(8,128)(2,1)S(1)} %slice.13), channel_id=1, source_target_pairs={{0,14},{2,0},{4,2},{6,4},{8,6},{10,8},{12,10},{14,12},{1,15},{3,1}... | collective-permute-start | bytes 393224 | tf_op jit(solution)/shard_map/ppermute | solution.py:343
  89.8 6.6 %collective-permute-start.9 = (bf16[2048,512]{1,0:T(8,128)(2,1)}, bf16[2048,512]{1,0:T(8,128)(2,1)}, u32[]{:S(2)}, u32[]{:S(2)}) collective-permute-start(bf16[2048,512]{1,0:T(8,128)(2,1)} %constant_dynamic-update-slice_fusion.mine_hbm), channel_id=1, source_target_pairs={{0,1},{1,0},{2,3},{3,2},{4,5},{5,4},{6,7},{7,6},{8,9},{9,8},{10,11... | collective-permute-start | bytes 6291464 | tf_op jit(solution)/shard_map/ppermute | solution.py:373
  100.5 7.0 %all-to-all-done.1.w_ref = bf16[16,3,224,128]{3,2,1,0:T(8,128)(2,1)S(1)} async-done(((bf16[16,3,224,128]{3,2,1,0:T(8,128)(2,1)}), bf16[16,3,224,128]{3,2,1,0:T(8,128)(2,1)S(1)}, u32[]{:S(2)}, u32[]{:S(2)}) %all-to-all-start.1) | async-done | bytes 2752544 | tf_op jit(solution)/shard_map/all_to_all | solution.py:370
  107.5 6.8 %grads.1 = (bf16[16,3,224,128]{3,2,1,0:T(8,128)(2,1)}, bf16[448,512]{1,0:T(8,128)(2,1)}) custom-call(s32[16]{0:T(128)S(1)} %multiply_add_fusion.2.place_ref, s32[1]{0:T(128)} %bitcast.4.core_ref, bf16[16,3,224,128]{3,2,1,0:T(8,128)(2,1)S(1)} %all-to-all-done.1.w_ref, bf16[2048,512]{1,0:T(8,128)(2,1)} %constant_dynamic-update-slice_fusion.mine_hbm, ...), custom_call_target="tpu_custom_call" | custom-call | flops 2818572288 | bytes 12582912 | tf_op jit(solution)/shard_map/grads/pallas_call | solution.py:226
  114.3 8.6 %all-to-all-start.2 = ((bf16[16,3,224,128]{3,2,1,0:T(8,128)(2,1)}), bf16[16,3,224,128]{3,2,1,0:T(8,128)(2,1)}, u32[]{:S(2)}, u32[]{:S(2)}) async-start(bf16[16,3,224,128]{3,2,1,0:T(8,128)(2,1)} %get-tuple-element.24), calls=%async_computation.2 | async-start | bytes 5505024 | tf_op jit(solution)/shard_map/all_to_all | solution.py:384
  125.8 3.1 %collective-permute-start.10 = (bf16[16,64,512]{2,1,0:T(8,128)(2,1)S(1)}, bf16[16,64,512]{2,1,0:T(8,128)(2,1)S(1)}, u32[]{:S(2)}, u32[]{:S(2)}) collective-permute-start(bf16[16,64,512]{2,1,0:T(8,128)(2,1)S(1)} %get-tuple-element.27), channel_id=1, source_target_pairs={{0,1},{1,0},{2,3},{3,2},{4,5},{5,4},{6,7},{7,6},{8,9},{9,8},{10,11... | collective-permute-start | bytes 3145736 | tf_op jit(solution)/shard_map/ppermute | solution.py:387
  128.9 2.3 %collective-permute-done.10.came_ref = bf16[16,64,512]{2,1,0:T(8,128)(2,1)S(1)} collective-permute-done((bf16[16,64,512]{2,1,0:T(8,128)(2,1)S(1)}, bf16[16,64,512]{2,1,0:T(8,128)(2,1)S(1)}, u32[]{:S(2)}, u32[]{:S(2)}) %collective-permute-start.10) | collective-permute-done | bytes 1048608 | tf_op jit(solution)/shard_map/ppermute | solution.py:387
  131.3 10.8 %collective-permute-start.17 = (bf16[2,64,512]{2,1,0:T(8,128)(2,1)S(1)}, bf16[2,64,512]{2,1,0:T(8,128)(2,1)S(1)}, u32[]{:S(2)}, u32[]{:S(2)}) collective-permute-start(bf16[2,64,512]{2,1,0:T(8,128)(2,1)S(1)} %get-tuple-element.35), channel_id=1, source_target_pairs={{0,14},{2,0},{4,2},{6,4},{8,6},{10,8},{12,10},{14,12},{1,15},{3,1}... | collective-permute-start | bytes 393224 | tf_op jit(solution)/shard_map/ppermute | solution.py:388
  142.1 2.2 %collective-permute-start.16 = (bf16[2,64,512]{2,1,0:T(8,128)(2,1)S(1)}, bf16[2,64,512]{2,1,0:T(8,128)(2,1)S(1)}, u32[]{:S(2)}, u32[]{:S(2)}) collective-permute-start(bf16[2,64,512]{2,1,0:T(8,128)(2,1)S(1)} %get-tuple-element.34), channel_id=1, source_target_pairs={{0,12},{2,14},{4,0},{6,2},{8,4},{10,6},{12,8},{14,10},{1,13},{3,15... | collective-permute-start | bytes 393224 | tf_op jit(solution)/shard_map/ppermute | solution.py:388
  144.3 1.9 collective-permute-start.15
  146.2 7.3 %collective-permute-start.14 = (bf16[2,64,512]{2,1,0:T(8,128)(2,1)S(1)}, bf16[2,64,512]{2,1,0:T(8,128)(2,1)S(1)}, u32[]{:S(2)}, u32[]{:S(2)}) collective-permute-start(bf16[2,64,512]{2,1,0:T(8,128)(2,1)S(1)} %get-tuple-element.32), channel_id=1, source_target_pairs={{0,8},{2,10},{4,12},{6,14},{8,0},{10,2},{12,4},{14,6},{1,9},{3,11}... | collective-permute-start | bytes 393224 | tf_op jit(solution)/shard_map/ppermute | solution.py:388
  153.5 1.9 collective-permute-start.13
  155.5 3.1 %collective-permute-start.12 = (bf16[2,64,512]{2,1,0:T(8,128)(2,1)S(1)}, bf16[2,64,512]{2,1,0:T(8,128)(2,1)}, u32[]{:S(2)}, u32[]{:S(2)}) collective-permute-start(bf16[2,64,512]{2,1,0:T(8,128)(2,1)S(1)} %get-tuple-element.30), channel_id=1, source_target_pairs={{0,4},{2,6},{4,8},{6,10},{8,12},{10,14},{12,0},{14,2},{1,5},{3,7},... | collective-permute-start | bytes 393224 | tf_op jit(solution)/shard_map/ppermute | solution.py:388
  158.6 3.3 %collective-permute-start.11 = (bf16[2,64,512]{2,1,0:T(8,128)(2,1)S(1)}, bf16[2,64,512]{2,1,0:T(8,128)(2,1)}, u32[]{:S(2)}, u32[]{:S(2)}) collective-permute-start(bf16[2,64,512]{2,1,0:T(8,128)(2,1)S(1)} %get-tuple-element.29), channel_id=1, source_target_pairs={{0,2},{2,4},{4,6},{6,8},{8,10},{10,12},{12,14},{14,0},{1,3},{3,5},... | collective-permute-start | bytes 393224 | tf_op jit(solution)/shard_map/ppermute | solution.py:388
  162.1 6.1 %collective-permute-done.13 = bf16[2,64,512]{2,1,0:T(8,128)(2,1)} collective-permute-done((bf16[2,64,512]{2,1,0:T(8,128)(2,1)S(1)}, bf16[2,64,512]{2,1,0:T(8,128)(2,1)}, u32[]{:S(2)}, u32[]{:S(2)}) %collective-permute-start.13) | collective-permute-done | bytes 131104 | tf_op jit(solution)/shard_map/ppermute | solution.py:388
  168.2 5.4 %collective-permute-done.12 = bf16[2,64,512]{2,1,0:T(8,128)(2,1)} collective-permute-done((bf16[2,64,512]{2,1,0:T(8,128)(2,1)S(1)}, bf16[2,64,512]{2,1,0:T(8,128)(2,1)}, u32[]{:S(2)}, u32[]{:S(2)}) %collective-permute-start.12) | collective-permute-done | bytes 131104 | tf_op jit(solution)/shard_map/ppermute | solution.py:388
  173.6 4.0 %collective-permute-done.11 = bf16[2,64,512]{2,1,0:T(8,128)(2,1)} collective-permute-done((bf16[2,64,512]{2,1,0:T(8,128)(2,1)S(1)}, bf16[2,64,512]{2,1,0:T(8,128)(2,1)}, u32[]{:S(2)}, u32[]{:S(2)}) %collective-permute-start.11) | collective-permute-done | bytes 131104 | tf_op jit(solution)/shard_map/ppermute | solution.py:388
  178.9 1.9 collective-permute-start.18
  180.8 7.3 %collective-permute-done.18.theirs_ref = f32[64,512]{1,0:T(8,128)S(1)} collective-permute-done((f32[64,512]{1,0:T(8,128)S(1)}, f32[64,512]{1,0:T(8,128)S(1)}, u32[]{:S(2)}, u32[]{:S(2)}) %collective-permute-start.18) | collective-permute-done | bytes 131104 | tf_op jit(solution)/shard_map/ppermute | solution.py:393
  188.1 4.3 %update.1 = (f32[4,3,224,128]{3,2,1,0:T(8,128)}, f32[4,3,224,128]{3,2,1,0:T(8,128)}, bf16[64,512]{1,0:T(8,128)(2,1)}) custom-call(s32[16]{0:T(128)S(1)} %reshape.130.module_ref, f32[4]{0:T(128)S(1)} %broadcast_divide_fusion.scale_ref, bf16[16,3,224,128]{3,2,1,0:T(8,128)(2,1)} %all-to-all-done.2.delta_hbm, bf16[4,3,224,128]{3,2,1,0:T(8,128)(2,1)S(1)} %bitcast.34, ...), custom_call_target="tpu_custom_call" | custom-call | flops 1000000 | bytes 8388608 | tf_op jit(solution)/shard_map/update/pallas_call | solution.py:293
  (77 shorter events, 27.2 us)
Async XLA Ops:
  0.6 98.4 %copy-start = (s32[4,16]{1,0:T(4,128)S(1)}, s32[4,16]{1,0:T(4,128)}, u32[]{:S(2)}) copy-start(s32[4,16]{1,0:T(4,128)} %param.14) | copy-start | bytes 772
  0.6 34.0 %copy-start.1 = (bf16[1,4,3,224,128]{4,3,2,1,0:T(8,128)(2,1)S(1)}, bf16[1,4,3,224,128]{4,3,2,1,0:T(8,128)(2,1)}, u32[]{:S(2)}) copy-start(bf16[1,4,3,224,128]{4,3,2,1,0:T(8,128)(2,1)} %param.10) | copy-start | bytes 2064388
  2.4 29.7 %all-to-all-start = ((bf16[32,64,128]{2,1,0:T(8,128)(2,1)}), bf16[32,64,128]{2,1,0:T(8,128)(2,1)S(1)}, u32[]{:S(2)}, u32[]{:S(2)}) async-start(bf16[32,64,128]{2,1,0:T(8,128)(2,1)} %bitcast.36), calls=%async_computation | async-start | bytes 1048576 | tf_op jit(solution)/shard_map/all_to_all | solution.py:359
  32.7 4.4 %copy-start.4 = (bf16[16,8,4,128]{3,1,2,0:T(8,128)(2,1)}, bf16[16,8,4,128]{3,1,2,0:T(8,128)(2,1)S(1)}, u32[]{:S(2)}) copy-start(bf16[16,8,4,128]{3,1,2,0:T(8,128)(2,1)S(1)} %copy.21) | copy-start | bytes 393220
  32.7 6.5 %collective-permute-start = (bf16[128,512]{1,0:T(8,128)(2,1)S(1)}, bf16[128,512]{1,0:T(8,128)(2,1)S(1)}, u32[]{:S(2)}, u32[]{:S(2)}) collective-permute-start(bf16[128,512]{1,0:T(8,128)(2,1)S(1)} %bitcast.37), channel_id=1, source_target_pairs={{0,16},{16,0},{1,17},{17,1},{2,18},{18,2},{3,19},{19,3},{4,20},{20... | collective-permute-start | bytes 393224 | tf_op jit(solution)/shard_map/ppermute | solution.py:368
  39.2 0.7 copy-start.5
  39.9 67.6 %all-to-all-start.1 = ((bf16[16,3,224,128]{3,2,1,0:T(8,128)(2,1)}), bf16[16,3,224,128]{3,2,1,0:T(8,128)(2,1)S(1)}, u32[]{:S(2)}, u32[]{:S(2)}) async-start(bf16[16,3,224,128]{3,2,1,0:T(8,128)(2,1)} %gather_fusion), calls=%async_computation.1 | async-start | bytes 5505024 | tf_op jit(solution)/shard_map/all_to_all | solution.py:370
  47.1 15.9 %collective-permute-start.1 = (bf16[256,512]{1,0:T(8,128)(2,1)S(1)}, bf16[256,512]{1,0:T(8,128)(2,1)S(1)}, u32[]{:S(2)}, u32[]{:S(2)}) collective-permute-start(bf16[256,512]{1,0:T(8,128)(2,1)S(1)} %pad_maximum_fusion), channel_id=1, source_target_pairs={{0,2},{2,4},{4,6},{6,8},{8,10},{10,12},{12,14},{14,0},{1,3},{3,5},... | collective-permute-start | bytes 786440 | tf_op jit(solution)/shard_map/ppermute | solution.py:336
  51.1 13.8 %collective-permute-start.2 = (bf16[256,512]{1,0:T(8,128)(2,1)S(1)}, bf16[256,512]{1,0:T(8,128)(2,1)S(1)}, u32[]{:S(2)}, u32[]{:S(2)}) collective-permute-start(bf16[256,512]{1,0:T(8,128)(2,1)S(1)} %pad_maximum_fusion), channel_id=1, source_target_pairs={{0,14},{2,0},{4,2},{6,4},{8,6},{10,8},{12,10},{14,12},{1,15},{3,1}... | collective-permute-start | bytes 786440 | tf_op jit(solution)/shard_map/ppermute | solution.py:337
  62.9 8.9 %collective-permute-start.3 = (bf16[256,512]{1,0:T(8,128)(2,1)S(1)}, bf16[256,512]{1,0:T(8,128)(2,1)S(1)}, u32[]{:S(2)}, u32[]{:S(2)}) collective-permute-start(bf16[256,512]{1,0:T(8,128)(2,1)S(1)} %collective-permute-done.1), channel_id=1, source_target_pairs={{0,2},{2,4},{4,6},{6,8},{8,10},{10,12},{12,14},{14,0},{1,3},{3,5},... | collective-permute-start | bytes 786440 | tf_op jit(solution)/shard_map/ppermute | solution.py:336
  64.9 8.8 %collective-permute-start.4 = (bf16[256,512]{1,0:T(8,128)(2,1)S(1)}, bf16[256,512]{1,0:T(8,128)(2,1)S(1)}, u32[]{:S(2)}, u32[]{:S(2)}) collective-permute-start(bf16[256,512]{1,0:T(8,128)(2,1)S(1)} %collective-permute-done.2), channel_id=1, source_target_pairs={{0,14},{2,0},{4,2},{6,4},{8,6},{10,8},{12,10},{14,12},{1,15},{3,1}... | collective-permute-start | bytes 786440 | tf_op jit(solution)/shard_map/ppermute | solution.py:337
  69.5 27.0 %copy-start.6 = (s32[16,1]{0,1:T(1,128)S(1)}, s32[16,1]{0,1:T(1,128)}, u32[]{:S(2)}) copy-start(s32[16,1]{0,1:T(1,128)} %param.13) | copy-start | bytes 196
  69.5 29.8 %copy-start.7 = (s32[8]{0:T(128)S(1)}, s32[8]{0:T(128)}, u32[]{:S(2)}) copy-start(s32[8]{0:T(128)} %constant.87.clone) | copy-start | bytes 100
  71.8 8.7 %collective-permute-start.5 = (bf16[256,512]{1,0:T(8,128)(2,1)S(1)}, bf16[256,512]{1,0:T(8,128)(2,1)S(1)}, u32[]{:S(2)}, u32[]{:S(2)}) collective-permute-start(bf16[256,512]{1,0:T(8,128)(2,1)S(1)} %collective-permute-done.3), channel_id=1, source_target_pairs={{0,2},{2,4},{4,6},{6,8},{8,10},{10,12},{12,14},{14,0},{1,3},{3,5},... | collective-permute-start | bytes 786440 | tf_op jit(solution)/shard_map/ppermute | solution.py:336
  73.7 8.7 %collective-permute-start.6 = (bf16[256,512]{1,0:T(8,128)(2,1)S(1)}, bf16[256,512]{1,0:T(8,128)(2,1)S(1)}, u32[]{:S(2)}, u32[]{:S(2)}) collective-permute-start(bf16[256,512]{1,0:T(8,128)(2,1)S(1)} %collective-permute-done.4), channel_id=1, source_target_pairs={{0,14},{2,0},{4,2},{6,4},{8,6},{10,8},{12,10},{14,12},{1,15},{3,1}... | collective-permute-start | bytes 786440 | tf_op jit(solution)/shard_map/ppermute | solution.py:337
  80.5 8.0 %collective-permute-start.7 = (bf16[128,512]{1,0:T(8,128)(2,1)S(1)}, bf16[128,512]{1,0:T(8,128)(2,1)S(1)}, u32[]{:S(2)}, u32[]{:S(2)}) collective-permute-start(bf16[128,512]{1,0:T(8,128)(2,1)S(1)} %slice.12), channel_id=1, source_target_pairs={{0,2},{2,4},{4,6},{6,8},{8,10},{10,12},{12,14},{14,0},{1,3},{3,5},... | collective-permute-start | bytes 393224 | tf_op jit(solution)/shard_map/ppermute | solution.py:342
  82.5 6.7 %collective-permute-start.8 = (bf16[128,512]{1,0:T(8,128)(2,1)S(1)}, bf16[128,512]{1,0:T(8,128)(2,1)S(1)}, u32[]{:S(2)}, u32[]{:S(2)}) collective-permute-start(bf16[128,512]{1,0:T(8,128)(2,1)S(1)} %slice.13), channel_id=1, source_target_pairs={{0,14},{2,0},{4,2},{6,4},{8,6},{10,8},{12,10},{14,12},{1,15},{3,1}... | collective-permute-start | bytes 393224 | tf_op jit(solution)/shard_map/ppermute | solution.py:343
  89.8 10.7 %collective-permute-start.9 = (bf16[2048,512]{1,0:T(8,128)(2,1)}, bf16[2048,512]{1,0:T(8,128)(2,1)}, u32[]{:S(2)}, u32[]{:S(2)}) collective-permute-start(bf16[2048,512]{1,0:T(8,128)(2,1)} %constant_dynamic-update-slice_fusion.mine_hbm), channel_id=1, source_target_pairs={{0,1},{1,0},{2,3},{3,2},{4,5},{5,4},{6,7},{7,6},{8,9},{9,8},{10,11... | collective-permute-start | bytes 6291464 | tf_op jit(solution)/shard_map/ppermute | solution.py:373
  114.3 73.8 %all-to-all-start.2 = ((bf16[16,3,224,128]{3,2,1,0:T(8,128)(2,1)}), bf16[16,3,224,128]{3,2,1,0:T(8,128)(2,1)}, u32[]{:S(2)}, u32[]{:S(2)}) async-start(bf16[16,3,224,128]{3,2,1,0:T(8,128)(2,1)} %get-tuple-element.24), calls=%async_computation.2 | async-start | bytes 5505024 | tf_op jit(solution)/shard_map/all_to_all | solution.py:384
  123.0 1.0 copy-start.3
  125.8 5.3 %collective-permute-start.10 = (bf16[16,64,512]{2,1,0:T(8,128)(2,1)S(1)}, bf16[16,64,512]{2,1,0:T(8,128)(2,1)S(1)}, u32[]{:S(2)}, u32[]{:S(2)}) collective-permute-start(bf16[16,64,512]{2,1,0:T(8,128)(2,1)S(1)} %get-tuple-element.27), channel_id=1, source_target_pairs={{0,1},{1,0},{2,3},{3,2},{4,5},{5,4},{6,7},{7,6},{8,9},{9,8},{10,11... | collective-permute-start | bytes 3145736 | tf_op jit(solution)/shard_map/ppermute | solution.py:387
  131.2 56.9 %copy-start.2 = (f32[1,4,3,224,128]{4,3,2,1,0:T(8,128)S(1)}, f32[1,4,3,224,128]{4,3,2,1,0:T(8,128)}, u32[]{:S(2)}) copy-start(f32[1,4,3,224,128]{4,3,2,1,0:T(8,128)} %param.11) | copy-start | bytes 4128772
  131.3 24.1 %collective-permute-start.17 = (bf16[2,64,512]{2,1,0:T(8,128)(2,1)S(1)}, bf16[2,64,512]{2,1,0:T(8,128)(2,1)S(1)}, u32[]{:S(2)}, u32[]{:S(2)}) collective-permute-start(bf16[2,64,512]{2,1,0:T(8,128)(2,1)S(1)} %get-tuple-element.35), channel_id=1, source_target_pairs={{0,14},{2,0},{4,2},{6,4},{8,6},{10,8},{12,10},{14,12},{1,15},{3,1}... | collective-permute-start | bytes 393224 | tf_op jit(solution)/shard_map/ppermute | solution.py:388
  142.1 16.5 %collective-permute-start.16 = (bf16[2,64,512]{2,1,0:T(8,128)(2,1)S(1)}, bf16[2,64,512]{2,1,0:T(8,128)(2,1)S(1)}, u32[]{:S(2)}, u32[]{:S(2)}) collective-permute-start(bf16[2,64,512]{2,1,0:T(8,128)(2,1)S(1)} %get-tuple-element.34), channel_id=1, source_target_pairs={{0,12},{2,14},{4,0},{6,2},{8,4},{10,6},{12,8},{14,10},{1,13},{3,15... | collective-permute-start | bytes 393224 | tf_op jit(solution)/shard_map/ppermute | solution.py:388
  144.3 17.8 %collective-permute-start.15 = (bf16[2,64,512]{2,1,0:T(8,128)(2,1)S(1)}, bf16[2,64,512]{2,1,0:T(8,128)(2,1)S(1)}, u32[]{:S(2)}, u32[]{:S(2)}) collective-permute-start(bf16[2,64,512]{2,1,0:T(8,128)(2,1)S(1)} %get-tuple-element.33), channel_id=1, source_target_pairs={{0,10},{2,12},{4,14},{6,0},{8,2},{10,4},{12,6},{14,8},{1,11},{3,13... | collective-permute-start | bytes 393224 | tf_op jit(solution)/shard_map/ppermute | solution.py:388
  146.2 15.9 %collective-permute-start.14 = (bf16[2,64,512]{2,1,0:T(8,128)(2,1)S(1)}, bf16[2,64,512]{2,1,0:T(8,128)(2,1)S(1)}, u32[]{:S(2)}, u32[]{:S(2)}) collective-permute-start(bf16[2,64,512]{2,1,0:T(8,128)(2,1)S(1)} %get-tuple-element.32), channel_id=1, source_target_pairs={{0,8},{2,10},{4,12},{6,14},{8,0},{10,2},{12,4},{14,6},{1,9},{3,11}... | collective-permute-start | bytes 393224 | tf_op jit(solution)/shard_map/ppermute | solution.py:388
  153.5 14.6 %collective-permute-start.13 = (bf16[2,64,512]{2,1,0:T(8,128)(2,1)S(1)}, bf16[2,64,512]{2,1,0:T(8,128)(2,1)}, u32[]{:S(2)}, u32[]{:S(2)}) collective-permute-start(bf16[2,64,512]{2,1,0:T(8,128)(2,1)S(1)} %get-tuple-element.31), channel_id=1, source_target_pairs={{0,6},{2,8},{4,10},{6,12},{8,14},{10,0},{12,2},{14,4},{1,7},{3,9},... | collective-permute-start | bytes 393224 | tf_op jit(solution)/shard_map/ppermute | solution.py:388
  155.5 18.1 %collective-permute-start.12 = (bf16[2,64,512]{2,1,0:T(8,128)(2,1)S(1)}, bf16[2,64,512]{2,1,0:T(8,128)(2,1)}, u32[]{:S(2)}, u32[]{:S(2)}) collective-permute-start(bf16[2,64,512]{2,1,0:T(8,128)(2,1)S(1)} %get-tuple-element.30), channel_id=1, source_target_pairs={{0,4},{2,6},{4,8},{6,10},{8,12},{10,14},{12,0},{14,2},{1,5},{3,7},... | collective-permute-start | bytes 393224 | tf_op jit(solution)/shard_map/ppermute | solution.py:388
  158.6 19.0 %collective-permute-start.11 = (bf16[2,64,512]{2,1,0:T(8,128)(2,1)S(1)}, bf16[2,64,512]{2,1,0:T(8,128)(2,1)}, u32[]{:S(2)}, u32[]{:S(2)}) collective-permute-start(bf16[2,64,512]{2,1,0:T(8,128)(2,1)S(1)} %get-tuple-element.29), channel_id=1, source_target_pairs={{0,2},{2,4},{4,6},{6,8},{8,10},{10,12},{12,14},{14,0},{1,3},{3,5},... | collective-permute-start | bytes 393224 | tf_op jit(solution)/shard_map/ppermute | solution.py:388
  178.9 9.2 %collective-permute-start.18 = (f32[64,512]{1,0:T(8,128)S(1)}, f32[64,512]{1,0:T(8,128)S(1)}, u32[]{:S(2)}, u32[]{:S(2)}) collective-permute-start(f32[64,512]{1,0:T(8,128)S(1)} %get-tuple-element.46), channel_id=1, source_target_pairs={{0,16},{16,0},{1,17},{17,1},{2,18},{18,2},{3,19},{19,3},{4,20},{20... | collective-permute-start | bytes 393224 | tf_op jit(solution)/shard_map/ppermute | solution.py:393
